TPU v7x, 512 devices: a whole 4x8x8 slice. The times are simulated.
512 devices in a mesh: dp: 32 (over y, x_lo, core), ctx: 16 (over z, x_hi).
Axes of the slice: x: 4 (x_hi: 2, x_lo: 2; x = x_hi * 2 + x_lo), y: 8, z: 8, core: 2. Of those that a mesh axis runs over, the one named last changes fastest.
Arguments:
- frames: bfloat16 [98304, 1536], P(('dp', 'ctx')), may hold values from -48 to 48
- seg_ids: int32 [32, 3072], P('dp'), may hold values from 0 to 7, never falling along the last dimension, each value on 1 to 768 neighbouring positions
- assign: int32 [32, 16], P('dp'), may hold values from 0 to 15, each once within a row
- w_qkv: bfloat16 [3, 1536, 1536], P(None, 'dp', 'ctx'), may hold values from -1 to 1
Outputs:
- context: bfloat16 [98304, 1536], P(('dp', 'ctx'))
Inputs may be any that keep to these rules, and one draw needn't show every extreme that they name: `seg_ids`: never falls along a sequence; each utterance has 1 to 768 frames, one exactly 768. `assign`: each row is a permutation.
All inputs are finite; a program needn't handle non-finite values.
Results may differ from a plain program's by a relative error of at most 0.0073.
Values may be sent and summed in bfloat16 or wider, within the bound.
No kernel may reach another device: no remote copies, remote signals or barrier semaphores. Data moves between devices by JAX's collectives and lax.ppermute only.
A program may use at most 64 MiB of HBM per device.

v0:
```python
import jax
import jax.numpy as jnp
from jax import lax
from jax.sharding import PartitionSpec as P

HEAD = 96


def attend_all(queries, keys, values, ids, block):
    scale = queries.shape[-1] ** (-0.5)
    count = queries.shape[0] // block

    def one(index):
        qblock = lax.dynamic_slice_in_dim(queries, index * block, block, 0)
        qids = lax.dynamic_slice_in_dim(ids, index * block, block, 0)
        scores = jnp.dot(qblock, keys.T, preferred_element_type=jnp.float32) * scale
        scores = jnp.where(qids[:, None] == ids[None, :], scores, -1e30)
        top = jnp.max(scores, axis=1, keepdims=True)
        expo = jnp.exp(scores - top)
        weights = (expo / jnp.sum(expo, axis=1, keepdims=True)).astype(jnp.bfloat16)
        return jnp.dot(weights, values, preferred_element_type=jnp.float32).astype(jnp.bfloat16)

    result = lax.map(one, jnp.arange(count, dtype=jnp.int32))
    return result.reshape(queries.shape[0], queries.shape[1])


def body(frames, seg_ids, assign, w_qkv):
    rows = frames.shape[0]
    parts = lax.axis_size("ctx")
    total = rows * parts
    order = assign[0]
    ids = seg_ids[0]
    columns = lax.all_gather(w_qkv, "ctx", axis=2, tiled=True)
    projected = jnp.einsum(
        "rd,tdc->trc",
        frames,
        lax.all_gather(columns, "dp", axis=1, tiled=True),
        preferred_element_type=jnp.float32,
    ).astype(jnp.bfloat16)
    queries, keys, values = (
        lax.all_to_all(projected[0], "ctx", split_axis=1, concat_axis=0, tiled=True),
        lax.all_to_all(projected[1], "ctx", split_axis=1, concat_axis=0, tiled=True),
        lax.all_to_all(projected[2], "ctx", split_axis=1, concat_axis=0, tiled=True),
    )
    local_heads = queries.shape[1] // HEAD
    block = min(512, total)

    def split_heads(array):
        return array.reshape(total, local_heads, HEAD).transpose(1, 0, 2)

    store_ids = jnp.take(ids.reshape(parts, rows), order, axis=0).reshape(total)

    def per_head(triple):
        return attend_all(triple[0], triple[1], triple[2], store_ids, block)

    heads_out = lax.map(per_head, (split_heads(queries), split_heads(keys), split_heads(values)))
    merged = heads_out.transpose(1, 0, 2).reshape(total, local_heads * HEAD)
    return lax.all_to_all(merged, "ctx", split_axis=0, concat_axis=1, tiled=True)


def solution(mesh):
    return jax.shard_map(
        body,
        mesh=mesh,
        in_specs=(P(("dp", "ctx"), None), P("dp", None), P("dp", None), P(None, "dp", "ctx")),
        out_specs=P(("dp", "ctx"), None),
        check_vma=False,
    )
```

profile of v0, /device:TPU:6, one launch (start us, length us, event | category | flops | bytes accessed | tf_op | source)
XLA Modules:
  0.0 330.4 jit_solution(11947252159614352941)
XLA Ops:
  6.5 0.9 copy.17
  7.5 59.7 %all_gather.6 = bf16[3,48,1536]{1,0,2:T(4,128)(2,1)S(1)} all-gather(bf16[3,48,96]{1,0,2:T(4,128)(2,1)S(1)} %copy.17), channel_id=1, replica_groups=mesh['dp'=32,'ctx'=16] {'ctx'}, dimensions={2}, use_global_device_ids=true | all-gather | bytes 470016 | tf_op jit(solution)/shard_map/all_gather | solution.py:33
  67.2 1.9 copy.18
  69.1 90.7 %all-gather.2.cloned.1.call-done = bf16[3,1536,1536]{2,1,0:T(8,128)(2,1)} async-done(((bf16[3,48,1536]{2,1,0:T(8,128)(2,1)}), bf16[3,1536,1536]{2,1,0:T(8,128)(2,1)}) %all-gather.2.cloned.1.call-update) | async-done | bytes 14155792 | tf_op jit(solution)/shard_map/all_gather | solution.py:37
  159.8 7.9 %fusion.7 = bf16[3,192,1536]{2,1,0:T(8,128)(2,1)S(1)} fusion(bf16[3,1536,1536]{2,1,0:T(8,128)(2,1)} %all-gather.2.cloned.1.call-done, bf16[192,1536]{1,0:T(8,128)(2,1)S(1)} %copy-done), kind=kOutput, calls=%fused_computation.12 | convolution fusion | flops 2718793728 | bytes 16515072 | tf_op jit(solution)/shard_map/rd,tdc->trc/dot_general | solution.py:34
  167.9 0.7 all_to_all.53
  168.5 1.1 copy.20
  169.6 10.4 %all-to-all-start.1 = ((bf16[192,16,96]{2,0,1:T(8,128)(2,1)}), bf16[192,16,96]{2,0,1:T(8,128)(2,1)S(1)}, u32[]{:S(2)}, u32[]{:S(2)}) async-start(bf16[192,16,96]{2,0,1:T(8,128)(2,1)} %copy.20), calls=%async_computation.1 | async-start | bytes 1572864 | tf_op jit(solution)/shard_map/all_to_all | solution.py:42
  180.0 0.7 all_to_all.56
  180.7 1.1 copy.21
  181.8 20.6 %all-to-all-done.1 = bf16[192,16,96]{2,0,1:T(8,128)(2,1)S(1)} async-done(((bf16[192,16,96]{2,0,1:T(8,128)(2,1)}), bf16[192,16,96]{2,0,1:T(8,128)(2,1)S(1)}, u32[]{:S(2)}, u32[]{:S(2)}) %all-to-all-start.1) | async-done | bytes 589856 | tf_op jit(solution)/shard_map/all_to_all | solution.py:42
  202.3 7.0 %all-to-all-start.2 = ((bf16[192,16,96]{2,0,1:T(8,128)(2,1)}), bf16[192,16,96]{2,0,1:T(8,128)(2,1)}, u32[]{:S(2)}, u32[]{:S(2)}) async-start(bf16[192,16,96]{2,0,1:T(8,128)(2,1)} %copy.21), calls=%async_computation.2 | async-start | bytes 1572864 | tf_op jit(solution)/shard_map/all_to_all | solution.py:43
  209.3 0.7 all_to_all.50
  210.0 1.1 copy.19
  211.1 17.8 %all-to-all-done.2 = bf16[192,16,96]{2,0,1:T(8,128)(2,1)} async-done(((bf16[192,16,96]{2,0,1:T(8,128)(2,1)}), bf16[192,16,96]{2,0,1:T(8,128)(2,1)}, u32[]{:S(2)}, u32[]{:S(2)}) %all-to-all-start.2) | async-done | bytes 589856 | tf_op jit(solution)/shard_map/all_to_all | solution.py:43
  228.8 6.8 %all-to-all-start = ((bf16[192,16,96]{2,0,1:T(8,128)(2,1)}), bf16[192,16,96]{2,0,1:T(8,128)(2,1)S(1)}, u32[]{:S(2)}, u32[]{:S(2)}) async-start(bf16[192,16,96]{2,0,1:T(8,128)(2,1)} %copy.19), calls=%async_computation | async-start | bytes 1572864 | tf_op jit(solution)/shard_map/all_to_all | solution.py:41
  235.6 0.5 broadcast.55
  236.1 0.7 reduce.3
  236.9 0.6 gather_fusion
  237.7 17.7 %all-to-all-done = bf16[192,16,96]{2,0,1:T(8,128)(2,1)S(1)} async-done(((bf16[192,16,96]{2,0,1:T(8,128)(2,1)}), bf16[192,16,96]{2,0,1:T(8,128)(2,1)S(1)}, u32[]{:S(2)}, u32[]{:S(2)}) %all-to-all-start) | async-done | bytes 589856 | tf_op jit(solution)/shard_map/all_to_all | solution.py:41
  255.4 37.4 %while.18 = (s32[]{:T(128)}, bf16[6,512,96]{1,2,0:T(8,128)(2,1)S(1)}, s32[6]{0:T(128)S(1)}, s32[3072]{0:T(1024)S(1)}, s32[16,192]{1,0:T(8,128)}, /*index=5*/bf16...) while((s32[]{:T(128)}, ...), condition=%wide.wide.region_3.4_spmd, body=%wide.wide.region_0.3_spmd.sunk | while | flops 618183680 | bytes 20508868 | solution.py:23
  255.4 0.6 dynamic_slice.28
  256.7 1.2 fusion.27
  257.9 1.0 fusion.28
  258.9 2.7 fusion.29
  261.6 0.6 dynamic_slice.28
  262.9 1.2 fusion.27
  264.2 1.0 fusion.28
  265.2 2.7 fusion.29
  267.9 0.6 dynamic_slice.28
  269.2 1.2 fusion.27
  270.4 1.0 fusion.28
  271.4 2.7 fusion.29
  274.1 0.6 dynamic_slice.28
  275.4 1.2 fusion.27
  276.6 1.0 fusion.28
  277.6 2.7 fusion.29
  280.3 0.6 dynamic_slice.28
  281.7 1.2 fusion.27
  282.9 1.0 fusion.28
  283.9 2.7 fusion.29
  286.6 0.6 dynamic_slice.28
  287.9 1.2 fusion.27
  289.1 1.0 fusion.28
  290.1 2.7 fusion.29
  293.2 28.1 %all_to_all.67 = bf16[16,192,96]{2,1,0:T(8,128)(2,1)S(1)} all-to-all(bf16[16,192,96]{2,1,0:T(8,128)(2,1)S(1)} %bitcast.43), channel_id=1, replica_groups=mesh['dp'=32,'ctx'=16] {'ctx'}, dimensions={0} | all-to-all | bytes 1179648 | tf_op jit(solution)/shard_map/all_to_all | solution.py:58
  321.3 0.5 copy.23
  321.8 1.7 all_to_all.62
  (27 shorter events, 1.3 us)
Async XLA Ops:
  6.5 153.3 %copy-start = (bf16[192,1536]{1,0:T(8,128)(2,1)S(1)}, bf16[192,1536]{1,0:T(8,128)(2,1)}, u32[]{:S(2)}) copy-start(bf16[192,1536]{1,0:T(8,128)(2,1)} %param.6) | copy-start | bytes 1769476
  6.5 153.3 %all-gather.2.cloned.1.call-start = ((), (), s32[]{:S(2)}) async-start(), calls=%async_computation.4 | async-start | bytes 14598144 | tf_op jit(solution)/shard_map/all_gather | solution.py:37
  168.5 67.6 %copy-start.2 = (s32[1,3072]{1,0:T(1,128)S(1)}, s32[1,3072]{1,0:T(1,128)}, u32[]{:S(2)}) copy-start(s32[1,3072]{1,0:T(1,128)} %param.7) | copy-start | bytes 36868
  168.5 68.3 %copy-start.3 = (s32[1,16]{1,0:T(1,128)S(1)}, s32[1,16]{1,0:T(1,128)}, u32[]{:S(2)}) copy-start(s32[1,16]{1,0:T(1,128)} %param.8) | copy-start | bytes 196
  169.6 32.7 %all-to-all-start.1 = ((bf16[192,16,96]{2,0,1:T(8,128)(2,1)}), bf16[192,16,96]{2,0,1:T(8,128)(2,1)S(1)}, u32[]{:S(2)}, u32[]{:S(2)}) async-start(bf16[192,16,96]{2,0,1:T(8,128)(2,1)} %copy.20), calls=%async_computation.1 | async-start | bytes 1572864 | tf_op jit(solution)/shard_map/all_to_all | solution.py:42
  202.3 26.5 %all-to-all-start.2 = ((bf16[192,16,96]{2,0,1:T(8,128)(2,1)}), bf16[192,16,96]{2,0,1:T(8,128)(2,1)}, u32[]{:S(2)}, u32[]{:S(2)}) async-start(bf16[192,16,96]{2,0,1:T(8,128)(2,1)} %copy.21), calls=%async_computation.2 | async-start | bytes 1572864 | tf_op jit(solution)/shard_map/all_to_all | solution.py:43
  228.8 26.6 %all-to-all-start = ((bf16[192,16,96]{2,0,1:T(8,128)(2,1)}), bf16[192,16,96]{2,0,1:T(8,128)(2,1)S(1)}, u32[]{:S(2)}, u32[]{:S(2)}) async-start(bf16[192,16,96]{2,0,1:T(8,128)(2,1)} %copy.19), calls=%async_computation | async-start | bytes 1572864 | tf_op jit(solution)/shard_map/all_to_all | solution.py:41
  237.5 17.8 %copy-start.1 = (s32[16,192]{1,0:T(8,128)}, s32[16,192]{1,0:T(8,128)S(1)}, u32[]{:S(2)}) copy-start(s32[16,192]{1,0:T(8,128)S(1)} %broadcast_select_fusion) | copy-start | bytes 36868
Sparse Core Ops, SparseCore 0:
  69.2 90.5 all-gather.1
where the time goes:
time: 335 us; the launch traced here: 330 us
  waiting for transfers between devices  147 us (44%)
  blocking collectives  87.8 us (26%)
  matrix products  31.5 us (9%)
  starting transfers between devices  24.1 us (7%)
  local copies, waits for them, and re-layouts  16.2 us (5%)
  between operations  13.5 us (4%)
  other arithmetic  6.74 us (2%)
  loops' own time  3.78 us (1%)
    all_gather x1, waiting for transfers between devices, body(): lax.all_gather(columns, 'dp', axis=1, tiled=True)  90.7 us
    all_gather x1, blocking collectives, body(): columns = lax.all_gather(w_qkv, 'ctx', axis=2, tiled=True)  59.7 us
    all_to_all x1, blocking collectives, body(): lax.all_to_all(merged, 'ctx', split_axis=0, concat_axis=1, tiled=True)  28.1 us
    all_to_all x1, waiting for transfers between devices, body(): lax.all_to_all(projected[1], 'ctx', split_axis=1, concat_axis=0, tiled=True)  20.6 us
    all_to_all x1, waiting for transfers between devices, body(): lax.all_to_all(projected[2], 'ctx', split_axis=1, concat_axis=0, tiled=True)  17.8 us
    all_to_all x1, waiting for transfers between devices, body(): lax.all_to_all(projected[0], 'ctx', split_axis=1, concat_axis=0, tiled=True)  17.7 us
    dot_general x6, matrix products, one(): jnp.dot(weights, values, preferred_element_type=jnp.float32)  16.1 us
    all_to_all x1, starting transfers between devices, body(): lax.all_to_all(projected[1], 'ctx', split_axis=1, concat_axis=0, tiled=True)  10.4 us
  transfers between devices with their start and end apart: 4, of which 4 were waited for; matrix products, arithmetic and copies ran while one was open for 1% of the time, Pallas kernels for 0%

commit v1 on v0

v1 whole, which is shorter than its diff:
```python
import functools

import jax
import jax.numpy as jnp
from jax import lax
from jax.experimental import pallas as pl
from jax.experimental.pallas import tpu as pltpu
from jax.sharding import Mesh
from jax.sharding import PartitionSpec as P

HEAD = 96
FR = 192
D = 1536
NZ = 8
SEQ = 3072
TILE = 256
MAX_TILES = 8
ROWS = NZ * FR
AXES = ("y", "xl", "core", "z", "xh")
SIZES = (8, 2, 2, 8, 2)


def swap(x, axis):
    return lax.ppermute(x, axis, [(0, 1), (1, 0)])


def both(own, other, index, axis):
    first = jnp.where(index == 0, own, other)
    second = jnp.where(index == 0, other, own)
    return jnp.stack([first, second], axis=axis)


def gather_weights(w):
    xh = lax.axis_index("xh")
    flat = jnp.transpose(w, (1, 0, 2)).reshape(w.shape[1], 3 * HEAD)
    heads = both(flat, swap(flat, "xh"), xh, 0)
    q, k, v = (heads[:, :, t * HEAD : (t + 1) * HEAD] for t in range(3))
    shard = jnp.concatenate([jnp.zeros_like(q[0, :, :64]), q[0], q[1], v[0], v[1], k[0], k[1]], axis=1)
    rows = lax.all_to_all(jnp.broadcast_to(shard[None], (8,) + shard.shape), "y", 0, 0, tiled=True)
    rows = both(rows, swap(rows, "xl"), lax.axis_index("xl"), 1)
    rows = both(rows, swap(rows, "core"), lax.axis_index("core"), 2)
    return rows.reshape(D, shard.shape[1])


def project_kernel(x_ref, w_ref, kv_ref, q_ref):
    x = x_ref[...]
    kv_ref[...] = jnp.dot(x, w_ref[:, 256:], preferred_element_type=jnp.float32).astype(jnp.bfloat16)
    q_ref[...] = jnp.dot(x, w_ref[:, :256], preferred_element_type=jnp.float32).astype(jnp.bfloat16)


def project(x, w):
    step = 256
    n = x.shape[0]
    return pl.pallas_call(
        project_kernel,
        grid=(n // step,),
        in_specs=[pl.BlockSpec((step, D), lambda i: (i, 0)), pl.BlockSpec((D, 640), lambda i: (0, 0))],
        out_specs=[pl.BlockSpec((step, 384), lambda i: (i, 0)), pl.BlockSpec((step, 256), lambda i: (i, 0))],
        out_shape=[jax.ShapeDtypeStruct((n, 384), jnp.bfloat16), jax.ShapeDtypeStruct((n, 256), jnp.bfloat16)],
        compiler_params=pltpu.CompilerParams(vmem_limit_bytes=24 << 20),
        cost_estimate=pl.CostEstimate(flops=2 * n * D * 640, bytes_accessed=2 * (n * D + D * 640 + n * 640), transcendentals=0),
    )(x, w)


def attend_kernel(info_ref, own_ref, other_ref, q_ref, qid_ref, kid_ref, out_ref, kv_ref, s_ref):
    xh = info_ref[32]
    kv_ref[SEQ:, :] = jnp.zeros((TILE, 384), jnp.bfloat16)
    for z in range(NZ):
        for ref, side in ((own_ref, xh), (other_ref, 1 - xh)):
            at = pl.multiple_of(info_ref[2 * z + side] * FR, FR)
            kv_ref[pl.ds(at, FR), :] = ref[z * FR : (z + 1) * FR, :]
    scale = HEAD**-0.5 * 1.4426950408889634
    lane = lax.broadcasted_iota(jnp.int32, (FR, 256), 1)

    def block(z, _):
        rows = pl.ds(pl.multiple_of(z * FR, FR), FR)
        q = q_ref[rows, :]
        zero = jnp.zeros_like(q)
        q2 = jnp.concatenate([jnp.where(lane < 160, q, zero), jnp.where(lane >= 160, q, zero)], axis=0)
        qid = qid_ref[rows, :]
        qid2 = jnp.concatenate([qid, qid], axis=0)
        first, count = info_ref[16 + z], info_ref[24 + z]

        def score(t, top):
            at = pl.multiple_of(first + t * TILE, 128)
            keys = kv_ref[pl.ds(at, TILE), 128:384]
            s = lax.dot_general(q2, keys, (((1,), (1,)), ((), ())), preferred_element_type=jnp.float32)
            s = jnp.where(qid2 == kid_ref[:, pl.ds(at, TILE)], s, -1e30)
            s_ref[t] = s
            return jnp.maximum(top, jnp.maximum(s[:, :128], s[:, 128:]))

        top = lax.fori_loop(0, count, score, jnp.full((2 * FR, 128), -1e30, jnp.float32))
        top = jnp.max(top, axis=1, keepdims=True)

        def weigh(t, carry):
            total, acc = carry
            at = pl.multiple_of(first + t * TILE, 128)
            p = jnp.exp2((s_ref[t] - top) * scale)
            total = total + (p[:, :128] + p[:, 128:])
            acc = acc + jnp.dot(p.astype(jnp.bfloat16), kv_ref[pl.ds(at, TILE), :256], preferred_element_type=jnp.float32)
            return total, acc

        total, acc = lax.fori_loop(
            0, count, weigh, (jnp.zeros((2 * FR, 128), jnp.float32), jnp.zeros((2 * FR, 256), jnp.float32))
        )
        acc = acc / jnp.sum(total, axis=1, keepdims=True)
        o = jnp.where(lane < HEAD, acc[:FR], acc[FR:])
        tail = o[:, 128:]
        half = lax.broadcasted_iota(jnp.int32, (FR // 2, 128), 1) < 64
        packed = jnp.where(half, tail[: FR // 2], pltpu.roll(tail[FR // 2 :], 64, 1))
        out_ref[z, :FR, :] = o[:, :128].astype(jnp.bfloat16)
        out_ref[z, FR:, :] = packed.astype(jnp.bfloat16)
        return 0

    lax.fori_loop(0, NZ, block, 0)


def attend(info, own, other, q, qid, kid):
    vmem = pl.BlockSpec(memory_space=pltpu.VMEM)
    return pl.pallas_call(
        attend_kernel,
        in_specs=[pl.BlockSpec(memory_space=pltpu.SMEM)] + [vmem] * 5,
        out_specs=vmem,
        out_shape=jax.ShapeDtypeStruct((NZ, FR * 3 // 2, 128), jnp.bfloat16),
        scratch_shapes=[
            pltpu.VMEM((SEQ + TILE, 384), jnp.bfloat16),
            pltpu.VMEM((MAX_TILES, 2 * FR, TILE), jnp.float32),
        ],
        compiler_params=pltpu.CompilerParams(vmem_limit_bytes=40 << 20),
        cost_estimate=pl.CostEstimate(flops=8 << 30, bytes_accessed=8 << 20, transcendentals=4 << 20),
    )(info, own, other, q, qid, kid)


def unpack_kernel(in_ref, out_ref):
    half = lax.broadcasted_iota(jnp.int32, (FR, 128), 1) < 64
    for z in range(0, NZ, 2):
        tails = []
        for i in (z, z + 1):
            packed = in_ref[i, FR:, :].astype(jnp.float32)
            tails.append(jnp.concatenate([packed, pltpu.roll(packed, 64, 1)], axis=0))
        second = pltpu.roll(in_ref[z + 1, :FR, :].astype(jnp.float32), 64, 1)
        out_ref[:, z * 192 : z * 192 + 128] = in_ref[z, :FR, :]
        out_ref[:, z * 192 + 128 : z * 192 + 256] = jnp.where(half, tails[0], second).astype(jnp.bfloat16)
        out_ref[:, z * 192 + 256 : z * 192 + 384] = jnp.where(half, second, pltpu.roll(tails[1], 64, 1)).astype(jnp.bfloat16)


def unpack(packed):
    vmem = pl.BlockSpec(memory_space=pltpu.VMEM)
    return pl.pallas_call(
        unpack_kernel,
        in_specs=[vmem],
        out_specs=vmem,
        out_shape=jax.ShapeDtypeStruct((FR, D), jnp.bfloat16),
        compiler_params=pltpu.CompilerParams(vmem_limit_bytes=8 << 20),
    )(packed)


def plan(ids, order, xh):
    blocks = ids.reshape(16, FR)
    own = lax.dynamic_index_in_dim(order.reshape(NZ, 2), xh, 1, keepdims=False)
    qid = jnp.take(blocks, own, axis=0)
    first = jnp.sum(ids[None, :] < qid[:, :1], axis=1, dtype=jnp.int32)
    last = jnp.sum(ids[None, :] <= qid[:, FR - 1 :], axis=1, dtype=jnp.int32)
    first = first // 128 * 128
    info = jnp.concatenate([order, first, (last - first + TILE - 1) // TILE, xh.astype(jnp.int32)[None]])
    kid = jnp.concatenate([ids, jnp.full((TILE,), -1, jnp.int32)])[None]
    return info, qid.reshape(ROWS, 1), kid


def body(frames, seg_ids, assign, w_qkv):
    xh = lax.axis_index("xh")
    x = lax.all_gather(frames, "z", axis=0, tiled=True)
    info, qid, kid = plan(seg_ids[0], assign[0], xh)
    kv, q = project(x, gather_weights(w_qkv))
    packed = attend(info, kv, swap(kv, "xh"), q, qid, kid)
    return unpack(lax.all_to_all(packed, "z", 0, 0, tiled=True))


def solution(mesh):
    fine = Mesh(mesh.devices.reshape(SIZES), AXES)
    dp, ctx = AXES[:3], AXES[3:]
    return jax.shard_map(
        body,
        mesh=fine,
        in_specs=(P(AXES, None), P(dp, None), P(dp, None), P(None, dp, ctx)),
        out_specs=P(AXES, None),
        check_vma=False,
    )
```

time: 335 us -> 167 us (0.50)
  waiting for transfers between devices: 147 us -> 61.8 us
  blocking collectives: 87.8 us -> 44 us
  matrix products: 31.5 us -> 0 us
  Pallas kernels: 0 us -> 23.3 us
  starting transfers between devices: 24.1 us -> 11.3 us
  local copies, waits for them, and re-layouts: 16.2 us -> 7.56 us
  other arithmetic: 6.74 us -> 2.75 us
  loops' own time: 3.78 us -> 0 us
    all_gather x1, waiting for transfers between devices: 90.7 us -> 22.1 us  [body(): x = lax.all_gather(frames, 'z', axis=0, tiled=True)]
    all_gather x1 -> x0, blocking collectives: 59.7 us -> none  [body(): columns = lax.all_gather(w_qkv, 'ctx', axis=2, tiled=True)]
    all_to_all x3 -> x0, waiting for transfers between devices: 56 us -> none  [the longest x1 20.6 us: body(): lax.all_to_all(projected[1], 'ctx', split_axis=1, concat_axis=0, tiled=True)]
    ppermute x0 -> x4, waiting for transfers between devices: none -> 39 us  [swap(): return lax.ppermute(x, axis, [(0, 1), (1, 0)])]
    dot_general x13 -> x0, matrix products: 31.5 us -> none  [the longest x6 16.1 us: one(): jnp.dot(weights, values, preferred_element_type=jnp.float32)]
    all_to_all x3 -> x0, starting transfers between devices: 24.1 us -> none  [the longest x1 10.4 us: body(): lax.all_to_all(projected[1], 'ctx', split_axis=1, concat_axis=0, tiled=True)]
    pallas_call x0 -> x3, Pallas kernels: none -> 23.3 us  [the longest x1 17.5 us: attend(): pl.pallas_call(attend_kernel, in_specs=[pl.BlockSpec(memory_space=pltpu.S...]
    all_to_all x1 -> x2, blocking collectives: 28.1 us -> 44 us  [the longest x1 22.5 us: gather_weights(): lax.all_to_all(jnp.broadcast_to(shard[None], (8,) + shard.shape), 'y', 0,...]
  transfers between devices with their start and end apart: 4 -> 5, of which waited for: 4 -> 5; matrix products, arithmetic and copies ran while one was open for 1% -> 4% of each run, Pallas kernels for 0% -> 0%
where the time goes in v1:
time: 167 us; the launch traced here: 164 us
  waiting for transfers between devices  61.8 us (37%)
  blocking collectives  44 us (26%)
  Pallas kernels  23.3 us (14%)
  between operations  13.6 us (8%)
  starting transfers between devices  11.3 us (7%)
  local copies, waits for them, and re-layouts  7.56 us (5%)
  other arithmetic  2.75 us (2%)
    ppermute x4, waiting for transfers between devices, swap(): return lax.ppermute(x, axis, [(0, 1), (1, 0)])  39 us
    all_to_all x1, blocking collectives, gather_weights(): lax.all_to_all(jnp.broadcast_to(shard[None], (8,) + shard.shape), 'y', 0,...  22.5 us
    all_gather x1, waiting for transfers between devices, body(): x = lax.all_gather(frames, 'z', axis=0, tiled=True)  22.1 us
    all_to_all x1, blocking collectives, body(): return unpack(lax.all_to_all(packed, 'z', 0, 0, tiled=True))  21.4 us
    pallas_call x1, Pallas kernels, attend(): pl.pallas_call(attend_kernel, in_specs=[pl.BlockSpec(memory_space=pltpu.S...  17.5 us
    ppermute x4, starting transfers between devices, swap(): return lax.ppermute(x, axis, [(0, 1), (1, 0)])  11.3 us
    unnamed x11, local copies, waits for them, and re-layouts  4.92 us
    pallas_call x1, Pallas kernels, project(): pl.pallas_call(project_kernel, grid=(n // step,), in_specs=[pl.BlockSpec(...  4.65 us
  transfers between devices with their start and end apart: 5, of which 5 were waited for; matrix products, arithmetic and copies ran while one was open for 4% of the time, Pallas kernels for 0%

profile of v1, /device:TPU:6, one launch (start us, length us, event | category | flops | bytes accessed | tf_op | source)
XLA Modules:
  0.0 164.3 jit_solution(7829797604897990706)
XLA Ops:
  6.5 0.0 all-gather.2.cloned.1.call-start
  6.5 0.7 all-gather.2.cloned.1.call-update
  7.3 0.8 copy.11
  8.0 0.1 reshape.33
  8.1 3.3 %collective-permute-start = (bf16[48,288]{1,0:T(8,128)(2,1)S(1)}, bf16[48,288]{1,0:T(8,128)(2,1)S(1)}, u32[]{:S(2)}, u32[]{:S(2)}) collective-permute-start(bf16[48,288]{1,0:T(8,128)(2,1)S(1)} %reshape.33), channel_id=1, source_target_pairs={{0,1},{1,0},{2,3},{3,2},{4,5},{5,4},{6,7},{7,6},{8,9},{9,8},{10,11... | collective-permute-start | bytes 82952 | tf_op jit(solution)/shard_map/ppermute | solution.py:24
  11.5 4.0 %collective-permute-done = bf16[48,288]{1,0:T(8,128)(2,1)S(1)} collective-permute-done((bf16[48,288]{1,0:T(8,128)(2,1)S(1)}, bf16[48,288]{1,0:T(8,128)(2,1)S(1)}, u32[]{:S(2)}, u32[]{:S(2)}) %collective-permute-start) | collective-permute-done | bytes 27680 | tf_op jit(solution)/shard_map/ppermute | solution.py:24
  15.5 0.1 slice_bitcast_fusion
  15.6 0.1 concatenate.10
  15.8 22.5 %all_to_all.10 = bf16[8,48,640]{2,1,0:T(8,128)(2,1)S(1)} all-to-all(bf16[8,48,640]{2,1,0:T(8,128)(2,1)S(1)} %broadcast_in_dim.30), channel_id=1, replica_groups=mesh['y'=8,'xl'=2,'core'=2,'z'=8,'xh'=2] {'y'}, dimensions={0} | all-to-all | bytes 983040 | tf_op jit(solution)/shard_map/all_to_all | solution.py:39
  38.3 2.7 %collective-permute-start.1 = (bf16[8,48,640]{2,1,0:T(8,128)(2,1)S(1)}, bf16[8,48,640]{2,1,0:T(8,128)(2,1)S(1)}, u32[]{:S(2)}, u32[]{:S(2)}) collective-permute-start(bf16[8,48,640]{2,1,0:T(8,128)(2,1)S(1)} %all_to_all.10), channel_id=1, source_target_pairs={{0,32},{32,0},{1,33},{33,1},{2,34},{34,2},{3,35},{35,3},{4,36},{36... | collective-permute-start | bytes 1474568 | tf_op jit(solution)/shard_map/ppermute | solution.py:24
  41.1 8.9 %collective-permute-done.1 = bf16[8,48,640]{2,1,0:T(8,128)(2,1)S(1)} collective-permute-done((bf16[8,48,640]{2,1,0:T(8,128)(2,1)S(1)}, bf16[8,48,640]{2,1,0:T(8,128)(2,1)S(1)}, u32[]{:S(2)}, u32[]{:S(2)}) %collective-permute-start.1) | collective-permute-done | bytes 491552 | tf_op jit(solution)/shard_map/ppermute | solution.py:24
  50.0 0.1 select_bitcast_fusion.3
  50.1 0.1 pad_maximum_fusion.1
  50.2 1.9 %collective-permute-start.2 = (bf16[8,2,48,640]{3,2,1,0:T(8,128)(2,1)S(1)}, bf16[8,2,48,640]{3,2,1,0:T(8,128)(2,1)S(1)}, u32[]{:S(2)}, u32[]{:S(2)}) collective-permute-start(bf16[8,2,48,640]{3,2,1,0:T(8,128)(2,1)S(1)} %pad_maximum_fusion.1), channel_id=1, source_target_pairs={{0,16},{16,0},{1,17},{17,1},{2,18},{18,2},{3,19},{19,3},{4,20},{20... | collective-permute-start | bytes 2949128 | tf_op jit(solution)/shard_map/ppermute | solution.py:24
  52.2 2.5 %collective-permute-done.2 = bf16[8,2,48,640]{3,2,1,0:T(8,128)(2,1)S(1)} collective-permute-done((bf16[8,2,48,640]{3,2,1,0:T(8,128)(2,1)S(1)}, bf16[8,2,48,640]{3,2,1,0:T(8,128)(2,1)S(1)}, u32[]{:S(2)}, u32[]{:S(2)}) %collective-permute-start.2) | collective-permute-done | bytes 983072 | tf_op jit(solution)/shard_map/ppermute | solution.py:24
  54.7 0.2 select_bitcast_fusion.1
  54.9 0.2 pad_maximum_fusion
  55.1 22.1 %all-gather.2.cloned.1.call-done.x_ref = bf16[1536,1536]{1,0:T(8,128)(2,1)} async-done(((bf16[192,1536]{1,0:T(8,128)(2,1)}), bf16[1536,1536]{1,0:T(8,128)(2,1)}) %all-gather.2.cloned.1.call-update) | async-done | bytes 4718608 | tf_op jit(solution)/shard_map/all_gather | solution.py:172
  77.2 0.0 copy-start
  77.2 2.3 %copy-done = bf16[1536,1536]{1,0:T(8,128)(2,1)S(1)} copy-done((bf16[1536,1536]{1,0:T(8,128)(2,1)S(1)}, bf16[1536,1536]{1,0:T(8,128)(2,1)}, u32[]{:S(2)}) %copy-start) | copy-done | bytes 4718616
  79.6 0.0 copy-start.4
  79.6 0.0 copy-start.3
  79.6 4.6 %shard_map.46 = (bf16[1536,384]{1,0:T(8,128)(2,1)S(1)}, bf16[1536,256]{1,0:T(8,128)(2,1)S(1)}) custom-call(bf16[1536,1536]{1,0:T(8,128)(2,1)S(1)} %copy-done, bf16[1536,640]{1,0:T(8,128)(2,1)S(1)} %bitcast.33), custom_call_target="tpu_custom_call" | custom-call | flops 3019898880 | bytes 8650752 | tf_op jit(solution)/shard_map/pallas_call | solution.py:54
  84.2 0.0 copy-start.1
  84.2 0.9 copy-done.1
  85.1 3.3 %collective-permute-start.3 = (bf16[1536,384]{1,0:T(8,128)(2,1)S(1)}, bf16[1536,384]{1,0:T(8,128)(2,1)S(1)}, u32[]{:S(2)}, u32[]{:S(2)}) collective-permute-start(bf16[1536,384]{1,0:T(8,128)(2,1)S(1)} %get-tuple-element.7.own_ref), channel_id=1, source_target_pairs={{0,1},{1,0},{2,3},{3,2},{4,5},{5,4},{6,7},{7,6},{8,9},{9,8},{10,11... | collective-permute-start | bytes 3538952 | tf_op jit(solution)/shard_map/ppermute | solution.py:24
  88.5 0.6 broadcast.75
  89.0 0.0 copy-done.4
  89.0 0.6 reduce.15
  89.7 0.1 reshape_squeeze.6
  89.8 0.0 copy-done.3
  89.8 0.7 reduce.14
  90.4 0.1 reshape_squeeze.7
  90.5 0.2 fusion
  90.7 0.6 gather_fusion
  91.3 0.2 and_reduce_fusion
  91.5 0.1 broadcast_select_fusion
  91.5 0.6 select_n.83.qid_ref
  92.2 0.2 slice_reduce_fusion.1
  92.4 0.2 convert_reduce_fusion.1
  92.6 0.1 pad_add_fusion.info_ref
  92.7 23.5 %collective-permute-done.3.other_ref = bf16[1536,384]{1,0:T(8,128)(2,1)S(1)} collective-permute-done((bf16[1536,384]{1,0:T(8,128)(2,1)S(1)}, bf16[1536,384]{1,0:T(8,128)(2,1)S(1)}, u32[]{:S(2)}, u32[]{:S(2)}) %collective-permute-start.3) | collective-permute-done | bytes 1179680 | tf_op jit(solution)/shard_map/ppermute | solution.py:24
  116.2 0.0 copy-start.2
  116.2 1.1 copy-done.2
  117.3 17.5 %shard_map.47 = bf16[8,288,128]{2,1,0:T(8,128)(2,1)S(1)} custom-call(s32[33]{0:T(128)S(1)} %pad_add_fusion.info_ref, bf16[1536,384]{1,0:T(8,128)(2,1)S(1)} %get-tuple-element.7.own_ref, bf16[1536,384]{1,0:T(8,128)(2,1)S(1)} %collective-permute-done.3.other_ref, bf16[1536,256]{1,0:T(8,128)(2,1)S(1)} %copy-done.2, s32[1536,1]{1,0:T(8,128)S(1)} %select_n.83.qid_ref, ...), custom_call_target="tpu_custom_call" | custom-call | flops 8589934592 | bytes 8388608 | tf_op jit(solution)/shard_map/pallas_call | solution.py:120
  134.8 21.4 %all_to_all.11.in_ref = bf16[8,288,128]{2,1,0:T(8,128)(2,1)S(1)} all-to-all(bf16[8,288,128]{2,1,0:T(8,128)(2,1)S(1)} %shard_map.47), channel_id=1, replica_groups=mesh['y'=8,'xl'=2,'core'=2,'z'=8,'xh'=2] {'z'}, dimensions={0} | all-to-all | bytes 1179648 | tf_op jit(solution)/shard_map/all_to_all | solution.py:176
  156.3 1.1 shard_map.48
  (7 shorter events, 0.1 us)
Async XLA Ops:
  6.5 70.7 %all-gather.2.cloned.1.call-start = ((), (), s32[]{:S(2)}) async-start(), calls=%async_computation.2 | async-start | bytes 5308416 | tf_op jit(solution)/shard_map/all_gather | solution.py:172
  8.1 7.4 %collective-permute-start = (bf16[48,288]{1,0:T(8,128)(2,1)S(1)}, bf16[48,288]{1,0:T(8,128)(2,1)S(1)}, u32[]{:S(2)}, u32[]{:S(2)}) collective-permute-start(bf16[48,288]{1,0:T(8,128)(2,1)S(1)} %reshape.33), channel_id=1, source_target_pairs={{0,1},{1,0},{2,3},{3,2},{4,5},{5,4},{6,7},{7,6},{8,9},{9,8},{10,11... | collective-permute-start | bytes 82952 | tf_op jit(solution)/shard_map/ppermute | solution.py:24
  38.3 11.7 %collective-permute-start.1 = (bf16[8,48,640]{2,1,0:T(8,128)(2,1)S(1)}, bf16[8,48,640]{2,1,0:T(8,128)(2,1)S(1)}, u32[]{:S(2)}, u32[]{:S(2)}) collective-permute-start(bf16[8,48,640]{2,1,0:T(8,128)(2,1)S(1)} %all_to_all.10), channel_id=1, source_target_pairs={{0,32},{32,0},{1,33},{33,1},{2,34},{34,2},{3,35},{35,3},{4,36},{36... | collective-permute-start | bytes 1474568 | tf_op jit(solution)/shard_map/ppermute | solution.py:24
  50.2 4.5 %collective-permute-start.2 = (bf16[8,2,48,640]{3,2,1,0:T(8,128)(2,1)S(1)}, bf16[8,2,48,640]{3,2,1,0:T(8,128)(2,1)S(1)}, u32[]{:S(2)}, u32[]{:S(2)}) collective-permute-start(bf16[8,2,48,640]{3,2,1,0:T(8,128)(2,1)S(1)} %pad_maximum_fusion.1), channel_id=1, source_target_pairs={{0,16},{16,0},{1,17},{17,1},{2,18},{18,2},{3,19},{19,3},{4,20},{20... | collective-permute-start | bytes 2949128 | tf_op jit(solution)/shard_map/ppermute | solution.py:24
  77.2 2.3 %copy-start = (bf16[1536,1536]{1,0:T(8,128)(2,1)S(1)}, bf16[1536,1536]{1,0:T(8,128)(2,1)}, u32[]{:S(2)}) copy-start(bf16[1536,1536]{1,0:T(8,128)(2,1)} %all-gather.2.cloned.1.call-done.x_ref) | copy-start | bytes 14155780
  79.6 9.5 %copy-start.4 = (s32[1,16]{1,0:T(1,128)S(1)}, s32[1,16]{1,0:T(1,128)}, u32[]{:S(2)}) copy-start(s32[1,16]{1,0:T(1,128)} %param.6) | copy-start | bytes 196
  79.6 10.2 %copy-start.3 = (s32[1,3072]{1,0:T(1,128)S(1)}, s32[1,3072]{1,0:T(1,128)}, u32[]{:S(2)}) copy-start(s32[1,3072]{1,0:T(1,128)} %param.5) | copy-start | bytes 36868
  84.2 0.9 copy-start.1
  85.1 31.1 %collective-permute-start.3 = (bf16[1536,384]{1,0:T(8,128)(2,1)S(1)}, bf16[1536,384]{1,0:T(8,128)(2,1)S(1)}, u32[]{:S(2)}, u32[]{:S(2)}) collective-permute-start(bf16[1536,384]{1,0:T(8,128)(2,1)S(1)} %get-tuple-element.7.own_ref), channel_id=1, source_target_pairs={{0,1},{1,0},{2,3},{3,2},{4,5},{5,4},{6,7},{7,6},{8,9},{9,8},{10,11... | collective-permute-start | bytes 3538952 | tf_op jit(solution)/shard_map/ppermute | solution.py:24
  116.2 1.1 copy-start.2
Sparse Core Ops, SparseCore 0:
  9.4 67.7 all-gather.1

commit v2 on v1

v2 whole, which is shorter than its diff:
```python
import functools

import jax
import jax.numpy as jnp
from jax import lax
from jax.experimental import pallas as pl
from jax.experimental.pallas import tpu as pltpu
from jax.sharding import Mesh
from jax.sharding import PartitionSpec as P

HEAD = 96
FR = 192
D = 1536
NZ = 8
SEQ = 3072
TILE = 256
MAX_TILES = 8
PAD = SEQ + TILE
AXES = ("y", "xl", "core", "z", "xh")
SIZES = (8, 2, 2, 8, 2)
SLOTS = (0, -1, 1, -2, 2, -3, 3, 4)
EARLY = 3
LATE = 7
WIDE = 704
VMEM = pl.BlockSpec(memory_space=pltpu.VMEM)
SMEM = pl.BlockSpec(memory_space=pltpu.SMEM)


def swap(x, axis):
    return lax.ppermute(x, axis, [(0, 1), (1, 0)])


def shift(x, by):
    return lax.ppermute(x, "z", [(i, (i - by) % NZ) for i in range(NZ)])


def both(own, other, index, axis):
    first = jnp.where(index == 0, own, other)
    second = jnp.where(index == 0, other, own)
    return jnp.stack([first, second], axis=axis)


def near_weights(w):
    flat = jnp.transpose(w, (1, 0, 2)).reshape(w.shape[1], 3 * HEAD)
    heads = both(flat, swap(flat, "xh"), lax.axis_index("xh"), 0)
    q, k, v = (heads[:, :, t * HEAD : (t + 1) * HEAD] for t in range(3))
    zero = jnp.zeros_like(q[0, :, :64])
    shard = jnp.concatenate([zero, q[0], q[1], v[0], v[1], k[0], k[1], zero], axis=1)
    return both(shard, swap(shard, "xl"), lax.axis_index("xl"), 0).reshape(96, WIDE)


def project_body(core_ref, wa_ref, wb_ref, own_refs, partner_refs, kv_ref, q_ref, part_ref, w_ref):
    core = core_ref[0]
    for i in range(16):
        for ref, side in ((wa_ref, core), (wb_ref, 1 - core)):
            at = pl.multiple_of(i * 96 + side * 48, 16)
            w_ref[pl.ds(at, 48), :] = ref[i * 48 : (i + 1) * 48, :640]
    if partner_refs:
        x = jnp.concatenate([r[...] for r in partner_refs], axis=0)
        part_ref[...] = jnp.dot(x, w_ref[:, 256:], preferred_element_type=jnp.float32).astype(jnp.bfloat16)
    x = jnp.concatenate([r[...] for r in own_refs], axis=0)
    kv_ref[...] = jnp.dot(x, w_ref[:, 256:], preferred_element_type=jnp.float32).astype(jnp.bfloat16)
    q_ref[...] = jnp.dot(x, w_ref[:, :256], preferred_element_type=jnp.float32).astype(jnp.bfloat16)


def project(core, wa, wb, own, partner):
    n, m = len(own), len(partner)

    def kernel(core_ref, wa_ref, wb_ref, *refs):
        outs = refs[n + m :]
        part_ref = outs[2] if m else None
        project_body(core_ref, wa_ref, wb_ref, refs[:n], refs[n : n + m], outs[0], outs[1], part_ref, outs[-1])

    shapes = [(n * FR, 384), (n * FR, 256)] + ([(m * FR, 384)] if m else [])
    return pl.pallas_call(
        kernel,
        in_specs=[SMEM] + [VMEM] * (2 + n + m),
        out_specs=[VMEM] * len(shapes),
        out_shape=[jax.ShapeDtypeStruct(s, jnp.bfloat16) for s in shapes],
        scratch_shapes=[pltpu.VMEM((D, 640), jnp.bfloat16)],
        compiler_params=pltpu.CompilerParams(vmem_limit_bytes=32 << 20),
        cost_estimate=pl.CostEstimate(flops=2 * (n + m) * FR * D * 640, bytes_accessed=4 << 20, transcendentals=0),
    )(core, wa, wb, *own, *partner)


def attend_kernel(info_ref, qid_ref, kid_ref, kva, kvb, qa, qb, part, kvra, kvrb, out_ref, kv_ref, q_ref):
    kv_ref[SEQ:, :] = jnp.zeros((TILE, 384), jnp.bfloat16)
    for s in range(NZ):
        own, i = (kva, s) if s < LATE else (kvb, s - LATE)
        kv_ref[pl.ds(pl.multiple_of(info_ref[s] * FR, FR), FR), :] = own[i * FR : (i + 1) * FR, :]
        if s < EARLY:
            other, i = part, s
        else:
            other, i = (kvra, s - EARLY) if s < LATE else (kvrb, s - LATE)
        kv_ref[pl.ds(pl.multiple_of(info_ref[8 + s] * FR, FR), FR), :] = other[i * FR : (i + 1) * FR, :]
    q_ref[: LATE * FR, :] = qa[...]
    q_ref[LATE * FR :, :] = qb[...]
    scale = HEAD**-0.5 * 1.4426950408889634
    lane = lax.broadcasted_iota(jnp.int32, (FR, 256), 1)
    half = lax.broadcasted_iota(jnp.int32, (FR // 2, 128), 1) < 64

    def attend_jobs(jobs, n):
        scores, tops, outs = [], [], []
        for q, qid, first in jobs:
            tiles, top = [], None
            for t in range(n):
                at = pl.multiple_of(first + t * TILE, 128)
                s = lax.dot_general(
                    q, kv_ref[pl.ds(at, TILE), 128:], (((1,), (1,)), ((), ())), preferred_element_type=jnp.float32
                )
                s = jnp.where(qid == kid_ref[:, pl.ds(at, TILE)], s, -1e30)
                tiles.append(s)
                most = jnp.maximum(s[:, :128], s[:, 128:])
                top = most if top is None else jnp.maximum(top, most)
            scores.append(tiles)
            tops.append(jnp.max(top, axis=1, keepdims=True))
        for (q, qid, first), tiles, top in zip(jobs, scores, tops):
            total = acc = None
            for t in range(n):
                at = pl.multiple_of(first + t * TILE, 128)
                p = jnp.exp2((tiles[t] - top) * scale)
                part_sum = p[:, :128] + p[:, 128:]
                out = jnp.dot(p.astype(jnp.bfloat16), kv_ref[pl.ds(at, TILE), :256], preferred_element_type=jnp.float32)
                total = part_sum if total is None else total + part_sum
                acc = out if acc is None else acc + out
            outs.append(acc * (1.0 / jnp.sum(total, axis=1, keepdims=True)))
        return outs

    def pair(g, _):
        slots = [info_ref[32 + 2 * g + i] for i in range(2)]
        count = info_ref[24 + slots[1]]
        jobs = []
        for s in slots:
            rows = pl.ds(pl.multiple_of(s * FR, FR), FR)
            q = q_ref[rows, :]
            zero = jnp.zeros_like(q)
            first = jnp.minimum(info_ref[16 + s], PAD - count * TILE)
            for head in (lane < 160, lane >= 160):
                jobs.append((jnp.where(head, q, zero), qid_ref[rows, :], first))

        def attend_pair(n):
            outs = attend_jobs(jobs, n)
            for i, s in enumerate(slots):
                z = info_ref[40 + s]
                o = jnp.where(lane < HEAD, outs[2 * i], outs[2 * i + 1])
                tail = o[:, 128:]
                out_ref[z, :FR, :] = o[:, :128].astype(jnp.bfloat16)
                packed = jnp.where(half, tail[: FR // 2], pltpu.roll(tail[FR // 2 :], 64, 1))
                out_ref[z, FR:, :] = packed.astype(jnp.bfloat16)

        for n in range(1, MAX_TILES + 1):
            pl.when(count == n)(functools.partial(attend_pair, n))
        return 0

    lax.fori_loop(0, NZ // 2, pair, 0)


def attend(*args):
    return pl.pallas_call(
        attend_kernel,
        in_specs=[SMEM] + [VMEM] * (len(args) - 1),
        out_specs=VMEM,
        out_shape=jax.ShapeDtypeStruct((NZ, FR * 3 // 2, 128), jnp.bfloat16),
        scratch_shapes=[pltpu.VMEM((PAD, 384), jnp.bfloat16), pltpu.VMEM((NZ * FR, 256), jnp.bfloat16)],
        compiler_params=pltpu.CompilerParams(vmem_limit_bytes=40 << 20),
        cost_estimate=pl.CostEstimate(flops=8 << 30, bytes_accessed=8 << 20, transcendentals=4 << 20),
    )(*args)


def unpack_kernel(in_ref, out_ref):
    half = lax.broadcasted_iota(jnp.int32, (FR, 128), 1) < 64
    for z in range(0, NZ, 2):
        tails = []
        for i in (z, z + 1):
            packed = in_ref[i, FR:, :].astype(jnp.float32)
            tails.append(jnp.concatenate([packed, pltpu.roll(packed, 64, 1)], axis=0))
        second = pltpu.roll(in_ref[z + 1, :FR, :].astype(jnp.float32), 64, 1)
        out_ref[:, z * 192 : z * 192 + 128] = in_ref[z, :FR, :]
        out_ref[:, z * 192 + 128 : z * 192 + 256] = jnp.where(half, tails[0], second).astype(jnp.bfloat16)
        out_ref[:, z * 192 + 256 : z * 192 + 384] = jnp.where(half, second, pltpu.roll(tails[1], 64, 1)).astype(jnp.bfloat16)


def unpack(packed):
    return pl.pallas_call(
        unpack_kernel,
        in_specs=[VMEM],
        out_specs=VMEM,
        out_shape=jax.ShapeDtypeStruct((FR, D), jnp.bfloat16),
        compiler_params=pltpu.CompilerParams(vmem_limit_bytes=8 << 20),
    )(packed)


def plan(ids, order, z, xh):
    blocks = ids.reshape(16, FR)
    zs = (z + jnp.asarray(SLOTS, jnp.int32)) % NZ
    places = jnp.take(order.reshape(NZ, 2), zs, axis=0)
    own = jnp.where(xh == 0, places[:, 0], places[:, 1])
    other = jnp.where(xh == 0, places[:, 1], places[:, 0])
    qid = jnp.take(blocks, own, axis=0)
    first = jnp.sum(ids[None, :] < qid[:, :1], axis=1, dtype=jnp.int32)
    last = jnp.sum(ids[None, :] <= qid[:, FR - 1 :], axis=1, dtype=jnp.int32)
    first = first // 128 * 128
    count = (last - first + TILE - 1) // TILE
    i = jnp.arange(NZ, dtype=jnp.int32)
    ahead = (count[None, :] < count[:, None]) | ((count[None, :] == count[:, None]) & (i[None, :] < i[:, None]))
    rank = jnp.sum(ahead, axis=1, dtype=jnp.int32)
    ranked = jnp.sum(jnp.where(rank[:, None] == i[None, :], i[:, None], 0), axis=0, dtype=jnp.int32)
    info = jnp.concatenate([own, other, first, count, ranked, zs])
    kid = jnp.concatenate([ids, jnp.full((TILE,), -1, jnp.int32)])[None]
    return info, qid.reshape(NZ * FR, 1), kid


def body(frames, seg_ids, assign, w_qkv):
    z, xh, core = (lax.axis_index(a) for a in ("z", "xh", "core"))
    near = near_weights(w_qkv)
    up, down, slots = frames, frames, [frames]
    for _ in range(3):
        up, down = shift(up, -1), shift(down, 1)
        slots += [up, down]
    mine = jnp.where(core == 0, up, down)
    by_core = [(c * NZ + i, c * NZ + (i + (1, -1)[c]) % NZ) for c in (0, 1) for i in range(NZ)]
    slots.append(lax.ppermute(mine, ("core", "z"), by_core))
    wa = lax.all_gather(near, "y", axis=0, tiled=True)
    wb = swap(wa, "core")
    early = [lax.optimization_barrier((slots[0], near))[0]] + slots[1:EARLY]
    partner = [swap(s, "xh") for s in early]
    info, qid, kid = plan(seg_ids[0], assign[0], z, xh)
    at = core.astype(jnp.int32)[None]
    kva, qa, part = project(at, wa, wb, slots[:LATE], partner)
    kvra = swap(kva[EARLY * FR :], "xh")
    kvb, qb = project(at, wa, wb, slots[LATE:], [])
    kvrb = swap(kvb, "xh")
    packed = attend(info, qid, kid, kva, kvb, qa, qb, part, kvra, kvrb)
    return unpack(lax.all_to_all(packed, "z", 0, 0, tiled=True))


def solution(mesh):
    fine = Mesh(mesh.devices.reshape(SIZES), AXES)
    dp, ctx = AXES[:3], AXES[3:]
    return jax.shard_map(
        body,
        mesh=fine,
        in_specs=(P(AXES, None), P(dp, None), P(dp, None), P(None, dp, ctx)),
        out_specs=P(AXES, None),
        check_vma=False,
    )
```

time: 167 us -> 196 us (1.17)
  starting transfers between devices: 11.3 us -> 57.8 us
  blocking collectives: 44 us -> 26.3 us
  Pallas kernels: 23.3 us -> 16.5 us
  local copies, waits for them, and re-layouts: 7.56 us -> 13.6 us
  other arithmetic: 2.75 us -> 5.27 us
    ppermute x0 -> x7, starting transfers between devices: none -> 29.4 us  [the longest x6 25.8 us: shift(): return lax.ppermute(x, 'z', [(i, (i - by) % NZ) for i in range(NZ)])]
    all_to_all x1 -> x0, blocking collectives: 22.5 us -> none  [gather_weights(): lax.all_to_all(jnp.broadcast_to(shard[None], (8,) + shard.shape), 'y', 0,...]
    all_gather x1, waiting for transfers between devices: 22.1 us -> 1.12 us  [body(): wa = lax.all_gather(near, 'y', axis=0, tiled=True)]
    ppermute x4 -> x8, starting transfers between devices: 11.3 us -> 28.4 us  [swap(): return lax.ppermute(x, axis, [(0, 1), (1, 0)])]
    ppermute x0 -> x7, waiting for transfers between devices: none -> 15.7 us  [the longest x6 15.7 us: shift(): return lax.ppermute(x, 'z', [(i, (i - by) % NZ) for i in range(NZ)])]
    pallas_call x3 -> x4, Pallas kernels: 23.3 us -> 16.5 us  [the longest x2 8.23 us: project(): pl.pallas_call(kernel, in_specs=[SMEM] + [VMEM] * (2 + n + m), out_specs=...]
    ppermute x4 -> x8, waiting for transfers between devices: 39 us -> 44.6 us  [swap(): return lax.ppermute(x, axis, [(0, 1), (1, 0)])]
    all_to_all x1, blocking collectives: 21.4 us -> 26.3 us  [body(): return unpack(lax.all_to_all(packed, 'z', 0, 0, tiled=True))]
  transfers between devices with their start and end apart: 5 -> 16, of which waited for: 5 -> 9; matrix products, arithmetic and copies ran while one was open for 4% -> 6% of each run, Pallas kernels for 0% -> 4%
where the time goes in v2:
time: 196 us; the launch traced here: 195 us
  waiting for transfers between devices  61.5 us (31%)
  starting transfers between devices  57.8 us (29%)
  blocking collectives  26.3 us (13%)
  Pallas kernels  16.5 us (8%)
  between operations  13.9 us (7%)
  local copies, waits for them, and re-layouts  13.6 us (7%)
  other arithmetic  5.27 us (3%)
    ppermute x8, waiting for transfers between devices, swap(): return lax.ppermute(x, axis, [(0, 1), (1, 0)])  44.6 us
    ppermute x8, starting transfers between devices, swap(): return lax.ppermute(x, axis, [(0, 1), (1, 0)])  28.4 us
    all_to_all x1, blocking collectives, body(): return unpack(lax.all_to_all(packed, 'z', 0, 0, tiled=True))  26.3 us
    ppermute x6, starting transfers between devices, shift(): return lax.ppermute(x, 'z', [(i, (i - by) % NZ) for i in range(NZ)])  25.8 us
    ppermute x6, waiting for transfers between devices, shift(): return lax.ppermute(x, 'z', [(i, (i - by) % NZ) for i in range(NZ)])  15.7 us
    pallas_call x2, Pallas kernels, project(): pl.pallas_call(kernel, in_specs=[SMEM] + [VMEM] * (2 + n + m), out_specs=...  8.23 us
    pallas_call x1, Pallas kernels, attend(): pl.pallas_call(attend_kernel, in_specs=[SMEM] + [VMEM] * (len(args) - 1),...  7.13 us
    unnamed x43, local copies, waits for them, and re-layouts  6.1 us
  transfers between devices with their start and end apart: 16, of which 9 were waited for; matrix products, arithmetic and copies ran while one was open for 6% of the time, Pallas kernels for 4%

profile of v2, /device:TPU:6, one launch (start us, length us, event | category | flops | bytes accessed | tf_op | source)
XLA Modules:
  0.0 194.7 jit_solution(6024278991288556906)
XLA Ops:
  6.5 0.8 copy.13
  7.5 3.3 %collective-permute-start = (bf16[48,288]{1,0:T(8,128)(2,1)S(1)}, bf16[48,288]{1,0:T(8,128)(2,1)S(1)}, u32[]{:S(2)}, u32[]{:S(2)}) collective-permute-start(bf16[48,288]{1,0:T(8,128)(2,1)S(1)} %reshape.116), channel_id=1, source_target_pairs={{0,1},{1,0},{2,3},{3,2},{4,5},{5,4},{6,7},{7,6},{8,9},{9,8},{10,11... | collective-permute-start | bytes 82952 | tf_op jit(solution)/shard_map/ppermute | solution.py:30
  10.8 4.0 %collective-permute-done = bf16[48,288]{1,0:T(8,128)(2,1)S(1)} collective-permute-done((bf16[48,288]{1,0:T(8,128)(2,1)S(1)}, bf16[48,288]{1,0:T(8,128)(2,1)S(1)}, u32[]{:S(2)}, u32[]{:S(2)}) %collective-permute-start) | collective-permute-done | bytes 27680 | tf_op jit(solution)/shard_map/ppermute | solution.py:30
  15.0 5.1 %collective-permute-start.1 = (bf16[48,704]{1,0:T(8,128)(2,1)S(1)}, bf16[48,704]{1,0:T(8,128)(2,1)S(1)}, u32[]{:S(2)}, u32[]{:S(2)}) collective-permute-start(bf16[48,704]{1,0:T(8,128)(2,1)S(1)} %concatenate.11), channel_id=1, source_target_pairs={{0,32},{32,0},{1,33},{33,1},{2,34},{34,2},{3,35},{35,3},{4,36},{36... | collective-permute-start | bytes 202760 | tf_op jit(solution)/shard_map/ppermute | solution.py:30
  20.2 2.3 %collective-permute-done.1 = bf16[48,704]{1,0:T(8,128)(2,1)S(1)} collective-permute-done((bf16[48,704]{1,0:T(8,128)(2,1)S(1)}, bf16[48,704]{1,0:T(8,128)(2,1)S(1)}, u32[]{:S(2)}, u32[]{:S(2)}) %collective-permute-start.1) | collective-permute-done | bytes 67616 | tf_op jit(solution)/shard_map/ppermute | solution.py:30
  22.5 0.7 pad_maximum_fusion
  23.2 3.1 %collective-permute-start.3 = (bf16[192,1536]{1,0:T(8,128)(2,1)}, bf16[192,1536]{1,0:T(8,128)(2,1)}, u32[]{:S(2)}, u32[]{:S(2)}) collective-permute-start(bf16[192,1536]{1,0:T(8,128)(2,1)} %refs_0_.1), channel_id=1, source_target_pairs={{0,2},{2,4},{4,6},{6,8},{8,10},{10,12},{12,14},{14,0},{1,3},{3,5},... | collective-permute-start | bytes 1769480 | tf_op jit(solution)/shard_map/ppermute | solution.py:34
  26.3 8.6 %collective-permute-start.4 = (bf16[192,1536]{1,0:T(8,128)(2,1)}, bf16[192,1536]{1,0:T(8,128)(2,1)}, u32[]{:S(2)}, u32[]{:S(2)}) collective-permute-start(bf16[192,1536]{1,0:T(8,128)(2,1)} %refs_0_.1), channel_id=1, source_target_pairs={{0,14},{2,0},{4,2},{6,4},{8,6},{10,8},{12,10},{14,12},{1,15},{3,1}... | collective-permute-start | bytes 1769480 | tf_op jit(solution)/shard_map/ppermute | solution.py:34
  34.9 9.4 %collective-permute-done.3.refs_1_ = bf16[192,1536]{1,0:T(8,128)(2,1)} collective-permute-done((bf16[192,1536]{1,0:T(8,128)(2,1)}, bf16[192,1536]{1,0:T(8,128)(2,1)}, u32[]{:S(2)}, u32[]{:S(2)}) %collective-permute-start.3) | collective-permute-done | bytes 589856 | tf_op jit(solution)/shard_map/ppermute | solution.py:34
  44.3 1.9 collective-permute-start.5
  46.3 5.1 %collective-permute-start.6 = (bf16[192,1536]{1,0:T(8,128)(2,1)}, bf16[192,1536]{1,0:T(8,128)(2,1)S(1)}, u32[]{:S(2)}, u32[]{:S(2)}) collective-permute-start(bf16[192,1536]{1,0:T(8,128)(2,1)} %collective-permute-done.4.refs_2_), channel_id=1, source_target_pairs={{0,14},{2,0},{4,2},{6,4},{8,6},{10,8},{12,10},{14,12},{1,15},{3,1}... | collective-permute-start | bytes 1769480 | tf_op jit(solution)/shard_map/ppermute | solution.py:34
  51.4 0.6 broadcast.228
  52.0 0.7 reduce.17
  52.8 0.6 gather_fusion
  53.4 6.3 %collective-permute-done.5.refs_3_ = bf16[192,1536]{1,0:T(8,128)(2,1)S(1)} collective-permute-done((bf16[192,1536]{1,0:T(8,128)(2,1)}, bf16[192,1536]{1,0:T(8,128)(2,1)S(1)}, u32[]{:S(2)}, u32[]{:S(2)}) %collective-permute-start.5) | collective-permute-done | bytes 589856 | tf_op jit(solution)/shard_map/ppermute | solution.py:34
  59.7 1.9 collective-permute-start.7
  61.9 5.1 %collective-permute-start.8 = (bf16[192,1536]{1,0:T(8,128)(2,1)S(1)}, bf16[192,1536]{1,0:T(8,128)(2,1)S(1)}, u32[]{:S(2)}, u32[]{:S(2)}) collective-permute-start(bf16[192,1536]{1,0:T(8,128)(2,1)S(1)} %collective-permute-done.6.refs_4_), channel_id=1, source_target_pairs={{0,14},{2,0},{4,2},{6,4},{8,6},{10,8},{12,10},{14,12},{1,15},{3,1}... | collective-permute-start | bytes 1769480 | tf_op jit(solution)/shard_map/ppermute | solution.py:34
  67.0 1.1 all-gather.2.cloned.1.call-done.wa_ref
  68.1 1.6 copy.14
  69.8 1.9 collective-permute-start.2
  71.7 0.6 fusion.2
  72.3 0.7 reduce.18
  73.1 0.6 gather_fusion.1
  74.0 3.4 %collective-permute-start.9 = (bf16[192,1536]{1,0:T(8,128)(2,1)}, bf16[192,1536]{1,0:T(8,128)(2,1)}, u32[]{:S(2)}, u32[]{:S(2)}) collective-permute-start(bf16[192,1536]{1,0:T(8,128)(2,1)} %refs_0_.1), channel_id=1, source_target_pairs={{0,1},{1,0},{2,3},{3,2},{4,5},{5,4},{6,7},{7,6},{8,9},{9,8},{10,11... | collective-permute-start | bytes 1769480 | tf_op jit(solution)/shard_map/ppermute | solution.py:30
  77.3 4.0 %collective-permute-start.10 = (bf16[192,1536]{1,0:T(8,128)(2,1)}, bf16[192,1536]{1,0:T(8,128)(2,1)}, u32[]{:S(2)}, u32[]{:S(2)}) collective-permute-start(bf16[192,1536]{1,0:T(8,128)(2,1)} %collective-permute-done.3.refs_1_), channel_id=1, source_target_pairs={{0,1},{1,0},{2,3},{3,2},{4,5},{5,4},{6,7},{7,6},{8,9},{9,8},{10,11... | collective-permute-start | bytes 1769480 | tf_op jit(solution)/shard_map/ppermute | solution.py:30
  81.4 3.4 %collective-permute-start.11 = (bf16[192,1536]{1,0:T(8,128)(2,1)}, bf16[192,1536]{1,0:T(8,128)(2,1)}, u32[]{:S(2)}, u32[]{:S(2)}) collective-permute-start(bf16[192,1536]{1,0:T(8,128)(2,1)} %collective-permute-done.4.refs_2_), channel_id=1, source_target_pairs={{0,1},{1,0},{2,3},{3,2},{4,5},{5,4},{6,7},{7,6},{8,9},{9,8},{10,11... | collective-permute-start | bytes 1769480 | tf_op jit(solution)/shard_map/ppermute | solution.py:30
  84.7 0.8 convert_reduce_fusion
  85.5 0.9 broadcast_select_fusion
  86.4 3.6 %collective-permute-start.12 = (bf16[192,1536]{1,0:T(8,128)(2,1)}, bf16[192,1536]{1,0:T(8,128)(2,1)}, u32[]{:S(2)}, u32[]{:S(2)}) collective-permute-start(bf16[192,1536]{1,0:T(8,128)(2,1)} %broadcast_select_fusion), channel_id=1, source_target_pairs={{0,2},{2,4},{4,6},{6,8},{8,10},{10,12},{12,14},{14,0},{16,30},{18,... | collective-permute-start | bytes 1769480 | tf_op jit(solution)/shard_map/ppermute | solution.py:222
  90.1 1.6 copy.15.wb_ref
  91.6 2.2 %collective-permute-done.9.refs_7_ = bf16[192,1536]{1,0:T(8,128)(2,1)} collective-permute-done((bf16[192,1536]{1,0:T(8,128)(2,1)}, bf16[192,1536]{1,0:T(8,128)(2,1)}, u32[]{:S(2)}, u32[]{:S(2)}) %collective-permute-start.9) | collective-permute-done | bytes 589856 | tf_op jit(solution)/shard_map/ppermute | solution.py:30
  93.8 12.6 %collective-permute-done.10.refs_8_ = bf16[192,1536]{1,0:T(8,128)(2,1)} collective-permute-done((bf16[192,1536]{1,0:T(8,128)(2,1)}, bf16[192,1536]{1,0:T(8,128)(2,1)}, u32[]{:S(2)}, u32[]{:S(2)}) %collective-permute-start.10) | collective-permute-done | bytes 589856 | tf_op jit(solution)/shard_map/ppermute | solution.py:30
  106.5 12.2 %collective-permute-done.11.refs_9_ = bf16[192,1536]{1,0:T(8,128)(2,1)} collective-permute-done((bf16[192,1536]{1,0:T(8,128)(2,1)}, bf16[192,1536]{1,0:T(8,128)(2,1)}, u32[]{:S(2)}, u32[]{:S(2)}) %collective-permute-start.11) | collective-permute-done | bytes 589856 | tf_op jit(solution)/shard_map/ppermute | solution.py:30
  118.7 1.1 copy-done.4
  119.8 1.1 copy-done.6
  120.8 6.4 %shard_map.55 = (bf16[1344,384]{1,0:T(8,128)(2,1)S(1)}, bf16[1344,256]{1,0:T(8,128)(2,1)S(1)}, bf16[576,384]{1,0:T(8,128)(2,1)S(1)}) custom-call(s32[1]{0:T(128)} %bitcast.1.core_ref, bf16[768,704]{1,0:T(8,128)(2,1)S(1)} %copy-done, bf16[768,704]{1,0:T(8,128)(2,1)S(1)} %copy.15.wb_ref, bf16[192,1536]{1,0:T(8,128)(2,1)} %refs_0_.1, ...), custom_call_target="tpu_custom_call" | custom-call | flops 3774873600 | bytes 4194304 | tf_op jit(solution)/shard_map/pallas_call | solution.py:75
  127.3 1.0 slice.60
  128.3 3.3 %collective-permute-start.13 = (bf16[768,384]{1,0:T(8,128)(2,1)}, bf16[768,384]{1,0:T(8,128)(2,1)S(1)}, u32[]{:S(2)}, u32[]{:S(2)}) collective-permute-start(bf16[768,384]{1,0:T(8,128)(2,1)} %slice.60), channel_id=1, source_target_pairs={{0,1},{1,0},{2,3},{3,2},{4,5},{5,4},{6,7},{7,6},{8,9},{9,8},{10,11... | collective-permute-start | bytes 1769480 | tf_op jit(solution)/shard_map/ppermute | solution.py:30
  131.9 1.8 shard_map.56
  133.8 4.0 %collective-permute-start.14 = (bf16[192,384]{1,0:T(8,128)(2,1)S(1)}, bf16[192,384]{1,0:T(8,128)(2,1)S(1)}, u32[]{:S(2)}, u32[]{:S(2)}) collective-permute-start(bf16[192,384]{1,0:T(8,128)(2,1)S(1)} %get-tuple-element.13.kvb), channel_id=1, source_target_pairs={{0,1},{1,0},{2,3},{3,2},{4,5},{5,4},{6,7},{7,6},{8,9},{9,8},{10,11... | collective-permute-start | bytes 442376 | tf_op jit(solution)/shard_map/ppermute | solution.py:30
  137.9 0.6 select_n.137.qid_ref
  138.8 11.2 %collective-permute-done.14.kvrb = bf16[192,384]{1,0:T(8,128)(2,1)S(1)} collective-permute-done((bf16[192,384]{1,0:T(8,128)(2,1)S(1)}, bf16[192,384]{1,0:T(8,128)(2,1)S(1)}, u32[]{:S(2)}, u32[]{:S(2)}) %collective-permute-start.14) | collective-permute-done | bytes 147488 | tf_op jit(solution)/shard_map/ppermute | solution.py:30
  150.0 1.2 copy-done.2
  151.2 1.1 copy-done.8
  152.3 1.0 copy-done.10
  153.3 7.1 %shard_map.57 = bf16[8,288,128]{2,1,0:T(8,128)(2,1)S(1)} custom-call(s32[48]{0:T(128)S(1)} %concatenate.9.info_ref, s32[1536,1]{1,0:T(8,128)S(1)} %select_n.137.qid_ref, s32[1,3328]{1,0:T(1,128)S(1)} %broadcast_in_dim.52.kid_ref, bf16[1344,384]{1,0:T(8,128)(2,1)S(1)} %copy-done.2, bf16[192,384]{1,0:T(8,128)(2,1)S(1)} %get-tuple-element.13.kvb, ...), custom_call_target="tpu_custom_call" | custom-call | flops 8589934592 | bytes 8388608 | tf_op jit(solution)/shard_map/pallas_call | solution.py:159
  160.5 26.3 %all_to_all.5.in_ref = bf16[8,288,128]{2,1,0:T(8,128)(2,1)S(1)} all-to-all(bf16[8,288,128]{2,1,0:T(8,128)(2,1)S(1)} %shard_map.57), channel_id=1, replica_groups=mesh['y'=8,'xl'=2,'core'=2,'z'=8,'xh'=2] {'z'}, dimensions={0} | all-to-all | bytes 1179648 | tf_op jit(solution)/shard_map/all_to_all | solution.py:234
  186.7 1.1 shard_map.58
  (69 shorter events, 1.7 us)
Async XLA Ops:
  6.5 39.7 %copy-start.19 = (s32[8]{0:T(128)S(1)}, s32[8]{0:T(128)}, u32[]{:S(2)}) copy-start(s32[8]{0:T(128)} %constant.96.clone) | copy-start | bytes 100
  6.5 45.5 %copy-start.20 = (s32[1,16]{1,0:T(1,128)S(1)}, s32[1,16]{1,0:T(1,128)}, u32[]{:S(2)}) copy-start(s32[1,16]{1,0:T(1,128)} %param.7) | copy-start | bytes 196
  6.5 61.6 %all-gather.2.cloned.1.call-start = ((), (), s32[]{:S(2)}) async-start(), calls=%async_computation.1 | async-start | bytes 1327104 | tf_op jit(solution)/shard_map/all_gather | solution.py:223
  7.5 7.4 %collective-permute-start = (bf16[48,288]{1,0:T(8,128)(2,1)S(1)}, bf16[48,288]{1,0:T(8,128)(2,1)S(1)}, u32[]{:S(2)}, u32[]{:S(2)}) collective-permute-start(bf16[48,288]{1,0:T(8,128)(2,1)S(1)} %reshape.116), channel_id=1, source_target_pairs={{0,1},{1,0},{2,3},{3,2},{4,5},{5,4},{6,7},{7,6},{8,9},{9,8},{10,11... | collective-permute-start | bytes 82952 | tf_op jit(solution)/shard_map/ppermute | solution.py:30
  15.0 7.4 %collective-permute-start.1 = (bf16[48,704]{1,0:T(8,128)(2,1)S(1)}, bf16[48,704]{1,0:T(8,128)(2,1)S(1)}, u32[]{:S(2)}, u32[]{:S(2)}) collective-permute-start(bf16[48,704]{1,0:T(8,128)(2,1)S(1)} %concatenate.11), channel_id=1, source_target_pairs={{0,32},{32,0},{1,33},{33,1},{2,34},{34,2},{3,35},{35,3},{4,36},{36... | collective-permute-start | bytes 202760 | tf_op jit(solution)/shard_map/ppermute | solution.py:30
  23.2 21.1 %collective-permute-start.3 = (bf16[192,1536]{1,0:T(8,128)(2,1)}, bf16[192,1536]{1,0:T(8,128)(2,1)}, u32[]{:S(2)}, u32[]{:S(2)}) collective-permute-start(bf16[192,1536]{1,0:T(8,128)(2,1)} %refs_0_.1), channel_id=1, source_target_pairs={{0,2},{2,4},{4,6},{6,8},{8,10},{10,12},{12,14},{14,0},{1,3},{3,5},... | collective-permute-start | bytes 1769480 | tf_op jit(solution)/shard_map/ppermute | solution.py:34
  26.3 20.0 %collective-permute-start.4 = (bf16[192,1536]{1,0:T(8,128)(2,1)}, bf16[192,1536]{1,0:T(8,128)(2,1)}, u32[]{:S(2)}, u32[]{:S(2)}) collective-permute-start(bf16[192,1536]{1,0:T(8,128)(2,1)} %refs_0_.1), channel_id=1, source_target_pairs={{0,14},{2,0},{4,2},{6,4},{8,6},{10,8},{12,10},{14,12},{1,15},{3,1}... | collective-permute-start | bytes 1769480 | tf_op jit(solution)/shard_map/ppermute | solution.py:34
  34.9 37.4 %copy-start.11 = (s32[1,3072]{1,0:T(1,128)S(1)}, s32[1,3072]{1,0:T(1,128)}, u32[]{:S(2)}) copy-start(s32[1,3072]{1,0:T(1,128)} %param.6) | copy-start | bytes 36868
  44.3 15.4 %collective-permute-start.5 = (bf16[192,1536]{1,0:T(8,128)(2,1)}, bf16[192,1536]{1,0:T(8,128)(2,1)S(1)}, u32[]{:S(2)}, u32[]{:S(2)}) collective-permute-start(bf16[192,1536]{1,0:T(8,128)(2,1)} %collective-permute-done.3.refs_1_), channel_id=1, source_target_pairs={{0,2},{2,4},{4,6},{6,8},{8,10},{10,12},{12,14},{14,0},{1,3},{3,5},... | collective-permute-start | bytes 1769480 | tf_op jit(solution)/shard_map/ppermute | solution.py:34
  46.3 5.8 %copy-start.15 = (s32[8]{0:T(128)}, s32[8]{0:T(128)S(1)}, u32[]{:S(2)}) copy-start(s32[8]{0:T(128)S(1)} %get-tuple-element.28) | copy-start | bytes 100
  46.3 15.6 %collective-permute-start.6 = (bf16[192,1536]{1,0:T(8,128)(2,1)}, bf16[192,1536]{1,0:T(8,128)(2,1)S(1)}, u32[]{:S(2)}, u32[]{:S(2)}) collective-permute-start(bf16[192,1536]{1,0:T(8,128)(2,1)} %collective-permute-done.4.refs_2_), channel_id=1, source_target_pairs={{0,14},{2,0},{4,2},{6,4},{8,6},{10,8},{12,10},{14,12},{1,15},{3,1}... | collective-permute-start | bytes 1769480 | tf_op jit(solution)/shard_map/ppermute | solution.py:34
  59.7 14.0 %copy-start.3 = (bf16[192,1536]{1,0:T(8,128)(2,1)}, bf16[192,1536]{1,0:T(8,128)(2,1)S(1)}, u32[]{:S(2)}) copy-start(bf16[192,1536]{1,0:T(8,128)(2,1)S(1)} %collective-permute-done.5.refs_3_) | copy-start | bytes 1769476
  59.7 21.6 %collective-permute-start.7 = (bf16[192,1536]{1,0:T(8,128)(2,1)S(1)}, bf16[192,1536]{1,0:T(8,128)(2,1)S(1)}, u32[]{:S(2)}, u32[]{:S(2)}) collective-permute-start(bf16[192,1536]{1,0:T(8,128)(2,1)S(1)} %collective-permute-done.5.refs_3_), channel_id=1, source_target_pairs={{0,2},{2,4},{4,6},{6,8},{8,10},{10,12},{12,14},{14,0},{1,3},{3,5},... | collective-permute-start | bytes 1769480 | tf_op jit(solution)/shard_map/ppermute | solution.py:34
  61.9 11.9 %copy-start.5 = (bf16[192,1536]{1,0:T(8,128)(2,1)}, bf16[192,1536]{1,0:T(8,128)(2,1)S(1)}, u32[]{:S(2)}) copy-start(bf16[192,1536]{1,0:T(8,128)(2,1)S(1)} %collective-permute-done.6.refs_4_) | copy-start | bytes 1769476
  61.9 23.7 %collective-permute-start.8 = (bf16[192,1536]{1,0:T(8,128)(2,1)S(1)}, bf16[192,1536]{1,0:T(8,128)(2,1)S(1)}, u32[]{:S(2)}, u32[]{:S(2)}) collective-permute-start(bf16[192,1536]{1,0:T(8,128)(2,1)S(1)} %collective-permute-done.6.refs_4_), channel_id=1, source_target_pairs={{0,14},{2,0},{4,2},{6,4},{8,6},{10,8},{12,10},{14,12},{1,15},{3,1}... | collective-permute-start | bytes 1769480 | tf_op jit(solution)/shard_map/ppermute | solution.py:34
  69.8 20.3 %collective-permute-start.2 = (bf16[768,704]{0,1:T(8,128)(2,1)S(1)}, bf16[768,704]{0,1:T(8,128)(2,1)}, u32[]{:S(2)}, u32[]{:S(2)}) collective-permute-start(bf16[768,704]{0,1:T(8,128)(2,1)S(1)} %copy.14), channel_id=1, source_target_pairs={{0,16},{16,0},{1,17},{17,1},{2,18},{18,2},{3,19},{19,3},{4,20},{20... | collective-permute-start | bytes 3244040 | tf_op jit(solution)/shard_map/ppermute | solution.py:30
  73.8 16.3 %copy-start.12 = (s32[8,192]{1,0:T(8,128)}, s32[8,192]{1,0:T(8,128)S(1)}, u32[]{:S(2)}) copy-start(s32[8,192]{1,0:T(8,128)S(1)} %broadcast_select_fusion.1) | copy-start | bytes 18436
  74.0 19.8 %collective-permute-start.9 = (bf16[192,1536]{1,0:T(8,128)(2,1)}, bf16[192,1536]{1,0:T(8,128)(2,1)}, u32[]{:S(2)}, u32[]{:S(2)}) collective-permute-start(bf16[192,1536]{1,0:T(8,128)(2,1)} %refs_0_.1), channel_id=1, source_target_pairs={{0,1},{1,0},{2,3},{3,2},{4,5},{5,4},{6,7},{7,6},{8,9},{9,8},{10,11... | collective-permute-start | bytes 1769480 | tf_op jit(solution)/shard_map/ppermute | solution.py:30
  77.3 29.1 %collective-permute-start.10 = (bf16[192,1536]{1,0:T(8,128)(2,1)}, bf16[192,1536]{1,0:T(8,128)(2,1)}, u32[]{:S(2)}, u32[]{:S(2)}) collective-permute-start(bf16[192,1536]{1,0:T(8,128)(2,1)} %collective-permute-done.3.refs_1_), channel_id=1, source_target_pairs={{0,1},{1,0},{2,3},{3,2},{4,5},{5,4},{6,7},{7,6},{8,9},{9,8},{10,11... | collective-permute-start | bytes 1769480 | tf_op jit(solution)/shard_map/ppermute | solution.py:30
  81.4 37.4 %collective-permute-start.11 = (bf16[192,1536]{1,0:T(8,128)(2,1)}, bf16[192,1536]{1,0:T(8,128)(2,1)}, u32[]{:S(2)}, u32[]{:S(2)}) collective-permute-start(bf16[192,1536]{1,0:T(8,128)(2,1)} %collective-permute-done.4.refs_2_), channel_id=1, source_target_pairs={{0,1},{1,0},{2,3},{3,2},{4,5},{5,4},{6,7},{7,6},{8,9},{9,8},{10,11... | collective-permute-start | bytes 1769480 | tf_op jit(solution)/shard_map/ppermute | solution.py:30
  86.4 32.3 %copy-start = (bf16[768,704]{1,0:T(8,128)(2,1)S(1)}, bf16[768,704]{1,0:T(8,128)(2,1)}, u32[]{:S(2)}) copy-start(bf16[768,704]{1,0:T(8,128)(2,1)} %all-gather.2.cloned.1.call-done.wa_ref) | copy-start | bytes 3244036
  86.4 45.5 %collective-permute-start.12 = (bf16[192,1536]{1,0:T(8,128)(2,1)}, bf16[192,1536]{1,0:T(8,128)(2,1)}, u32[]{:S(2)}, u32[]{:S(2)}) collective-permute-start(bf16[192,1536]{1,0:T(8,128)(2,1)} %broadcast_select_fusion), channel_id=1, source_target_pairs={{0,2},{2,4},{4,6},{6,8},{8,10},{10,12},{12,14},{14,0},{16,30},{18,... | collective-permute-start | bytes 1769480 | tf_op jit(solution)/shard_map/ppermute | solution.py:222
  118.7 1.1 copy-start.4
  119.8 1.1 copy-start.6
  127.2 6.5 %copy-start.1 = (bf16[1344,384]{1,0:T(8,128)(2,1)}, bf16[1344,384]{1,0:T(8,128)(2,1)S(1)}, u32[]{:S(2)}) copy-start(bf16[1344,384]{1,0:T(8,128)(2,1)S(1)} %get-tuple-element.12.kva) | copy-start | bytes 3096580
  127.2 6.5 %copy-start.7 = (bf16[1344,256]{1,0:T(8,128)(2,1)}, bf16[1344,256]{1,0:T(8,128)(2,1)S(1)}, u32[]{:S(2)}) copy-start(bf16[1344,256]{1,0:T(8,128)(2,1)S(1)} %get-tuple-element.14.qa) | copy-start | bytes 2064388
  127.3 6.5 %copy-start.9 = (bf16[576,384]{1,0:T(8,128)(2,1)}, bf16[576,384]{1,0:T(8,128)(2,1)S(1)}, u32[]{:S(2)}) copy-start(bf16[576,384]{1,0:T(8,128)(2,1)S(1)} %get-tuple-element.16.part) | copy-start | bytes 1327108
  127.3 4.4 %copy-start.17 = (s32[8]{0:T(128)S(1)}, s32[8]{0:T(128)}, u32[]{:S(2)}) copy-start(s32[8]{0:T(128)} %get-tuple-element.17) | copy-start | bytes 100
  127.3 4.4 %copy-start.18 = (s32[8]{0:T(128)S(1)}, s32[8]{0:T(128)}, u32[]{:S(2)}) copy-start(s32[8]{0:T(128)} %get-tuple-element.18) | copy-start | bytes 100
  128.3 21.7 %collective-permute-start.13 = (bf16[768,384]{1,0:T(8,128)(2,1)}, bf16[768,384]{1,0:T(8,128)(2,1)S(1)}, u32[]{:S(2)}, u32[]{:S(2)}) collective-permute-start(bf16[768,384]{1,0:T(8,128)(2,1)} %slice.60), channel_id=1, source_target_pairs={{0,1},{1,0},{2,3},{3,2},{4,5},{5,4},{6,7},{7,6},{8,9},{9,8},{10,11... | collective-permute-start | bytes 1769480 | tf_op jit(solution)/shard_map/ppermute | solution.py:30
  131.9 6.1 %copy-start.13 = (s32[8,192]{1,0:T(8,128)S(1)}, s32[8,192]{1,0:T(8,128)}, u32[]{:S(2)}) copy-start(s32[8,192]{1,0:T(8,128)} %copy-done.12) | copy-start | bytes 18436
  131.9 6.8 %copy-start.14 = (s32[8]{0:T(128)S(1)}, s32[8]{0:T(128)}, u32[]{:S(2)}) copy-start(s32[8]{0:T(128)} %get-tuple-element.22) | copy-start | bytes 100
  131.9 6.8 %copy-start.16 = (s32[8]{0:T(128)S(1)}, s32[8]{0:T(128)}, u32[]{:S(2)}) copy-start(s32[8]{0:T(128)} %copy-done.15) | copy-start | bytes 100
  133.8 16.2 %collective-permute-start.14 = (bf16[192,384]{1,0:T(8,128)(2,1)S(1)}, bf16[192,384]{1,0:T(8,128)(2,1)S(1)}, u32[]{:S(2)}, u32[]{:S(2)}) collective-permute-start(bf16[192,384]{1,0:T(8,128)(2,1)S(1)} %get-tuple-element.13.kvb), channel_id=1, source_target_pairs={{0,1},{1,0},{2,3},{3,2},{4,5},{5,4},{6,7},{7,6},{8,9},{9,8},{10,11... | collective-permute-start | bytes 442376 | tf_op jit(solution)/shard_map/ppermute | solution.py:30
  150.0 1.2 copy-start.2
  151.2 1.1 copy-start.8
  152.3 1.0 copy-start.10
Sparse Core Ops, SparseCore 0:
  23.3 44.7 all-gather.1

commit v3 on v0

v3 whole, which is shorter than its diff:
```python
import functools

import jax
import jax.numpy as jnp
from jax import lax
from jax.experimental import pallas as pl
from jax.experimental.pallas import tpu as pltpu
from jax.sharding import Mesh
from jax.sharding import PartitionSpec as P

HEAD = 96
FR = 192
D = 1536
NZ = 8
ROWS = NZ * FR
SEQ = 3072
TILE = 256
MAX_TILES = 8
PAD = SEQ + TILE
AXES = ("y", "xl", "core", "z", "xh")
SIZES = (8, 2, 2, 8, 2)
VMEM = pl.BlockSpec(memory_space=pltpu.VMEM)
SMEM = pl.BlockSpec(memory_space=pltpu.SMEM)


def swap(x, axis):
    return lax.ppermute(x, axis, [(0, 1), (1, 0)])


def both(own, other, index, axis):
    first = jnp.where(index == 0, own, other)
    second = jnp.where(index == 0, other, own)
    return jnp.stack([first, second], axis=axis)


def gather_weights(w):
    flat = jnp.transpose(w, (1, 0, 2)).reshape(w.shape[1], 3 * HEAD)
    heads = both(flat, swap(flat, "xh"), lax.axis_index("xh"), 0)
    q, k, v = (heads[:, :, t * HEAD : (t + 1) * HEAD] for t in range(3))
    shard = jnp.concatenate([k[0], v[0], v[1], k[1], q[0], jnp.zeros_like(q[0, :, :64]), q[1]], axis=1)
    rows = lax.all_to_all(jnp.broadcast_to(shard[None], (8,) + shard.shape), "y", 0, 0, tiled=True)
    rows = both(rows, swap(rows, "xl"), lax.axis_index("xl"), 1)
    rows = both(rows, swap(rows, "core"), lax.axis_index("core"), 2)
    return rows.reshape(D, shard.shape[1])


def low_lanes(rows, lanes, below):
    return lax.broadcasted_iota(jnp.int32, (rows, lanes), 1) < below


def project_first(x_ref, w_ref, kv_ref, wire_ref):
    kv = jnp.dot(x_ref[...], w_ref[...], preferred_element_type=jnp.float32)
    kv_ref[...] = kv.astype(jnp.bfloat16)
    half = low_lanes(FR // 2, 128, 64)
    for b in range(kv.shape[0] // FR):
        rest = kv[b * FR : (b + 1) * FR, 128:]
        wire_ref[b, :FR, :] = kv[b * FR : (b + 1) * FR, :128].astype(jnp.bfloat16)
        packed = jnp.where(half, rest[: FR // 2], pltpu.roll(rest[FR // 2 :], 64, 1))
        wire_ref[b, FR:, :] = packed.astype(jnp.bfloat16)


def project_second(x_ref, w_ref, kv_ref, last_ref, q_ref, wire_ref):
    x = x_ref[...]
    last = jnp.dot(x, w_ref[:, 256:384], preferred_element_type=jnp.float32).astype(jnp.bfloat16)
    last_ref[...] = last
    q_ref[...] = jnp.dot(x, w_ref[:, 384:], preferred_element_type=jnp.float32).astype(jnp.bfloat16)
    half = low_lanes(FR // 2, 128, 64)
    for b in range(x.shape[0] // FR):
        rest = kv_ref[b * FR : (b + 1) * FR, 128:].astype(jnp.float32)
        wire_ref[b, :FR, :] = last[b * FR : (b + 1) * FR]
        packed = jnp.where(half, pltpu.roll(rest[FR // 2 :], 64, 1), rest[: FR // 2])
        wire_ref[b, FR:, :] = packed.astype(jnp.bfloat16)


def project_call(kernel, widths, ins, specs):
    step = 2 * FR
    row = lambda width: pl.BlockSpec((step, width), lambda i: (i, 0))
    wire = pl.BlockSpec((step // FR, FR * 3 // 2, 128), lambda i: (i, 0, 0))
    return pl.pallas_call(
        kernel,
        grid=(ROWS // step,),
        in_specs=[row(D), pl.BlockSpec((D, specs[0]), lambda i: (0, 0))] + [row(s) for s in specs[1:]],
        out_specs=[row(s) for s in widths] + [wire],
        out_shape=[jax.ShapeDtypeStruct((ROWS, s), jnp.bfloat16) for s in widths]
        + [jax.ShapeDtypeStruct((NZ, FR * 3 // 2, 128), jnp.bfloat16)],
        compiler_params=pltpu.CompilerParams(vmem_limit_bytes=56 << 20),
        cost_estimate=pl.CostEstimate(flops=2 * ROWS * D * 384, bytes_accessed=8 << 20, transcendentals=0),
    )(*ins)


def attend_jobs(jobs, n, kid_ref, kv_ref, key_lane):
    scale = HEAD**-0.5 * 1.4426950408889634
    scores, tops, outs = [], [], []
    for q, qid, first in jobs:
        tiles, top = [], None
        for t in range(n):
            at = pl.multiple_of(first + t * TILE, 128)
            keys = kv_ref[pl.ds(at, TILE), key_lane : key_lane + 128]
            s = lax.dot_general(q, keys, (((1,), (1,)), ((), ())), preferred_element_type=jnp.float32)
            s = jnp.where(qid == kid_ref[:, pl.ds(at, TILE)], s, -1e30)
            tiles.append(s)
            most = jnp.maximum(s[:, :128], s[:, 128:])
            top = most if top is None else jnp.maximum(top, most)
        scores.append(tiles)
        tops.append(jnp.max(top, axis=1, keepdims=True))
    for (q, qid, first), tiles, top in zip(jobs, scores, tops):
        total = acc = None
        for t in range(n):
            at = pl.multiple_of(first + t * TILE, 128)
            p = jnp.exp2((tiles[t] - top) * scale)
            part_sum = p[:, :128] + p[:, 128:]
            out = jnp.dot(p.astype(jnp.bfloat16), kv_ref[pl.ds(at, TILE), :], preferred_element_type=jnp.float32)
            total = part_sum if total is None else total + part_sum
            acc = out if acc is None else acc + out
        outs.append(acc * (1.0 / jnp.sum(total, axis=1, keepdims=True)))
    return outs


def attend_kernel(head, info_ref, qid_ref, kid_ref, q_ref, *refs):
    own_refs, (other_ref, out_ref, kv_ref) = refs[:-3], refs[-3:]
    kv_ref[SEQ:, :] = jnp.zeros((TILE, 256), jnp.bfloat16)
    whole, shared = (slice(0, 128), slice(128, 256)) if head == 0 else (slice(128, 256), slice(0, 128))
    for z in range(NZ):
        at = pl.ds(pl.multiple_of(info_ref[z] * FR, FR), FR)
        if head == 0:
            kv_ref[at, :] = own_refs[0][z * FR : (z + 1) * FR, :]
        else:
            kv_ref[at, :128] = own_refs[0][z * FR : (z + 1) * FR, 128:]
            kv_ref[at, 128:] = own_refs[1][z * FR : (z + 1) * FR, :]
        place = info_ref[8 + z] * FR
        kv_ref[pl.ds(pl.multiple_of(place, FR), FR), whole] = other_ref[z, :FR, :]
        packed = other_ref[z, FR:, :]
        kv_ref[pl.ds(pl.multiple_of(place, 96), 96), shared] = packed
        turned = pltpu.roll(packed.astype(jnp.float32), 64, 1).astype(jnp.bfloat16)
        kv_ref[pl.ds(pl.multiple_of(place + 96, 96), 96), shared] = turned

    def pair(g, _):
        slots = [info_ref[32 + 2 * g + i] for i in range(2)]
        count = info_ref[24 + slots[1]]
        jobs = []
        for s in slots:
            rows = pl.ds(pl.multiple_of(s * FR, FR), FR)
            first = jnp.minimum(info_ref[16 + s], PAD - count * TILE)
            jobs.append((q_ref[rows, head * 128 : head * 128 + 128], qid_ref[rows, :], first))

        def attend_pair(n):
            outs = attend_jobs(jobs, n, kid_ref, kv_ref, head * 128)
            lane = lax.broadcasted_iota(jnp.int32, (FR, 128), 1)
            spare = (lane[:48] >= 64) & (lane[:48] < 96) if head == 0 else (lane[:48] >= 32) & (lane[:48] < 64)
            for s, acc in zip(slots, outs):
                m = jnp.where(lane < (64 if head == 0 else 32), acc[:, 128:], acc[:, :128])
                for i, by in enumerate((96, 64, 32)):
                    moved = jnp.where(spare, pltpu.roll(m[144:], by, 1), m[i * 48 : (i + 1) * 48])
                    out_ref[s, i * 48 : (i + 1) * 48, :] = moved.astype(jnp.bfloat16)

        for n in range(1, MAX_TILES + 1):
            pl.when(count == n)(functools.partial(attend_pair, n))
        return 0

    lax.fori_loop(0, NZ // 2, pair, 0)


def attend(head, *args):
    return pl.pallas_call(
        functools.partial(attend_kernel, head),
        in_specs=[SMEM] + [VMEM] * (len(args) - 1),
        out_specs=VMEM,
        out_shape=jax.ShapeDtypeStruct((NZ, 144, 128), jnp.bfloat16),
        scratch_shapes=[pltpu.VMEM((PAD, 256), jnp.bfloat16)],
        compiler_params=pltpu.CompilerParams(vmem_limit_bytes=36 << 20),
        cost_estimate=pl.CostEstimate(flops=4 << 30, bytes_accessed=4 << 20, transcendentals=2 << 20),
    )(*args)


def unpack_kernel(first_ref, second_ref, out_ref):
    lane = lax.broadcasted_iota(jnp.int32, (FR, 128), 1)
    for z in range(0, NZ, 2):
        heads = []
        for i in (z, z + 1):
            for head, ref in enumerate((first_ref, second_ref)):
                m = ref[i].astype(jnp.float32)
                tail = [pltpu.roll(m[j * 48 : (j + 1) * 48], by, 1) for j, by in enumerate((32, 64, 96))]
                if head == 0:
                    parts = jnp.where(lane[:48] >= 96, tail[0], jnp.where(lane[:48] < 32, tail[1], tail[2]))
                else:
                    parts = jnp.where(lane[:48] < 32, tail[2], jnp.where(lane[:48] < 96, tail[0], tail[1]))
                m = jnp.concatenate([m, parts], axis=0)
                heads.append(pltpu.roll(m, 32 if head == 0 else 64, 1))
        a, b, c, d = heads
        tiles = (
            jnp.where(lane < 96, a, pltpu.roll(b, 96, 1)),
            jnp.where(lane < 64, pltpu.roll(b, 96, 1), pltpu.roll(c, 64, 1)),
            jnp.where(lane < 32, pltpu.roll(c, 64, 1), pltpu.roll(d, 32, 1)),
        )
        for i, tile in enumerate(tiles):
            out_ref[:, z * 192 + i * 128 : z * 192 + (i + 1) * 128] = tile.astype(jnp.bfloat16)


def unpack(first, second):
    return pl.pallas_call(
        unpack_kernel,
        in_specs=[VMEM] * 2,
        out_specs=VMEM,
        out_shape=jax.ShapeDtypeStruct((FR, D), jnp.bfloat16),
        compiler_params=pltpu.CompilerParams(vmem_limit_bytes=8 << 20),
    )(first, second)


def plan(ids, order, xh):
    blocks = ids.reshape(16, FR)
    places = order.reshape(NZ, 2)
    own = jnp.where(xh == 0, places[:, 0], places[:, 1])
    other = jnp.where(xh == 0, places[:, 1], places[:, 0])
    qid = jnp.take(blocks, own, axis=0)
    first = jnp.sum(ids[None, :] < qid[:, :1], axis=1, dtype=jnp.int32)
    last = jnp.sum(ids[None, :] <= qid[:, FR - 1 :], axis=1, dtype=jnp.int32)
    first = first // 128 * 128
    count = (last - first + TILE - 1) // TILE
    i = jnp.arange(NZ, dtype=jnp.int32)
    ahead = (count[None, :] < count[:, None]) | ((count[None, :] == count[:, None]) & (i[None, :] < i[:, None]))
    rank = jnp.sum(ahead, axis=1, dtype=jnp.int32)
    ranked = jnp.sum(jnp.where(rank[:, None] == i[None, :], i[:, None], 0), axis=0, dtype=jnp.int32)
    info = jnp.concatenate([own, other, first, count, ranked])
    kid = jnp.concatenate([ids, jnp.full((TILE,), -1, jnp.int32)])[None]
    return info, qid.reshape(ROWS, 1), kid


def body(frames, seg_ids, assign, w_qkv):
    x = lax.all_gather(frames, "z", axis=0, tiled=True)
    w = gather_weights(w_qkv)
    info, qid, kid = plan(seg_ids[0], assign[0], lax.axis_index("xh"))
    x, w, info, qid, kid = lax.optimization_barrier((x, w, info, qid, kid))
    kv, wire0 = project_call(project_first, [256], (x, w), [256])
    other0 = swap(wire0, "xh")
    last, q, wire1 = project_call(project_second, [128, 256], (x, w, kv), [640, 256])
    other1 = swap(wire1, "xh")
    packed0 = attend(0, info, qid, kid, q, kv, other0)
    home0 = lax.all_to_all(packed0, "z", 0, 0, tiled=True)
    packed1 = attend(1, info, qid, kid, q, kv, last, other1)
    home1 = lax.all_to_all(packed1, "z", 0, 0, tiled=True)
    return unpack(home0, home1)


def solution(mesh):
    fine = Mesh(mesh.devices.reshape(SIZES), AXES)
    dp, ctx = AXES[:3], AXES[3:]
    return jax.shard_map(
        body,
        mesh=fine,
        in_specs=(P(AXES, None), P(dp, None), P(dp, None), P(None, dp, ctx)),
        out_specs=P(AXES, None),
        check_vma=False,
    )
```

time: 335 us -> 157 us (0.47); the launches traced: 330 us -> 156 us
  waiting for transfers between devices: 147 us -> 50.6 us
  blocking collectives: 87.8 us -> 35.7 us
  matrix products: 31.5 us -> 0 us
  Pallas kernels: 0 us -> 25.5 us
  local copies, waits for them, and re-layouts: 16.2 us -> 7.03 us
  starting transfers between devices: 24.1 us -> 19.4 us
  loops' own time: 3.78 us -> 0 us
    all_gather x1, waiting for transfers between devices: 90.7 us -> 20.8 us  [body(): x = lax.all_gather(frames, 'z', axis=0, tiled=True)]
    all_gather x1 -> x0, blocking collectives: 59.7 us -> none  [body(): columns = lax.all_gather(w_qkv, 'ctx', axis=2, tiled=True)]
    all_to_all x3 -> x1, waiting for transfers between devices: 56 us -> 5.53 us  [body(): home1 = lax.all_to_all(packed1, 'z', 0, 0, tiled=True)]
    dot_general x13 -> x0, matrix products: 31.5 us -> none  [the longest x6 16.1 us: one(): jnp.dot(weights, values, preferred_element_type=jnp.float32)]
    pallas_call x0 -> x5, Pallas kernels: none -> 25.5 us  [the longest x2 12.4 us: project_call(): pl.pallas_call(kernel, grid=(ROWS // step,), in_specs=[row(D), pl.BlockSp...]
    ppermute x0 -> x5, waiting for transfers between devices: none -> 23.5 us  [swap(): return lax.ppermute(x, axis, [(0, 1), (1, 0)])]
    all_to_all x3 -> x1, starting transfers between devices: 24.1 us -> 4.13 us  [body(): home1 = lax.all_to_all(packed1, 'z', 0, 0, tiled=True)]
    ppermute x0 -> x5, starting transfers between devices: none -> 15.3 us  [swap(): return lax.ppermute(x, axis, [(0, 1), (1, 0)])]
  transfers between devices with their start and end apart: 4 -> 7, of which waited for: 4 -> 6; matrix products, arithmetic and copies ran while one was open for 1% -> 5% of each run, Pallas kernels for 0% -> 7%
where the time goes in v3:
time: 157 us; the launch traced here: 156 us
  waiting for transfers between devices  50.6 us (32%)
  blocking collectives  35.7 us (23%)
  Pallas kernels  25.5 us (16%)
  starting transfers between devices  19.4 us (12%)
  between operations  13.6 us (9%)
  local copies, waits for them, and re-layouts  7.03 us (4%)
  other arithmetic  4.42 us (3%)
    ppermute x5, waiting for transfers between devices, swap(): return lax.ppermute(x, axis, [(0, 1), (1, 0)])  23.5 us
    all_to_all x1, blocking collectives, gather_weights(): lax.all_to_all(jnp.broadcast_to(shard[None], (8,) + shard.shape), 'y', 0,...  22.5 us
    all_gather x1, waiting for transfers between devices, body(): x = lax.all_gather(frames, 'z', axis=0, tiled=True)  20.8 us
    ppermute x5, starting transfers between devices, swap(): return lax.ppermute(x, axis, [(0, 1), (1, 0)])  15.3 us
    all_to_all x1, blocking collectives, body(): home0 = lax.all_to_all(packed0, 'z', 0, 0, tiled=True)  13.2 us
    pallas_call x2, Pallas kernels, project_call(): pl.pallas_call(kernel, grid=(ROWS // step,), in_specs=[row(D), pl.BlockSp...  12.4 us
    pallas_call x2, Pallas kernels, attend(): pl.pallas_call(functools.partial(attend_kernel, head), in_specs=[SMEM] +...  10.8 us
    all_to_all x1, waiting for transfers between devices, body(): home1 = lax.all_to_all(packed1, 'z', 0, 0, tiled=True)  5.53 us
  transfers between devices with their start and end apart: 7, of which 6 were waited for; matrix products, arithmetic and copies ran while one was open for 5% of the time, Pallas kernels for 7%

profile of v3, /device:TPU:6, one launch (start us, length us, event | category | flops | bytes accessed | tf_op | source)
XLA Modules:
  0.0 156.2 jit_solution(12994517599004648261)
XLA Ops:
  6.5 0.7 all-gather.2.cloned.1.call-update
  7.3 0.8 copy.12
  8.1 0.1 reshape.112
  8.2 3.3 %collective-permute-start = (bf16[48,288]{1,0:T(8,128)(2,1)S(1)}, bf16[48,288]{1,0:T(8,128)(2,1)S(1)}, u32[]{:S(2)}, u32[]{:S(2)}) collective-permute-start(bf16[48,288]{1,0:T(8,128)(2,1)S(1)} %reshape.112), channel_id=1, source_target_pairs={{0,1},{1,0},{2,3},{3,2},{4,5},{5,4},{6,7},{7,6},{8,9},{9,8},{10,11... | collective-permute-start | bytes 82952 | tf_op jit(solution)/shard_map/ppermute | solution.py:27
  11.5 4.0 %collective-permute-done = bf16[48,288]{1,0:T(8,128)(2,1)S(1)} collective-permute-done((bf16[48,288]{1,0:T(8,128)(2,1)S(1)}, bf16[48,288]{1,0:T(8,128)(2,1)S(1)}, u32[]{:S(2)}, u32[]{:S(2)}) %collective-permute-start) | collective-permute-done | bytes 27680 | tf_op jit(solution)/shard_map/ppermute | solution.py:27
  15.5 0.1 slice_bitcast_fusion
  15.6 0.1 concatenate.9
  15.8 22.5 %all_to_all.15 = bf16[8,48,640]{2,1,0:T(8,128)(2,1)S(1)} all-to-all(bf16[8,48,640]{2,1,0:T(8,128)(2,1)S(1)} %broadcast_in_dim.23), channel_id=1, replica_groups=mesh['y'=8,'xl'=2,'core'=2,'z'=8,'xh'=2] {'y'}, dimensions={0} | all-to-all | bytes 983040 | tf_op jit(solution)/shard_map/all_to_all | solution.py:41
  38.3 2.7 %collective-permute-start.1 = (bf16[8,48,640]{2,1,0:T(8,128)(2,1)S(1)}, bf16[8,48,640]{2,1,0:T(8,128)(2,1)S(1)}, u32[]{:S(2)}, u32[]{:S(2)}) collective-permute-start(bf16[8,48,640]{2,1,0:T(8,128)(2,1)S(1)} %all_to_all.15), channel_id=1, source_target_pairs={{0,32},{32,0},{1,33},{33,1},{2,34},{34,2},{3,35},{35,3},{4,36},{36... | collective-permute-start | bytes 1474568 | tf_op jit(solution)/shard_map/ppermute | solution.py:27
  41.1 0.5 broadcast.203
  41.6 0.7 reduce.17
  42.3 0.1 reshape_squeeze.6
  42.3 0.7 reduce.18
  43.1 0.2 and_reduce_fusion
  43.3 0.1 fusion.2
  43.5 0.6 gather_fusion
  44.0 6.0 %collective-permute-done.1 = bf16[8,48,640]{2,1,0:T(8,128)(2,1)S(1)} collective-permute-done((bf16[8,48,640]{2,1,0:T(8,128)(2,1)S(1)}, bf16[8,48,640]{2,1,0:T(8,128)(2,1)S(1)}, u32[]{:S(2)}, u32[]{:S(2)}) %collective-permute-start.1) | collective-permute-done | bytes 491552 | tf_op jit(solution)/shard_map/ppermute | solution.py:27
  50.0 0.1 select_bitcast_fusion.3
  50.1 0.1 pad_maximum_fusion.1
  50.2 1.9 %collective-permute-start.2 = (bf16[8,2,48,640]{3,2,1,0:T(8,128)(2,1)S(1)}, bf16[8,2,48,640]{3,2,1,0:T(8,128)(2,1)S(1)}, u32[]{:S(2)}, u32[]{:S(2)}) collective-permute-start(bf16[8,2,48,640]{3,2,1,0:T(8,128)(2,1)S(1)} %pad_maximum_fusion.1), channel_id=1, source_target_pairs={{0,16},{16,0},{1,17},{17,1},{2,18},{18,2},{3,19},{19,3},{4,20},{20... | collective-permute-start | bytes 2949128 | tf_op jit(solution)/shard_map/ppermute | solution.py:27
  52.1 0.1 broadcast_select_fusion
  52.2 0.1 select_n.123
  52.3 0.2 slice_reduce_fusion
  52.5 0.2 select_reduce_fusion.1
  52.7 0.2 convert_reduce_fusion
  53.0 0.2 convert_reduce_fusion.2
  53.1 0.1 select_reduce_fusion
  53.2 0.1 concatenate.10.info_ref
  53.3 1.4 collective-permute-done.2
  54.7 0.2 select_bitcast_fusion.1
  54.9 1.5 pad_maximum_fusion
  56.4 20.8 %all-gather.2.cloned.1.call-done.x_ref = bf16[1536,1536]{1,0:T(8,128)(2,1)} async-done(((bf16[192,1536]{1,0:T(8,128)(2,1)}), bf16[1536,1536]{1,0:T(8,128)(2,1)}) %all-gather.2.cloned.1.call-update) | async-done | bytes 4718608 | tf_op jit(solution)/shard_map/all_gather | solution.py:229
  77.2 5.3 %shard_map.46 = (bf16[1536,256]{1,0:T(8,128)(2,1)}, bf16[8,288,128]{2,1,0:T(8,128)(2,1)}) custom-call(bf16[1536,1536]{1,0:T(8,128)(2,1)} %all-gather.2.cloned.1.call-done.x_ref, bf16[1536,640]{1,0:T(8,128)(2,1)} %bitcast.31), custom_call_target="tpu_custom_call" | custom-call | flops 1811939328 | bytes 8388608 | tf_op jit(solution)/shard_map/pallas_call | solution.py:79
  82.5 7.1 %shard_map.47 = (bf16[1536,128]{1,0:T(8,128)(2,1)}, bf16[1536,256]{1,0:T(8,128)(2,1)}, bf16[8,288,128]{2,1,0:T(8,128)(2,1)}) custom-call(bf16[1536,1536]{1,0:T(8,128)(2,1)} %all-gather.2.cloned.1.call-done.x_ref, bf16[1536,640]{1,0:T(8,128)(2,1)} %bitcast.32, bf16[1536,256]{1,0:T(8,128)(2,1)} %get-tuple-element.20.kv_ref.refs_0_), custom_call_target="tpu_custom_call" | custom-call | flops 1811939328 | bytes 8388608 | tf_op jit(solution)/shard_map/pallas_call | solution.py:79
  89.6 3.3 %collective-permute-start.4 = (bf16[8,288,128]{2,1,0:T(8,128)(2,1)}, bf16[8,288,128]{2,1,0:T(8,128)(2,1)S(1)}, u32[]{:S(2)}, u32[]{:S(2)}) collective-permute-start(bf16[8,288,128]{2,1,0:T(8,128)(2,1)} %get-tuple-element.24), channel_id=1, source_target_pairs={{0,1},{1,0},{2,3},{3,2},{4,5},{5,4},{6,7},{7,6},{8,9},{9,8},{10,11... | collective-permute-start | bytes 1769480 | tf_op jit(solution)/shard_map/ppermute | solution.py:27
  93.0 4.0 %collective-permute-start.3 = (bf16[8,288,128]{2,1,0:T(8,128)(2,1)}, bf16[8,288,128]{2,1,0:T(8,128)(2,1)}, u32[]{:S(2)}, u32[]{:S(2)}) collective-permute-start(bf16[8,288,128]{2,1,0:T(8,128)(2,1)} %get-tuple-element.22), channel_id=1, source_target_pairs={{0,1},{1,0},{2,3},{3,2},{4,5},{5,4},{6,7},{7,6},{8,9},{9,8},{10,11... | collective-permute-start | bytes 1769480 | tf_op jit(solution)/shard_map/ppermute | solution.py:27
  97.0 0.3 copy.15.qid_ref
  97.3 12.2 %collective-permute-done.4.refs_2_ = bf16[8,288,128]{2,1,0:T(8,128)(2,1)S(1)} collective-permute-done((bf16[8,288,128]{2,1,0:T(8,128)(2,1)}, bf16[8,288,128]{2,1,0:T(8,128)(2,1)S(1)}, u32[]{:S(2)}, u32[]{:S(2)}) %collective-permute-start.4) | collective-permute-done | bytes 589856 | tf_op jit(solution)/shard_map/ppermute | solution.py:27
  109.4 0.8 copy-done.3
  110.2 1.1 copy-done.1
  111.4 1.1 copy-done.4
  112.4 1.0 copy-done.5
  113.4 5.6 %shard_map.49 = bf16[8,144,128]{2,1,0:T(8,128)(2,1)} custom-call(s32[40]{0:T(128)S(1)} %concatenate.10.info_ref, s32[1536,1]{1,0:T(8,128)S(1)} %copy.15.qid_ref, s32[1,3328]{1,0:T(1,128)S(1)} %broadcast_in_dim.47.kid_ref, bf16[1536,256]{1,0:T(8,128)(2,1)S(1)} %copy-done.1, bf16[1536,256]{1,0:T(8,128)(2,1)S(1)} %copy-done, bf16[1536,128]{1,0:T(8,128)(2,1)S(1)} %copy-done.5, ...), custom_call_target="tpu_custom_call" | custom-call | flops 4294967296 | bytes 4194304 | tf_op jit(solution)/shard_map/pallas_call | solution.py:164
  119.0 4.1 %all-to-all-start.2 = ((bf16[8,144,128]{2,1,0:T(8,128)(2,1)}), bf16[8,144,128]{2,1,0:T(8,128)(2,1)S(1)}, u32[]{:S(2)}, u32[]{:S(2)}) async-start(bf16[8,144,128]{2,1,0:T(8,128)(2,1)} %shard_map.49), calls=%async_computation.2 | async-start | bytes 589824 | tf_op jit(solution)/shard_map/all_to_all | solution.py:240
  123.1 5.3 %shard_map.48 = bf16[8,144,128]{2,1,0:T(8,128)(2,1)S(1)} custom-call(s32[40]{0:T(128)S(1)} %concatenate.10.info_ref, s32[1536,1]{1,0:T(8,128)S(1)} %copy.15.qid_ref, s32[1,3328]{1,0:T(1,128)S(1)} %broadcast_in_dim.47.kid_ref, bf16[1536,256]{1,0:T(8,128)(2,1)S(1)} %copy-done.2, bf16[1536,256]{1,0:T(8,128)(2,1)S(1)} %copy-done, ...), custom_call_target="tpu_custom_call" | custom-call | flops 4294967296 | bytes 4194304 | tf_op jit(solution)/shard_map/pallas_call | solution.py:164
  128.4 5.5 %all-to-all-done.2.second_ref = bf16[8,144,128]{2,1,0:T(8,128)(2,1)S(1)} async-done(((bf16[8,144,128]{2,1,0:T(8,128)(2,1)}), bf16[8,144,128]{2,1,0:T(8,128)(2,1)S(1)}, u32[]{:S(2)}, u32[]{:S(2)}) %all-to-all-start.2) | async-done | bytes 294944 | tf_op jit(solution)/shard_map/all_to_all | solution.py:240
  134.0 13.2 %all_to_all.16.first_ref = bf16[8,144,128]{2,1,0:T(8,128)(2,1)S(1)} all-to-all(bf16[8,144,128]{2,1,0:T(8,128)(2,1)S(1)} %shard_map.48), channel_id=1, replica_groups=mesh['y'=8,'xl'=2,'core'=2,'z'=8,'xh'=2] {'z'}, dimensions={0} | all-to-all | bytes 589824 | tf_op jit(solution)/shard_map/all_to_all | solution.py:238
  147.2 2.2 %shard_map.50 = bf16[192,1536]{1,0:T(8,128)(2,1)} custom-call(bf16[8,144,128]{2,1,0:T(8,128)(2,1)S(1)} %all_to_all.16.first_ref, bf16[8,144,128]{2,1,0:T(8,128)(2,1)S(1)} %all-to-all-done.2.second_ref), custom_call_target="tpu_custom_call" | custom-call | tf_op jit(solution)/shard_map/pallas_call | solution.py:200
  (22 shorter events, 0.2 us)
Async XLA Ops:
  6.5 35.1 %copy-start.7 = (s32[1,16]{1,0:T(1,128)S(1)}, s32[1,16]{1,0:T(1,128)}, u32[]{:S(2)}) copy-start(s32[1,16]{1,0:T(1,128)} %param.6) | copy-start | bytes 196
  6.5 35.8 %copy-start.6 = (s32[1,3072]{1,0:T(1,128)S(1)}, s32[1,3072]{1,0:T(1,128)}, u32[]{:S(2)}) copy-start(s32[1,3072]{1,0:T(1,128)} %param.5) | copy-start | bytes 36868
  6.5 70.7 %all-gather.2.cloned.1.call-start = ((), (), s32[]{:S(2)}) async-start(), calls=%async_computation.3 | async-start | bytes 5308416 | tf_op jit(solution)/shard_map/all_gather | solution.py:229
  8.2 7.4 %collective-permute-start = (bf16[48,288]{1,0:T(8,128)(2,1)S(1)}, bf16[48,288]{1,0:T(8,128)(2,1)S(1)}, u32[]{:S(2)}, u32[]{:S(2)}) collective-permute-start(bf16[48,288]{1,0:T(8,128)(2,1)S(1)} %reshape.112), channel_id=1, source_target_pairs={{0,1},{1,0},{2,3},{3,2},{4,5},{5,4},{6,7},{7,6},{8,9},{9,8},{10,11... | collective-permute-start | bytes 82952 | tf_op jit(solution)/shard_map/ppermute | solution.py:27
  38.3 11.7 %collective-permute-start.1 = (bf16[8,48,640]{2,1,0:T(8,128)(2,1)S(1)}, bf16[8,48,640]{2,1,0:T(8,128)(2,1)S(1)}, u32[]{:S(2)}, u32[]{:S(2)}) collective-permute-start(bf16[8,48,640]{2,1,0:T(8,128)(2,1)S(1)} %all_to_all.15), channel_id=1, source_target_pairs={{0,32},{32,0},{1,33},{33,1},{2,34},{34,2},{3,35},{35,3},{4,36},{36... | collective-permute-start | bytes 1474568 | tf_op jit(solution)/shard_map/ppermute | solution.py:27
  50.2 4.5 %collective-permute-start.2 = (bf16[8,2,48,640]{3,2,1,0:T(8,128)(2,1)S(1)}, bf16[8,2,48,640]{3,2,1,0:T(8,128)(2,1)S(1)}, u32[]{:S(2)}, u32[]{:S(2)}) collective-permute-start(bf16[8,2,48,640]{3,2,1,0:T(8,128)(2,1)S(1)} %pad_maximum_fusion.1), channel_id=1, source_target_pairs={{0,16},{16,0},{1,17},{17,1},{2,18},{18,2},{3,19},{19,3},{4,20},{20... | collective-permute-start | bytes 2949128 | tf_op jit(solution)/shard_map/ppermute | solution.py:27
  82.5 27.8 %copy-start = (bf16[1536,256]{1,0:T(8,128)(2,1)S(1)}, bf16[1536,256]{1,0:T(8,128)(2,1)}, u32[]{:S(2)}) copy-start(bf16[1536,256]{1,0:T(8,128)(2,1)} %get-tuple-element.20.kv_ref.refs_0_) | copy-start | bytes 2359300
  89.6 19.8 %collective-permute-start.4 = (bf16[8,288,128]{2,1,0:T(8,128)(2,1)}, bf16[8,288,128]{2,1,0:T(8,128)(2,1)S(1)}, u32[]{:S(2)}, u32[]{:S(2)}) collective-permute-start(bf16[8,288,128]{2,1,0:T(8,128)(2,1)} %get-tuple-element.24), channel_id=1, source_target_pairs={{0,1},{1,0},{2,3},{3,2},{4,5},{5,4},{6,7},{7,6},{8,9},{9,8},{10,11... | collective-permute-start | bytes 1769480 | tf_op jit(solution)/shard_map/ppermute | solution.py:27
  93.0 30.2 %collective-permute-start.3 = (bf16[8,288,128]{2,1,0:T(8,128)(2,1)}, bf16[8,288,128]{2,1,0:T(8,128)(2,1)}, u32[]{:S(2)}, u32[]{:S(2)}) collective-permute-start(bf16[8,288,128]{2,1,0:T(8,128)(2,1)} %get-tuple-element.22), channel_id=1, source_target_pairs={{0,1},{1,0},{2,3},{3,2},{4,5},{5,4},{6,7},{7,6},{8,9},{9,8},{10,11... | collective-permute-start | bytes 1769480 | tf_op jit(solution)/shard_map/ppermute | solution.py:27
  109.4 0.8 copy-start.3
  110.2 1.1 copy-start.1
  111.4 1.1 copy-start.4
  112.4 1.0 copy-start.5
  113.4 9.7 %copy-start.2 = (bf16[1536,256]{1,0:T(8,128)(2,1)S(1)}, bf16[1536,256]{1,0:T(8,128)(2,1)}, u32[]{:S(2)}) copy-start(bf16[1536,256]{1,0:T(8,128)(2,1)} %get-tuple-element.21.q_ref) | copy-start | bytes 2359300
  119.0 15.0 %all-to-all-start.2 = ((bf16[8,144,128]{2,1,0:T(8,128)(2,1)}), bf16[8,144,128]{2,1,0:T(8,128)(2,1)S(1)}, u32[]{:S(2)}, u32[]{:S(2)}) async-start(bf16[8,144,128]{2,1,0:T(8,128)(2,1)} %shard_map.49), calls=%async_computation.2 | async-start | bytes 589824 | tf_op jit(solution)/shard_map/all_to_all | solution.py:240
Sparse Core Ops, SparseCore 0:
  9.4 67.7 all-gather.1

commit v4 on v3

--- a/solution.py
+++ b/solution.py
@@ -21,6 +21,7 @@
 SIZES = (8, 2, 2, 8, 2)
 VMEM = pl.BlockSpec(memory_space=pltpu.VMEM)
 SMEM = pl.BlockSpec(memory_space=pltpu.SMEM)
+HBM = pl.BlockSpec(memory_space=pltpu.HBM)
 
 
 def swap(x, axis):
@@ -44,48 +45,25 @@
     return rows.reshape(D, shard.shape[1])
 
 
-def low_lanes(rows, lanes, below):
-    return lax.broadcasted_iota(jnp.int32, (rows, lanes), 1) < below
-
-
-def project_first(x_ref, w_ref, kv_ref, wire_ref):
-    kv = jnp.dot(x_ref[...], w_ref[...], preferred_element_type=jnp.float32)
-    kv_ref[...] = kv.astype(jnp.bfloat16)
-    half = low_lanes(FR // 2, 128, 64)
-    for b in range(kv.shape[0] // FR):
-        rest = kv[b * FR : (b + 1) * FR, 128:]
-        wire_ref[b, :FR, :] = kv[b * FR : (b + 1) * FR, :128].astype(jnp.bfloat16)
-        packed = jnp.where(half, rest[: FR // 2], pltpu.roll(rest[FR // 2 :], 64, 1))
-        wire_ref[b, FR:, :] = packed.astype(jnp.bfloat16)
-
-
-def project_second(x_ref, w_ref, kv_ref, last_ref, q_ref, wire_ref):
-    x = x_ref[...]
-    last = jnp.dot(x, w_ref[:, 256:384], preferred_element_type=jnp.float32).astype(jnp.bfloat16)
-    last_ref[...] = last
-    q_ref[...] = jnp.dot(x, w_ref[:, 384:], preferred_element_type=jnp.float32).astype(jnp.bfloat16)
-    half = low_lanes(FR // 2, 128, 64)
-    for b in range(x.shape[0] // FR):
-        rest = kv_ref[b * FR : (b + 1) * FR, 128:].astype(jnp.float32)
-        wire_ref[b, :FR, :] = last[b * FR : (b + 1) * FR]
-        packed = jnp.where(half, pltpu.roll(rest[FR // 2 :], 64, 1), rest[: FR // 2])
-        wire_ref[b, FR:, :] = packed.astype(jnp.bfloat16)
-
-
-def project_call(kernel, widths, ins, specs):
-    step = 2 * FR
+def project_kernel(x_ref, w_ref, most_ref, last_ref, q_ref):
+    y = jnp.dot(x_ref[...], w_ref[...], preferred_element_type=jnp.float32).astype(jnp.bfloat16)
+    most_ref[...] = y[:, :256]
+    last_ref[...] = y[:, 256:384]
+    q_ref[...] = y[:, 384:]
+
+
+def project(x, w, step=ROWS // 2):
     row = lambda width: pl.BlockSpec((step, width), lambda i: (i, 0))
-    wire = pl.BlockSpec((step // FR, FR * 3 // 2, 128), lambda i: (i, 0, 0))
+    widths = (256, 128, 256)
     return pl.pallas_call(
-        kernel,
+        project_kernel,
         grid=(ROWS // step,),
-        in_specs=[row(D), pl.BlockSpec((D, specs[0]), lambda i: (0, 0))] + [row(s) for s in specs[1:]],
-        out_specs=[row(s) for s in widths] + [wire],
-        out_shape=[jax.ShapeDtypeStruct((ROWS, s), jnp.bfloat16) for s in widths]
-        + [jax.ShapeDtypeStruct((NZ, FR * 3 // 2, 128), jnp.bfloat16)],
+        in_specs=[row(D), VMEM],
+        out_specs=[row(width) for width in widths],
+        out_shape=[jax.ShapeDtypeStruct((ROWS, width), jnp.bfloat16) for width in widths],
         compiler_params=pltpu.CompilerParams(vmem_limit_bytes=56 << 20),
-        cost_estimate=pl.CostEstimate(flops=2 * ROWS * D * 384, bytes_accessed=8 << 20, transcendentals=0),
-    )(*ins)
+        cost_estimate=pl.CostEstimate(flops=2 * ROWS * D * 640, bytes_accessed=10 << 20, transcendentals=0),
+    )(x, w)
 
 
 def attend_jobs(jobs, n, kid_ref, kv_ref, key_lane):
@@ -116,34 +94,36 @@
     return outs
 
 
-def attend_kernel(head, info_ref, qid_ref, kid_ref, q_ref, *refs):
-    own_refs, (other_ref, out_ref, kv_ref) = refs[:-3], refs[-3:]
+def attend_kernel(head, group, info_ref, qid_ref, kid_ref, q_hbm, *refs):
+    *parts, out_ref, kv_ref, q_ref, sems = refs
+    copies = [pltpu.make_async_copy(q_hbm.at[:, head * 128 : head * 128 + 128], q_ref, sems.at[0])]
+    for z in range(NZ):
+        rows = pl.ds(z * FR, FR)
+        for side in range(2):
+            at = pl.ds(pl.multiple_of(info_ref[side * NZ + z] * FR, FR), FR)
+            sem = 1 + 4 * z + 2 * side
+            if head == 0:
+                copies.append(pltpu.make_async_copy(parts[side].at[rows, :], kv_ref.at[at, :], sems.at[sem]))
+            else:
+                most, last = parts[side], parts[2 + side]
+                copies.append(pltpu.make_async_copy(most.at[rows, 128:], kv_ref.at[at, :128], sems.at[sem]))
+                copies.append(pltpu.make_async_copy(last.at[rows, :], kv_ref.at[at, 128:], sems.at[sem + 1]))
+    for copy in copies:
+        copy.start()
     kv_ref[SEQ:, :] = jnp.zeros((TILE, 256), jnp.bfloat16)
-    whole, shared = (slice(0, 128), slice(128, 256)) if head == 0 else (slice(128, 256), slice(0, 128))
-    for z in range(NZ):
-        at = pl.ds(pl.multiple_of(info_ref[z] * FR, FR), FR)
-        if head == 0:
-            kv_ref[at, :] = own_refs[0][z * FR : (z + 1) * FR, :]
-        else:
-            kv_ref[at, :128] = own_refs[0][z * FR : (z + 1) * FR, 128:]
-            kv_ref[at, 128:] = own_refs[1][z * FR : (z + 1) * FR, :]
-        place = info_ref[8 + z] * FR
-        kv_ref[pl.ds(pl.multiple_of(place, FR), FR), whole] = other_ref[z, :FR, :]
-        packed = other_ref[z, FR:, :]
-        kv_ref[pl.ds(pl.multiple_of(place, 96), 96), shared] = packed
-        turned = pltpu.roll(packed.astype(jnp.float32), 64, 1).astype(jnp.bfloat16)
-        kv_ref[pl.ds(pl.multiple_of(place + 96, 96), 96), shared] = turned
-
-    def pair(g, _):
-        slots = [info_ref[32 + 2 * g + i] for i in range(2)]
-        count = info_ref[24 + slots[1]]
+    for copy in copies:
+        copy.wait()
+
+    def some(g, _):
+        slots = [info_ref[32 + group * g + i] for i in range(group)]
+        count = info_ref[24 + slots[-1]]
         jobs = []
         for s in slots:
             rows = pl.ds(pl.multiple_of(s * FR, FR), FR)
             first = jnp.minimum(info_ref[16 + s], PAD - count * TILE)
-            jobs.append((q_ref[rows, head * 128 : head * 128 + 128], qid_ref[rows, :], first))
-
-        def attend_pair(n):
+            jobs.append((q_ref[rows, :], qid_ref[rows, :], first))
+
+        def attend_some(n):
             outs = attend_jobs(jobs, n, kid_ref, kv_ref, head * 128)
             lane = lax.broadcasted_iota(jnp.int32, (FR, 128), 1)
             spare = (lane[:48] >= 64) & (lane[:48] < 96) if head == 0 else (lane[:48] >= 32) & (lane[:48] < 64)
@@ -154,22 +134,26 @@
                     out_ref[s, i * 48 : (i + 1) * 48, :] = moved.astype(jnp.bfloat16)
 
         for n in range(1, MAX_TILES + 1):
-            pl.when(count == n)(functools.partial(attend_pair, n))
+            pl.when(count == n)(functools.partial(attend_some, n))
         return 0
 
-    lax.fori_loop(0, NZ // 2, pair, 0)
-
-
-def attend(head, *args):
+    lax.fori_loop(0, NZ // group, some, 0)
+
+
+def attend(head, info, qid, kid, q, *parts, group=2):
     return pl.pallas_call(
-        functools.partial(attend_kernel, head),
-        in_specs=[SMEM] + [VMEM] * (len(args) - 1),
+        functools.partial(attend_kernel, head, group),
+        in_specs=[SMEM, VMEM, VMEM] + [HBM] * (1 + len(parts)),
         out_specs=VMEM,
         out_shape=jax.ShapeDtypeStruct((NZ, 144, 128), jnp.bfloat16),
-        scratch_shapes=[pltpu.VMEM((PAD, 256), jnp.bfloat16)],
+        scratch_shapes=[
+            pltpu.VMEM((PAD, 256), jnp.bfloat16),
+            pltpu.VMEM((ROWS, 128), jnp.bfloat16),
+            pltpu.SemaphoreType.DMA((1 + 4 * NZ,)),
+        ],
         compiler_params=pltpu.CompilerParams(vmem_limit_bytes=36 << 20),
         cost_estimate=pl.CostEstimate(flops=4 << 30, bytes_accessed=4 << 20, transcendentals=2 << 20),
-    )(*args)
+    )(info, qid, kid, q, *parts)
 
 
 def unpack_kernel(first_ref, second_ref, out_ref):
@@ -230,13 +214,10 @@
     w = gather_weights(w_qkv)
     info, qid, kid = plan(seg_ids[0], assign[0], lax.axis_index("xh"))
     x, w, info, qid, kid = lax.optimization_barrier((x, w, info, qid, kid))
-    kv, wire0 = project_call(project_first, [256], (x, w), [256])
-    other0 = swap(wire0, "xh")
-    last, q, wire1 = project_call(project_second, [128, 256], (x, w, kv), [640, 256])
-    other1 = swap(wire1, "xh")
-    packed0 = attend(0, info, qid, kid, q, kv, other0)
-    home0 = lax.all_to_all(packed0, "z", 0, 0, tiled=True)
-    packed1 = attend(1, info, qid, kid, q, kv, last, other1)
+    most, last, q = project(x, w)
+    other_most, other_last = swap(most, "xh"), swap(last, "xh")
+    home0 = lax.all_to_all(attend(0, info, qid, kid, q, most, other_most), "z", 0, 0, tiled=True)
+    packed1 = attend(1, info, qid, kid, q, most, other_most, last, other_last)
     home1 = lax.all_to_all(packed1, "z", 0, 0, tiled=True)
     return unpack(home0, home1)
 

time: 157 us -> 166 us (1.057)
  waiting for transfers between devices: 50.6 us -> 60.4 us
  Pallas kernels: 25.5 us -> 22.5 us
  blocking collectives: 35.7 us -> 37.6 us
    ppermute x5, waiting for transfers between devices: 23.5 us -> 35 us  [swap(): return lax.ppermute(x, axis, [(0, 1), (1, 0)])]
    pallas_call x4 -> x3, Pallas kernels: 23.2 us -> 20.2 us  [the longest x2 13.1 us: attend(): pl.pallas_call(functools.partial(attend_kernel, head, group), in_specs=[S...]
    all_to_all x1, blocking collectives: 13.2 us -> 15 us  [body(): lax.all_to_all(attend(0, info, qid, kid, q, most, other_most), 'z', 0, 0,...]
    all_to_all x1, waiting for transfers between devices: 5.53 us -> 3.81 us  [body(): home1 = lax.all_to_all(packed1, 'z', 0, 0, tiled=True)]
    unnamed x17 -> x15, local copies, waits for them, and re-layouts: 4.53 us -> 4.91 us
  transfers between devices with their start and end apart: 7 -> 7, of which waited for: 6 -> 6; matrix products, arithmetic and copies ran while one was open for 5% -> 4% of each run, Pallas kernels for 7% -> 4%
where the time goes in v4:
time: 166 us; the launch traced here: 165 us
  waiting for transfers between devices  60.4 us (36%)
  blocking collectives  37.6 us (23%)
  Pallas kernels  22.5 us (14%)
  starting transfers between devices  19.5 us (12%)
  between operations  13.6 us (8%)
  local copies, waits for them, and re-layouts  7.41 us (4%)
  other arithmetic  4.42 us (3%)
    ppermute x5, waiting for transfers between devices, swap(): return lax.ppermute(x, axis, [(0, 1), (1, 0)])  35 us
    all_to_all x1, blocking collectives, gather_weights(): lax.all_to_all(jnp.broadcast_to(shard[None], (8,) + shard.shape), 'y', 0,...  22.5 us
    all_gather x1, waiting for transfers between devices, body(): x = lax.all_gather(frames, 'z', axis=0, tiled=True)  20.8 us
    ppermute x5, starting transfers between devices, swap(): return lax.ppermute(x, axis, [(0, 1), (1, 0)])  15.3 us
    all_to_all x1, blocking collectives, body(): lax.all_to_all(attend(0, info, qid, kid, q, most, other_most), 'z', 0, 0,...  15 us
    pallas_call x2, Pallas kernels, attend(): pl.pallas_call(functools.partial(attend_kernel, head, group), in_specs=[S...  13.1 us
    pallas_call x1, Pallas kernels, project(): pl.pallas_call(project_kernel, grid=(ROWS // step,), in_specs=[row(D), VM...  7.08 us
    unnamed x15, local copies, waits for them, and re-layouts  4.91 us
  transfers between devices with their start and end apart: 7, of which 6 were waited for; matrix products, arithmetic and copies ran while one was open for 4% of the time, Pallas kernels for 4%

profile of v4, /device:TPU:6, one launch (start us, length us, event | category | flops | bytes accessed | tf_op | source)
XLA Modules:
  0.0 165.3 jit_solution(8320261633768774395)
XLA Ops:
  6.5 0.7 all-gather.2.cloned.1.call-update
  7.3 0.8 copy.12
  8.1 0.1 reshape.112
  8.2 3.3 %collective-permute-start = (bf16[48,288]{1,0:T(8,128)(2,1)S(1)}, bf16[48,288]{1,0:T(8,128)(2,1)S(1)}, u32[]{:S(2)}, u32[]{:S(2)}) collective-permute-start(bf16[48,288]{1,0:T(8,128)(2,1)S(1)} %reshape.112), channel_id=1, source_target_pairs={{0,1},{1,0},{2,3},{3,2},{4,5},{5,4},{6,7},{7,6},{8,9},{9,8},{10,11... | collective-permute-start | bytes 82952 | tf_op jit(solution)/shard_map/ppermute | solution.py:28
  11.5 4.0 %collective-permute-done = bf16[48,288]{1,0:T(8,128)(2,1)S(1)} collective-permute-done((bf16[48,288]{1,0:T(8,128)(2,1)S(1)}, bf16[48,288]{1,0:T(8,128)(2,1)S(1)}, u32[]{:S(2)}, u32[]{:S(2)}) %collective-permute-start) | collective-permute-done | bytes 27680 | tf_op jit(solution)/shard_map/ppermute | solution.py:28
  15.5 0.1 slice_bitcast_fusion
  15.6 0.1 concatenate.9
  15.8 22.5 %all_to_all.15 = bf16[8,48,640]{2,1,0:T(8,128)(2,1)S(1)} all-to-all(bf16[8,48,640]{2,1,0:T(8,128)(2,1)S(1)} %broadcast_in_dim.23), channel_id=1, replica_groups=mesh['y'=8,'xl'=2,'core'=2,'z'=8,'xh'=2] {'y'}, dimensions={0} | all-to-all | bytes 983040 | tf_op jit(solution)/shard_map/all_to_all | solution.py:42
  38.3 2.7 %collective-permute-start.1 = (bf16[8,48,640]{2,1,0:T(8,128)(2,1)S(1)}, bf16[8,48,640]{2,1,0:T(8,128)(2,1)S(1)}, u32[]{:S(2)}, u32[]{:S(2)}) collective-permute-start(bf16[8,48,640]{2,1,0:T(8,128)(2,1)S(1)} %all_to_all.15), channel_id=1, source_target_pairs={{0,32},{32,0},{1,33},{33,1},{2,34},{34,2},{3,35},{35,3},{4,36},{36... | collective-permute-start | bytes 1474568 | tf_op jit(solution)/shard_map/ppermute | solution.py:28
  41.1 0.5 broadcast.203
  41.6 0.7 reduce.17
  42.3 0.1 reshape_squeeze.6
  42.3 0.7 reduce.18
  43.0 0.1 reshape_squeeze.7
  43.1 0.2 and_reduce_fusion
  43.3 0.1 fusion.2
  43.5 0.6 gather_fusion
  44.0 6.0 %collective-permute-done.1 = bf16[8,48,640]{2,1,0:T(8,128)(2,1)S(1)} collective-permute-done((bf16[8,48,640]{2,1,0:T(8,128)(2,1)S(1)}, bf16[8,48,640]{2,1,0:T(8,128)(2,1)S(1)}, u32[]{:S(2)}, u32[]{:S(2)}) %collective-permute-start.1) | collective-permute-done | bytes 491552 | tf_op jit(solution)/shard_map/ppermute | solution.py:28
  50.0 0.1 select_bitcast_fusion.3
  50.1 0.1 pad_maximum_fusion.1
  50.2 1.9 %collective-permute-start.2 = (bf16[8,2,48,640]{3,2,1,0:T(8,128)(2,1)S(1)}, bf16[8,2,48,640]{3,2,1,0:T(8,128)(2,1)S(1)}, u32[]{:S(2)}, u32[]{:S(2)}) collective-permute-start(bf16[8,2,48,640]{3,2,1,0:T(8,128)(2,1)S(1)} %pad_maximum_fusion.1), channel_id=1, source_target_pairs={{0,16},{16,0},{1,17},{17,1},{2,18},{18,2},{3,19},{19,3},{4,20},{20... | collective-permute-start | bytes 2949128 | tf_op jit(solution)/shard_map/ppermute | solution.py:28
  52.1 0.1 broadcast_select_fusion
  52.2 0.1 select_n.123
  52.3 0.2 slice_reduce_fusion
  52.5 0.2 select_reduce_fusion.1
  52.7 0.2 convert_reduce_fusion
  53.0 0.2 convert_reduce_fusion.2
  53.1 0.1 select_reduce_fusion
  53.2 0.1 concatenate.10.info_ref
  53.3 1.4 collective-permute-done.2
  54.7 0.2 select_bitcast_fusion.1
  54.9 1.5 pad_maximum_fusion
  56.4 20.8 %all-gather.2.cloned.1.call-done.x_ref = bf16[1536,1536]{1,0:T(8,128)(2,1)} async-done(((bf16[192,1536]{1,0:T(8,128)(2,1)}), bf16[1536,1536]{1,0:T(8,128)(2,1)}) %all-gather.2.cloned.1.call-update) | async-done | bytes 4718608 | tf_op jit(solution)/shard_map/all_gather | solution.py:213
  77.2 7.1 %shard_map.46 = (bf16[1536,256]{1,0:T(8,128)(2,1)}, bf16[1536,128]{1,0:T(8,128)(2,1)}, bf16[1536,256]{1,0:T(8,128)(2,1)}) custom-call(bf16[1536,1536]{1,0:T(8,128)(2,1)} %all-gather.2.cloned.1.call-done.x_ref, bf16[1536,640]{1,0:T(8,128)(2,1)} %bitcast.31), custom_call_target="tpu_custom_call" | custom-call | flops 3019898880 | bytes 10485760 | tf_op jit(solution)/shard_map/pallas_call | solution.py:58
  84.3 3.3 %collective-permute-start.3 = (bf16[1536,256]{1,0:T(8,128)(2,1)}, bf16[1536,256]{1,0:T(8,128)(2,1)S(1)}, u32[]{:S(2)}, u32[]{:S(2)}) collective-permute-start(bf16[1536,256]{1,0:T(8,128)(2,1)} %get-tuple-element.19.refs_0_), channel_id=1, source_target_pairs={{0,1},{1,0},{2,3},{3,2},{4,5},{5,4},{6,7},{7,6},{8,9},{9,8},{10,11... | collective-permute-start | bytes 2359304 | tf_op jit(solution)/shard_map/ppermute | solution.py:28
  87.7 4.0 %collective-permute-start.4 = (bf16[1536,128]{1,0:T(8,128)(2,1)}, bf16[1536,128]{1,0:T(8,128)(2,1)S(1)}, u32[]{:S(2)}, u32[]{:S(2)}) collective-permute-start(bf16[1536,128]{1,0:T(8,128)(2,1)} %get-tuple-element.20.refs_2_), channel_id=1, source_target_pairs={{0,1},{1,0},{2,3},{3,2},{4,5},{5,4},{6,7},{7,6},{8,9},{9,8},{10,11... | collective-permute-start | bytes 1179656 | tf_op jit(solution)/shard_map/ppermute | solution.py:28
  91.7 0.3 copy.15.qid_ref
  92.0 23.7 %collective-permute-done.4.refs_3_ = bf16[1536,128]{1,0:T(8,128)(2,1)S(1)} collective-permute-done((bf16[1536,128]{1,0:T(8,128)(2,1)}, bf16[1536,128]{1,0:T(8,128)(2,1)S(1)}, u32[]{:S(2)}, u32[]{:S(2)}) %collective-permute-start.4) | collective-permute-done | bytes 393248 | tf_op jit(solution)/shard_map/ppermute | solution.py:28
  115.6 1.1 copy-done
  116.8 1.0 copy-done.2
  117.8 1.1 copy-done.3
  118.9 6.1 %shard_map.48 = bf16[8,144,128]{2,1,0:T(8,128)(2,1)} custom-call(s32[40]{0:T(128)S(1)} %concatenate.10.info_ref, s32[1536,1]{1,0:T(8,128)S(1)} %copy.15.qid_ref, s32[1,3328]{1,0:T(1,128)S(1)} %broadcast_in_dim.47.kid_ref, bf16[1536,256]{1,0:T(8,128)(2,1)S(1)} %copy-done.3, bf16[1536,256]{1,0:T(8,128)(2,1)S(1)} %copy-done, ...), custom_call_target="tpu_custom_call" | custom-call | flops 4294967296 | bytes 4194304 | tf_op jit(solution)/shard_map/pallas_call | solution.py:144
  125.0 4.2 %all-to-all-start.2 = ((bf16[8,144,128]{2,1,0:T(8,128)(2,1)}), bf16[8,144,128]{2,1,0:T(8,128)(2,1)S(1)}, u32[]{:S(2)}, u32[]{:S(2)}) async-start(bf16[8,144,128]{2,1,0:T(8,128)(2,1)} %shard_map.48), calls=%async_computation.2 | async-start | bytes 589824 | tf_op jit(solution)/shard_map/all_to_all | solution.py:221
  129.1 1.1 copy-done.4
  130.3 7.1 %shard_map.47 = bf16[8,144,128]{2,1,0:T(8,128)(2,1)S(1)} custom-call(s32[40]{0:T(128)S(1)} %concatenate.10.info_ref, s32[1536,1]{1,0:T(8,128)S(1)} %copy.15.qid_ref, s32[1,3328]{1,0:T(1,128)S(1)} %broadcast_in_dim.47.kid_ref, bf16[1536,256]{1,0:T(8,128)(2,1)S(1)} %copy-done.4, bf16[1536,256]{1,0:T(8,128)(2,1)S(1)} %copy-done.1, ...), custom_call_target="tpu_custom_call" | custom-call | flops 4294967296 | bytes 4194304 | tf_op jit(solution)/shard_map/pallas_call | solution.py:144
  137.3 3.8 %all-to-all-done.2.second_ref = bf16[8,144,128]{2,1,0:T(8,128)(2,1)S(1)} async-done(((bf16[8,144,128]{2,1,0:T(8,128)(2,1)}), bf16[8,144,128]{2,1,0:T(8,128)(2,1)S(1)}, u32[]{:S(2)}, u32[]{:S(2)}) %all-to-all-start.2) | async-done | bytes 294944 | tf_op jit(solution)/shard_map/all_to_all | solution.py:221
  141.2 15.0 %all_to_all.16.first_ref = bf16[8,144,128]{2,1,0:T(8,128)(2,1)S(1)} all-to-all(bf16[8,144,128]{2,1,0:T(8,128)(2,1)S(1)} %shard_map.47), channel_id=1, replica_groups=mesh['y'=8,'xl'=2,'core'=2,'z'=8,'xh'=2] {'z'}, dimensions={0} | all-to-all | bytes 589824 | tf_op jit(solution)/shard_map/all_to_all | solution.py:219
  156.2 2.2 %shard_map.49 = bf16[192,1536]{1,0:T(8,128)(2,1)} custom-call(bf16[8,144,128]{2,1,0:T(8,128)(2,1)S(1)} %all_to_all.16.first_ref, bf16[8,144,128]{2,1,0:T(8,128)(2,1)S(1)} %all-to-all-done.2.second_ref), custom_call_target="tpu_custom_call" | custom-call | tf_op jit(solution)/shard_map/pallas_call | solution.py:184
  (19 shorter events, 0.1 us)
Async XLA Ops:
  6.5 35.1 %copy-start.6 = (s32[1,16]{1,0:T(1,128)S(1)}, s32[1,16]{1,0:T(1,128)}, u32[]{:S(2)}) copy-start(s32[1,16]{1,0:T(1,128)} %param.6) | copy-start | bytes 196
  6.5 35.8 %copy-start.5 = (s32[1,3072]{1,0:T(1,128)S(1)}, s32[1,3072]{1,0:T(1,128)}, u32[]{:S(2)}) copy-start(s32[1,3072]{1,0:T(1,128)} %param.5) | copy-start | bytes 36868
  6.5 70.7 %all-gather.2.cloned.1.call-start = ((), (), s32[]{:S(2)}) async-start(), calls=%async_computation.3 | async-start | bytes 5308416 | tf_op jit(solution)/shard_map/all_gather | solution.py:213
  8.2 7.4 %collective-permute-start = (bf16[48,288]{1,0:T(8,128)(2,1)S(1)}, bf16[48,288]{1,0:T(8,128)(2,1)S(1)}, u32[]{:S(2)}, u32[]{:S(2)}) collective-permute-start(bf16[48,288]{1,0:T(8,128)(2,1)S(1)} %reshape.112), channel_id=1, source_target_pairs={{0,1},{1,0},{2,3},{3,2},{4,5},{5,4},{6,7},{7,6},{8,9},{9,8},{10,11... | collective-permute-start | bytes 82952 | tf_op jit(solution)/shard_map/ppermute | solution.py:28
  38.3 11.7 %collective-permute-start.1 = (bf16[8,48,640]{2,1,0:T(8,128)(2,1)S(1)}, bf16[8,48,640]{2,1,0:T(8,128)(2,1)S(1)}, u32[]{:S(2)}, u32[]{:S(2)}) collective-permute-start(bf16[8,48,640]{2,1,0:T(8,128)(2,1)S(1)} %all_to_all.15), channel_id=1, source_target_pairs={{0,32},{32,0},{1,33},{33,1},{2,34},{34,2},{3,35},{35,3},{4,36},{36... | collective-permute-start | bytes 1474568 | tf_op jit(solution)/shard_map/ppermute | solution.py:28
  50.2 4.5 %collective-permute-start.2 = (bf16[8,2,48,640]{3,2,1,0:T(8,128)(2,1)S(1)}, bf16[8,2,48,640]{3,2,1,0:T(8,128)(2,1)S(1)}, u32[]{:S(2)}, u32[]{:S(2)}) collective-permute-start(bf16[8,2,48,640]{3,2,1,0:T(8,128)(2,1)S(1)} %pad_maximum_fusion.1), channel_id=1, source_target_pairs={{0,16},{16,0},{1,17},{17,1},{2,18},{18,2},{3,19},{19,3},{4,20},{20... | collective-permute-start | bytes 2949128 | tf_op jit(solution)/shard_map/ppermute | solution.py:28
  84.3 31.3 %collective-permute-start.3 = (bf16[1536,256]{1,0:T(8,128)(2,1)}, bf16[1536,256]{1,0:T(8,128)(2,1)S(1)}, u32[]{:S(2)}, u32[]{:S(2)}) collective-permute-start(bf16[1536,256]{1,0:T(8,128)(2,1)} %get-tuple-element.19.refs_0_), channel_id=1, source_target_pairs={{0,1},{1,0},{2,3},{3,2},{4,5},{5,4},{6,7},{7,6},{8,9},{9,8},{10,11... | collective-permute-start | bytes 2359304 | tf_op jit(solution)/shard_map/ppermute | solution.py:28
  87.7 28.0 %collective-permute-start.4 = (bf16[1536,128]{1,0:T(8,128)(2,1)}, bf16[1536,128]{1,0:T(8,128)(2,1)S(1)}, u32[]{:S(2)}, u32[]{:S(2)}) collective-permute-start(bf16[1536,128]{1,0:T(8,128)(2,1)} %get-tuple-element.20.refs_2_), channel_id=1, source_target_pairs={{0,1},{1,0},{2,3},{3,2},{4,5},{5,4},{6,7},{7,6},{8,9},{9,8},{10,11... | collective-permute-start | bytes 1179656 | tf_op jit(solution)/shard_map/ppermute | solution.py:28
  115.6 1.1 copy-start
  116.8 1.0 copy-start.2
  117.7 1.1 copy-start.3
  118.9 10.2 %copy-start.1 = (bf16[1536,256]{1,0:T(8,128)(2,1)S(1)}, bf16[1536,256]{1,0:T(8,128)(2,1)}, u32[]{:S(2)}) copy-start(bf16[1536,256]{1,0:T(8,128)(2,1)} %get-tuple-element.19.refs_0_) | copy-start | bytes 2359300
  125.0 16.2 %all-to-all-start.2 = ((bf16[8,144,128]{2,1,0:T(8,128)(2,1)}), bf16[8,144,128]{2,1,0:T(8,128)(2,1)S(1)}, u32[]{:S(2)}, u32[]{:S(2)}) async-start(bf16[8,144,128]{2,1,0:T(8,128)(2,1)} %shard_map.48), calls=%async_computation.2 | async-start | bytes 589824 | tf_op jit(solution)/shard_map/all_to_all | solution.py:221
  129.1 1.1 copy-start.4
Sparse Core Ops, SparseCore 0:
  9.4 67.7 all-gather.1

commit v5 on v4

--- a/solution.py
+++ b/solution.py
@@ -21,7 +21,6 @@
 SIZES = (8, 2, 2, 8, 2)
 VMEM = pl.BlockSpec(memory_space=pltpu.VMEM)
 SMEM = pl.BlockSpec(memory_space=pltpu.SMEM)
-HBM = pl.BlockSpec(memory_space=pltpu.HBM)
 
 
 def swap(x, axis):
@@ -61,7 +60,7 @@
         in_specs=[row(D), VMEM],
         out_specs=[row(width) for width in widths],
         out_shape=[jax.ShapeDtypeStruct((ROWS, width), jnp.bfloat16) for width in widths],
-        compiler_params=pltpu.CompilerParams(vmem_limit_bytes=56 << 20),
+        compiler_params=pltpu.CompilerParams(vmem_limit_bytes=24 << 20),
         cost_estimate=pl.CostEstimate(flops=2 * ROWS * D * 640, bytes_accessed=10 << 20, transcendentals=0),
     )(x, w)
 
@@ -94,25 +93,20 @@
     return outs
 
 
-def attend_kernel(head, group, info_ref, qid_ref, kid_ref, q_hbm, *refs):
-    *parts, out_ref, kv_ref, q_ref, sems = refs
-    copies = [pltpu.make_async_copy(q_hbm.at[:, head * 128 : head * 128 + 128], q_ref, sems.at[0])]
+def attend_kernel(head, group, info_ref, qid_ref, kid_ref, q_ref, *refs):
+    *parts, out_ref, kv_ref = refs
+    kv_ref[SEQ:, :] = jnp.zeros((TILE, 256), jnp.bfloat16)
+    if head == 1:
+        out_ref[:, :144, :] = parts[4][...]
     for z in range(NZ):
-        rows = pl.ds(z * FR, FR)
+        rows = slice(z * FR, (z + 1) * FR)
         for side in range(2):
             at = pl.ds(pl.multiple_of(info_ref[side * NZ + z] * FR, FR), FR)
-            sem = 1 + 4 * z + 2 * side
             if head == 0:
-                copies.append(pltpu.make_async_copy(parts[side].at[rows, :], kv_ref.at[at, :], sems.at[sem]))
+                kv_ref[at, :] = parts[side][rows, :]
             else:
-                most, last = parts[side], parts[2 + side]
-                copies.append(pltpu.make_async_copy(most.at[rows, 128:], kv_ref.at[at, :128], sems.at[sem]))
-                copies.append(pltpu.make_async_copy(last.at[rows, :], kv_ref.at[at, 128:], sems.at[sem + 1]))
-    for copy in copies:
-        copy.start()
-    kv_ref[SEQ:, :] = jnp.zeros((TILE, 256), jnp.bfloat16)
-    for copy in copies:
-        copy.wait()
+                kv_ref[at, :128] = parts[side][rows, 128:]
+                kv_ref[at, 128:] = parts[2 + side][rows, :]
 
     def some(g, _):
         slots = [info_ref[32 + group * g + i] for i in range(group)]
@@ -121,7 +115,7 @@
         for s in slots:
             rows = pl.ds(pl.multiple_of(s * FR, FR), FR)
             first = jnp.minimum(info_ref[16 + s], PAD - count * TILE)
-            jobs.append((q_ref[rows, :], qid_ref[rows, :], first))
+            jobs.append((q_ref[rows, head * 128 : head * 128 + 128], qid_ref[rows, :], first))
 
         def attend_some(n):
             outs = attend_jobs(jobs, n, kid_ref, kv_ref, head * 128)
@@ -131,7 +125,7 @@
                 m = jnp.where(lane < (64 if head == 0 else 32), acc[:, 128:], acc[:, :128])
                 for i, by in enumerate((96, 64, 32)):
                     moved = jnp.where(spare, pltpu.roll(m[144:], by, 1), m[i * 48 : (i + 1) * 48])
-                    out_ref[s, i * 48 : (i + 1) * 48, :] = moved.astype(jnp.bfloat16)
+                    out_ref[s, head * 144 + i * 48 : head * 144 + (i + 1) * 48, :] = moved.astype(jnp.bfloat16)
 
         for n in range(1, MAX_TILES + 1):
             pl.when(count == n)(functools.partial(attend_some, n))
@@ -143,26 +137,22 @@
 def attend(head, info, qid, kid, q, *parts, group=2):
     return pl.pallas_call(
         functools.partial(attend_kernel, head, group),
-        in_specs=[SMEM, VMEM, VMEM] + [HBM] * (1 + len(parts)),
+        in_specs=[SMEM, VMEM, VMEM] + [VMEM] * (1 + len(parts)),
         out_specs=VMEM,
-        out_shape=jax.ShapeDtypeStruct((NZ, 144, 128), jnp.bfloat16),
-        scratch_shapes=[
-            pltpu.VMEM((PAD, 256), jnp.bfloat16),
-            pltpu.VMEM((ROWS, 128), jnp.bfloat16),
-            pltpu.SemaphoreType.DMA((1 + 4 * NZ,)),
-        ],
-        compiler_params=pltpu.CompilerParams(vmem_limit_bytes=36 << 20),
+        out_shape=jax.ShapeDtypeStruct((NZ, 144 * (1 + head), 128), jnp.bfloat16),
+        scratch_shapes=[pltpu.VMEM((PAD, 256), jnp.bfloat16)],
+        compiler_params=pltpu.CompilerParams(vmem_limit_bytes=28 << 20),
         cost_estimate=pl.CostEstimate(flops=4 << 30, bytes_accessed=4 << 20, transcendentals=2 << 20),
     )(info, qid, kid, q, *parts)
 
 
-def unpack_kernel(first_ref, second_ref, out_ref):
+def unpack_kernel(in_ref, out_ref):
     lane = lax.broadcasted_iota(jnp.int32, (FR, 128), 1)
     for z in range(0, NZ, 2):
         heads = []
         for i in (z, z + 1):
-            for head, ref in enumerate((first_ref, second_ref)):
-                m = ref[i].astype(jnp.float32)
+            for head in range(2):
+                m = in_ref[i, head * 144 : (head + 1) * 144, :].astype(jnp.float32)
                 tail = [pltpu.roll(m[j * 48 : (j + 1) * 48], by, 1) for j, by in enumerate((32, 64, 96))]
                 if head == 0:
                     parts = jnp.where(lane[:48] >= 96, tail[0], jnp.where(lane[:48] < 32, tail[1], tail[2]))
@@ -180,14 +170,14 @@
             out_ref[:, z * 192 + i * 128 : z * 192 + (i + 1) * 128] = tile.astype(jnp.bfloat16)
 
 
-def unpack(first, second):
+def unpack(packed):
     return pl.pallas_call(
         unpack_kernel,
-        in_specs=[VMEM] * 2,
+        in_specs=[VMEM],
         out_specs=VMEM,
         out_shape=jax.ShapeDtypeStruct((FR, D), jnp.bfloat16),
         compiler_params=pltpu.CompilerParams(vmem_limit_bytes=8 << 20),
-    )(first, second)
+    )(packed)
 
 
 def plan(ids, order, xh):
@@ -216,10 +206,9 @@
     x, w, info, qid, kid = lax.optimization_barrier((x, w, info, qid, kid))
     most, last, q = project(x, w)
     other_most, other_last = swap(most, "xh"), swap(last, "xh")
-    home0 = lax.all_to_all(attend(0, info, qid, kid, q, most, other_most), "z", 0, 0, tiled=True)
-    packed1 = attend(1, info, qid, kid, q, most, other_most, last, other_last)
-    home1 = lax.all_to_all(packed1, "z", 0, 0, tiled=True)
-    return unpack(home0, home1)
+    packed = attend(0, info, qid, kid, q, most, other_most)
+    packed = attend(1, info, qid, kid, q, most, other_most, last, other_last, packed)
+    return unpack(lax.all_to_all(packed, "z", 0, 0, tiled=True))
 
 
 def solution(mesh):

time: 166 us -> 152 us (0.916)
  waiting for transfers between devices: 60.4 us -> 51.9 us
  Pallas kernels: 22.5 us -> 15.8 us
  blocking collectives: 37.6 us -> 44.1 us
  starting transfers between devices: 19.5 us -> 15.3 us
    all_to_all x1, blocking collectives: 15 us -> 21.6 us  [body(): return unpack(lax.all_to_all(packed, 'z', 0, 0, tiled=True))]
    ppermute x5, waiting for transfers between devices: 35 us -> 29.1 us  [swap(): return lax.ppermute(x, axis, [(0, 1), (1, 0)])]
    all_to_all x1 -> x0, starting transfers between devices: 4.16 us -> none  [body(): home1 = lax.all_to_all(packed1, 'z', 0, 0, tiled=True)]
    all_to_all x1 -> x0, waiting for transfers between devices: 3.81 us -> none  [body(): home1 = lax.all_to_all(packed1, 'z', 0, 0, tiled=True)]
    pallas_call x2, Pallas kernels: 13.1 us -> 9.58 us  [attend(): pl.pallas_call(functools.partial(attend_kernel, head, group), in_specs=[S...]
    pallas_call x1, Pallas kernels: 7.08 us -> 4 us  [project(): pl.pallas_call(project_kernel, grid=(ROWS // step,), in_specs=[row(D), VM...]
    unnamed x15 -> x11, local copies, waits for them, and re-layouts: 4.91 us -> 4.86 us
  transfers between devices with their start and end apart: 7 -> 6, of which waited for: 6 -> 6; matrix products, arithmetic and copies ran while one was open for 4% -> 4% of each run, Pallas kernels for 4% -> 3%
where the time goes in v5:
time: 152 us; the launch traced here: 151 us
  waiting for transfers between devices  51.9 us (34%)
  blocking collectives  44.1 us (29%)
  Pallas kernels  15.8 us (10%)
  starting transfers between devices  15.3 us (10%)
  between operations  13.6 us (9%)
  local copies, waits for them, and re-layouts  7.36 us (5%)
  other arithmetic  3.12 us (2%)
    ppermute x5, waiting for transfers between devices, swap(): return lax.ppermute(x, axis, [(0, 1), (1, 0)])  29.1 us
    all_to_all x1, blocking collectives, gather_weights(): lax.all_to_all(jnp.broadcast_to(shard[None], (8,) + shard.shape), 'y', 0,...  22.5 us
    all_gather x1, waiting for transfers between devices, body(): x = lax.all_gather(frames, 'z', axis=0, tiled=True)  22.1 us
    all_to_all x1, blocking collectives, body(): return unpack(lax.all_to_all(packed, 'z', 0, 0, tiled=True))  21.6 us
    ppermute x5, starting transfers between devices, swap(): return lax.ppermute(x, axis, [(0, 1), (1, 0)])  15.3 us
    pallas_call x2, Pallas kernels, attend(): pl.pallas_call(functools.partial(attend_kernel, head, group), in_specs=[S...  9.58 us
    unnamed x11, local copies, waits for them, and re-layouts  4.86 us
    pallas_call x1, Pallas kernels, project(): pl.pallas_call(project_kernel, grid=(ROWS // step,), in_specs=[row(D), VM...  4 us
  transfers between devices with their start and end apart: 6, of which 6 were waited for; matrix products, arithmetic and copies ran while one was open for 4% of the time, Pallas kernels for 3%

profile of v5, /device:TPU:6, one launch (start us, length us, event | category | flops | bytes accessed | tf_op | source)
XLA Modules:
  0.0 151.2 jit_solution(1806339294782530495)
XLA Ops:
  6.5 0.0 all-gather.2.cloned.1.call-start
  6.5 0.7 all-gather.2.cloned.1.call-update
  7.3 0.8 copy.12
  8.1 0.1 reshape.112
  8.2 3.3 %collective-permute-start = (bf16[48,288]{1,0:T(8,128)(2,1)S(1)}, bf16[48,288]{1,0:T(8,128)(2,1)S(1)}, u32[]{:S(2)}, u32[]{:S(2)}) collective-permute-start(bf16[48,288]{1,0:T(8,128)(2,1)S(1)} %reshape.112), channel_id=1, source_target_pairs={{0,1},{1,0},{2,3},{3,2},{4,5},{5,4},{6,7},{7,6},{8,9},{9,8},{10,11... | collective-permute-start | bytes 82952 | tf_op jit(solution)/shard_map/ppermute | solution.py:27
  11.5 4.0 %collective-permute-done = bf16[48,288]{1,0:T(8,128)(2,1)S(1)} collective-permute-done((bf16[48,288]{1,0:T(8,128)(2,1)S(1)}, bf16[48,288]{1,0:T(8,128)(2,1)S(1)}, u32[]{:S(2)}, u32[]{:S(2)}) %collective-permute-start) | collective-permute-done | bytes 27680 | tf_op jit(solution)/shard_map/ppermute | solution.py:27
  15.5 0.1 slice_bitcast_fusion
  15.6 0.1 concatenate.9
  15.8 22.5 %all_to_all.10 = bf16[8,48,640]{2,1,0:T(8,128)(2,1)S(1)} all-to-all(bf16[8,48,640]{2,1,0:T(8,128)(2,1)S(1)} %broadcast_in_dim.23), channel_id=1, replica_groups=mesh['y'=8,'xl'=2,'core'=2,'z'=8,'xh'=2] {'y'}, dimensions={0} | all-to-all | bytes 983040 | tf_op jit(solution)/shard_map/all_to_all | solution.py:41
  38.3 2.7 %collective-permute-start.1 = (bf16[8,48,640]{2,1,0:T(8,128)(2,1)S(1)}, bf16[8,48,640]{2,1,0:T(8,128)(2,1)S(1)}, u32[]{:S(2)}, u32[]{:S(2)}) collective-permute-start(bf16[8,48,640]{2,1,0:T(8,128)(2,1)S(1)} %all_to_all.10), channel_id=1, source_target_pairs={{0,32},{32,0},{1,33},{33,1},{2,34},{34,2},{3,35},{35,3},{4,36},{36... | collective-permute-start | bytes 1474568 | tf_op jit(solution)/shard_map/ppermute | solution.py:27
  41.1 0.5 broadcast.203
  41.6 0.0 copy-done.4
  41.6 0.7 reduce.17
  42.3 0.1 reshape_squeeze.6
  42.3 0.7 reduce.18
  43.0 0.1 reshape_squeeze.7
  43.1 0.2 and_reduce_fusion
  43.3 0.1 fusion.2
  43.5 0.6 gather_fusion
  44.0 6.0 %collective-permute-done.1 = bf16[8,48,640]{2,1,0:T(8,128)(2,1)S(1)} collective-permute-done((bf16[8,48,640]{2,1,0:T(8,128)(2,1)S(1)}, bf16[8,48,640]{2,1,0:T(8,128)(2,1)S(1)}, u32[]{:S(2)}, u32[]{:S(2)}) %collective-permute-start.1) | collective-permute-done | bytes 491552 | tf_op jit(solution)/shard_map/ppermute | solution.py:27
  50.0 0.1 select_bitcast_fusion.3
  50.1 0.1 pad_maximum_fusion.1
  50.2 1.9 %collective-permute-start.2 = (bf16[8,2,48,640]{3,2,1,0:T(8,128)(2,1)S(1)}, bf16[8,2,48,640]{3,2,1,0:T(8,128)(2,1)S(1)}, u32[]{:S(2)}, u32[]{:S(2)}) collective-permute-start(bf16[8,2,48,640]{3,2,1,0:T(8,128)(2,1)S(1)} %pad_maximum_fusion.1), channel_id=1, source_target_pairs={{0,16},{16,0},{1,17},{17,1},{2,18},{18,2},{3,19},{19,3},{4,20},{20... | collective-permute-start | bytes 2949128 | tf_op jit(solution)/shard_map/ppermute | solution.py:27
  52.1 0.1 broadcast_select_fusion
  52.2 0.1 select_n.123
  52.3 0.2 slice_reduce_fusion
  52.5 0.2 select_reduce_fusion.1
  52.7 0.2 convert_reduce_fusion
  53.0 0.2 convert_reduce_fusion.2
  53.1 0.1 select_reduce_fusion
  53.2 0.1 concatenate.10.info_ref
  53.3 1.4 collective-permute-done.2
  54.7 0.2 select_bitcast_fusion.1
  54.9 0.2 pad_maximum_fusion
  55.1 22.1 %all-gather.2.cloned.1.call-done.x_ref = bf16[1536,1536]{1,0:T(8,128)(2,1)} async-done(((bf16[192,1536]{1,0:T(8,128)(2,1)}), bf16[1536,1536]{1,0:T(8,128)(2,1)}) %all-gather.2.cloned.1.call-update) | async-done | bytes 4718608 | tf_op jit(solution)/shard_map/all_gather | solution.py:203
  77.2 2.3 %copy-done = bf16[1536,1536]{1,0:T(8,128)(2,1)S(1)} copy-done((bf16[1536,1536]{1,0:T(8,128)(2,1)S(1)}, bf16[1536,1536]{1,0:T(8,128)(2,1)}, u32[]{:S(2)}) %copy-start) | copy-done | bytes 4718616
  79.6 4.0 %shard_map.46 = (bf16[1536,256]{1,0:T(8,128)(2,1)S(1)}, bf16[1536,128]{1,0:T(8,128)(2,1)S(1)}, bf16[1536,256]{1,0:T(8,128)(2,1)S(1)}) custom-call(bf16[1536,1536]{1,0:T(8,128)(2,1)S(1)} %copy-done, bf16[1536,640]{1,0:T(8,128)(2,1)S(1)} %bitcast.31), custom_call_target="tpu_custom_call" | custom-call | flops 3019898880 | bytes 10485760 | tf_op jit(solution)/shard_map/pallas_call | solution.py:57
  83.6 0.9 copy-done.1
  84.5 3.3 %collective-permute-start.3 = (bf16[1536,256]{1,0:T(8,128)(2,1)S(1)}, bf16[1536,256]{1,0:T(8,128)(2,1)S(1)}, u32[]{:S(2)}, u32[]{:S(2)}) collective-permute-start(bf16[1536,256]{1,0:T(8,128)(2,1)S(1)} %get-tuple-element.19.refs_0_), channel_id=1, source_target_pairs={{0,1},{1,0},{2,3},{3,2},{4,5},{5,4},{6,7},{7,6},{8,9},{9,8},{10,11... | collective-permute-start | bytes 2359304 | tf_op jit(solution)/shard_map/ppermute | solution.py:27
  87.8 0.3 copy.16.qid_ref
  88.1 4.0 %collective-permute-start.4 = (bf16[1536,128]{1,0:T(8,128)(2,1)S(1)}, bf16[1536,128]{1,0:T(8,128)(2,1)S(1)}, u32[]{:S(2)}, u32[]{:S(2)}) collective-permute-start(bf16[1536,128]{1,0:T(8,128)(2,1)S(1)} %get-tuple-element.20.refs_2_), channel_id=1, source_target_pairs={{0,1},{1,0},{2,3},{3,2},{4,5},{5,4},{6,7},{7,6},{8,9},{9,8},{10,11... | collective-permute-start | bytes 1179656 | tf_op jit(solution)/shard_map/ppermute | solution.py:27
  92.1 16.2 %collective-permute-done.3.refs_1_ = bf16[1536,256]{1,0:T(8,128)(2,1)S(1)} collective-permute-done((bf16[1536,256]{1,0:T(8,128)(2,1)S(1)}, bf16[1536,256]{1,0:T(8,128)(2,1)S(1)}, u32[]{:S(2)}, u32[]{:S(2)}) %collective-permute-start.3) | collective-permute-done | bytes 786464 | tf_op jit(solution)/shard_map/ppermute | solution.py:27
  108.3 1.1 copy-done.2
  109.4 4.6 %shard_map.47.refs_4_ = bf16[8,144,128]{2,1,0:T(8,128)(2,1)S(1)} custom-call(s32[40]{0:T(128)S(1)} %concatenate.10.info_ref, s32[1536,1]{1,0:T(8,128)S(1)} %copy.16.qid_ref, s32[1,3328]{1,0:T(1,128)S(1)} %broadcast_in_dim.47.kid_ref, bf16[1536,256]{1,0:T(8,128)(2,1)S(1)} %copy-done.2, bf16[1536,256]{1,0:T(8,128)(2,1)S(1)} %get-tuple-element.19.refs_0_, ...), custom_call_target="tpu_custom_call" | custom-call | flops 4294967296 | bytes 4194304 | tf_op jit(solution)/shard_map/pallas_call | solution.py:138
  114.0 1.5 %collective-permute-done.4.refs_3_ = bf16[1536,128]{1,0:T(8,128)(2,1)S(1)} collective-permute-done((bf16[1536,128]{1,0:T(8,128)(2,1)S(1)}, bf16[1536,128]{1,0:T(8,128)(2,1)S(1)}, u32[]{:S(2)}, u32[]{:S(2)}) %collective-permute-start.4) | collective-permute-done | bytes 393248 | tf_op jit(solution)/shard_map/ppermute | solution.py:27
  115.5 5.0 %shard_map.48 = bf16[8,288,128]{2,1,0:T(8,128)(2,1)S(1)} custom-call(s32[40]{0:T(128)S(1)} %concatenate.10.info_ref, s32[1536,1]{1,0:T(8,128)S(1)} %copy.16.qid_ref, s32[1,3328]{1,0:T(1,128)S(1)} %broadcast_in_dim.47.kid_ref, bf16[1536,256]{1,0:T(8,128)(2,1)S(1)} %copy-done.2, bf16[1536,256]{1,0:T(8,128)(2,1)S(1)} %get-tuple-element.19.refs_0_, ...), custom_call_target="tpu_custom_call" | custom-call | flops 4294967296 | bytes 4194304 | tf_op jit(solution)/shard_map/pallas_call | solution.py:138
  120.5 21.6 %all_to_all.11.in_ref = bf16[8,288,128]{2,1,0:T(8,128)(2,1)S(1)} all-to-all(bf16[8,288,128]{2,1,0:T(8,128)(2,1)S(1)} %shard_map.48), channel_id=1, replica_groups=mesh['y'=8,'xl'=2,'core'=2,'z'=8,'xh'=2] {'z'}, dimensions={0} | all-to-all | bytes 1179648 | tf_op jit(solution)/shard_map/all_to_all | solution.py:211
  142.1 2.2 %shard_map.49 = bf16[192,1536]{1,0:T(8,128)(2,1)} custom-call(bf16[8,288,128]{2,1,0:T(8,128)(2,1)S(1)} %all_to_all.11.in_ref), custom_call_target="tpu_custom_call" | custom-call | tf_op jit(solution)/shard_map/pallas_call | solution.py:174
  (13 shorter events, 0.1 us)
Async XLA Ops:
  6.5 35.1 %copy-start.4 = (s32[1,16]{1,0:T(1,128)S(1)}, s32[1,16]{1,0:T(1,128)}, u32[]{:S(2)}) copy-start(s32[1,16]{1,0:T(1,128)} %param.6) | copy-start | bytes 196
  6.5 35.8 %copy-start.3 = (s32[1,3072]{1,0:T(1,128)S(1)}, s32[1,3072]{1,0:T(1,128)}, u32[]{:S(2)}) copy-start(s32[1,3072]{1,0:T(1,128)} %param.5) | copy-start | bytes 36868
  6.5 70.7 %all-gather.2.cloned.1.call-start = ((), (), s32[]{:S(2)}) async-start(), calls=%async_computation.2 | async-start | bytes 5308416 | tf_op jit(solution)/shard_map/all_gather | solution.py:203
  8.2 7.4 %collective-permute-start = (bf16[48,288]{1,0:T(8,128)(2,1)S(1)}, bf16[48,288]{1,0:T(8,128)(2,1)S(1)}, u32[]{:S(2)}, u32[]{:S(2)}) collective-permute-start(bf16[48,288]{1,0:T(8,128)(2,1)S(1)} %reshape.112), channel_id=1, source_target_pairs={{0,1},{1,0},{2,3},{3,2},{4,5},{5,4},{6,7},{7,6},{8,9},{9,8},{10,11... | collective-permute-start | bytes 82952 | tf_op jit(solution)/shard_map/ppermute | solution.py:27
  38.3 11.7 %collective-permute-start.1 = (bf16[8,48,640]{2,1,0:T(8,128)(2,1)S(1)}, bf16[8,48,640]{2,1,0:T(8,128)(2,1)S(1)}, u32[]{:S(2)}, u32[]{:S(2)}) collective-permute-start(bf16[8,48,640]{2,1,0:T(8,128)(2,1)S(1)} %all_to_all.10), channel_id=1, source_target_pairs={{0,32},{32,0},{1,33},{33,1},{2,34},{34,2},{3,35},{35,3},{4,36},{36... | collective-permute-start | bytes 1474568 | tf_op jit(solution)/shard_map/ppermute | solution.py:27
  50.2 4.5 %collective-permute-start.2 = (bf16[8,2,48,640]{3,2,1,0:T(8,128)(2,1)S(1)}, bf16[8,2,48,640]{3,2,1,0:T(8,128)(2,1)S(1)}, u32[]{:S(2)}, u32[]{:S(2)}) collective-permute-start(bf16[8,2,48,640]{3,2,1,0:T(8,128)(2,1)S(1)} %pad_maximum_fusion.1), channel_id=1, source_target_pairs={{0,16},{16,0},{1,17},{17,1},{2,18},{18,2},{3,19},{19,3},{4,20},{20... | collective-permute-start | bytes 2949128 | tf_op jit(solution)/shard_map/ppermute | solution.py:27
  77.2 2.3 %copy-start = (bf16[1536,1536]{1,0:T(8,128)(2,1)S(1)}, bf16[1536,1536]{1,0:T(8,128)(2,1)}, u32[]{:S(2)}) copy-start(bf16[1536,1536]{1,0:T(8,128)(2,1)} %all-gather.2.cloned.1.call-done.x_ref) | copy-start | bytes 14155780
  83.6 0.9 copy-start.1
  84.5 23.8 %collective-permute-start.3 = (bf16[1536,256]{1,0:T(8,128)(2,1)S(1)}, bf16[1536,256]{1,0:T(8,128)(2,1)S(1)}, u32[]{:S(2)}, u32[]{:S(2)}) collective-permute-start(bf16[1536,256]{1,0:T(8,128)(2,1)S(1)} %get-tuple-element.19.refs_0_), channel_id=1, source_target_pairs={{0,1},{1,0},{2,3},{3,2},{4,5},{5,4},{6,7},{7,6},{8,9},{9,8},{10,11... | collective-permute-start | bytes 2359304 | tf_op jit(solution)/shard_map/ppermute | solution.py:27
  88.1 27.4 %collective-permute-start.4 = (bf16[1536,128]{1,0:T(8,128)(2,1)S(1)}, bf16[1536,128]{1,0:T(8,128)(2,1)S(1)}, u32[]{:S(2)}, u32[]{:S(2)}) collective-permute-start(bf16[1536,128]{1,0:T(8,128)(2,1)S(1)} %get-tuple-element.20.refs_2_), channel_id=1, source_target_pairs={{0,1},{1,0},{2,3},{3,2},{4,5},{5,4},{6,7},{7,6},{8,9},{9,8},{10,11... | collective-permute-start | bytes 1179656 | tf_op jit(solution)/shard_map/ppermute | solution.py:27
  108.3 1.1 copy-start.2
Sparse Core Ops, SparseCore 0:
  9.4 67.7 all-gather.1

commit v6 on v5

v6 whole, which is shorter than its diff:
```python
import functools

import jax
import jax.numpy as jnp
from jax import lax
from jax.experimental import pallas as pl
from jax.experimental.pallas import tpu as pltpu
from jax.sharding import Mesh
from jax.sharding import PartitionSpec as P

HEAD = 96
FR = 192
D = 1536
NZ = 8
ROWS = NZ * FR
SEQ = 3072
TILE = 256
MAX_TILES = 8
PAD = SEQ + TILE
AXES = ("y", "xl", "core", "z", "xh")
SIZES = (8, 2, 2, 8, 2)
VMEM = pl.BlockSpec(memory_space=pltpu.VMEM)
SMEM = pl.BlockSpec(memory_space=pltpu.SMEM)


def swap(x, axis):
    return lax.ppermute(x, axis, [(0, 1), (1, 0)])


def both(own, other, index, axis):
    first = jnp.where(index == 0, own, other)
    second = jnp.where(index == 0, other, own)
    return jnp.stack([first, second], axis=axis)


def gather_weights(w, frames):
    flat = jnp.transpose(w, (1, 0, 2)).reshape(w.shape[1], 3 * HEAD)
    heads = both(flat, swap(flat, "xh"), lax.axis_index("xh"), 0)
    q, k, v = (heads[:, :, t * HEAD : (t + 1) * HEAD] for t in range(3))
    shard = jnp.concatenate([k[0], v[0], v[1], k[1], q[0], jnp.zeros_like(q[0, :, :64]), q[1]], axis=1)
    frames, shard = lax.optimization_barrier((frames, shard))
    partner = swap(frames, "xh")
    rows = lax.all_to_all(jnp.broadcast_to(shard[None], (8,) + shard.shape), "y", 0, 0, tiled=True)
    rows, partner = lax.optimization_barrier((rows, partner))
    rows = both(rows, swap(rows, "xl"), lax.axis_index("xl"), 1)
    rows = both(rows, swap(rows, "core"), lax.axis_index("core"), 2)
    return rows.reshape(D, shard.shape[1]), partner


def project_rows(x, w_ref, rows, most_ref, last_ref):
    y = jnp.dot(x, w_ref[:, :384], preferred_element_type=jnp.float32).astype(jnp.bfloat16)
    most_ref[rows, :] = y[:, :256]
    last_ref[rows, :] = y[:, 256:]


def project_near_kernel(own_ref, other_ref, w_ref, *outs):
    x = jnp.concatenate([own_ref[...], other_ref[...]], axis=0)
    project_rows(x, w_ref, slice(0, 2 * FR), *outs)


def project_far_kernel(z_ref, x_ref, w_ref, most_ref, last_ref):
    starts = [pl.multiple_of(lax.rem(z_ref[0] + 1 + i, NZ) * FR, FR) for i in range(7)]
    x = jnp.concatenate([x_ref[pl.ds(start, FR), :] for start in starts], axis=0)
    project_rows(x, w_ref, slice(0, 7 * FR), most_ref, last_ref)


def project_queries_kernel(x_ref, w_ref, q_ref):
    q_ref[...] = jnp.dot(x_ref[...], w_ref[:, 384:], preferred_element_type=jnp.float32).astype(jnp.bfloat16)


def project(kernel, specs, args, rows):
    return pl.pallas_call(
        kernel,
        in_specs=specs,
        out_specs=[VMEM] * 2,
        out_shape=[jax.ShapeDtypeStruct((rows, width), jnp.bfloat16) for width in (256, 128)],
        compiler_params=pltpu.CompilerParams(vmem_limit_bytes=24 << 20),
        cost_estimate=pl.CostEstimate(flops=2 * rows * D * 384, bytes_accessed=rows * D * 4, transcendentals=0),
    )(*args)


def project_near(own, other, w):
    return project(project_near_kernel, [VMEM] * 3, (own, other, w), 2 * FR)


def project_far(z, x, w):
    return project(project_far_kernel, [SMEM, VMEM, VMEM], (z[None], x, w), 7 * FR)


def project_queries(x, w):
    return pl.pallas_call(
        project_queries_kernel,
        in_specs=[VMEM, VMEM],
        out_specs=VMEM,
        out_shape=jax.ShapeDtypeStruct((ROWS, 256), jnp.bfloat16),
        compiler_params=pltpu.CompilerParams(vmem_limit_bytes=24 << 20),
        cost_estimate=pl.CostEstimate(flops=2 * ROWS * D * 256, bytes_accessed=ROWS * D * 3, transcendentals=0),
    )(x, w)


def attend_jobs(jobs, n, kid_ref, kv_ref, key_lane):
    scale = HEAD**-0.5 * 1.4426950408889634
    scores, tops, outs = [], [], []
    for q, qid, first in jobs:
        tiles, top = [], None
        for t in range(n):
            at = pl.multiple_of(first + t * TILE, 128)
            keys = kv_ref[pl.ds(at, TILE), key_lane : key_lane + 128]
            s = lax.dot_general(q, keys, (((1,), (1,)), ((), ())), preferred_element_type=jnp.float32)
            s = jnp.where(qid == kid_ref[:, pl.ds(at, TILE)], s, -1e30)
            tiles.append(s)
            most = jnp.maximum(s[:, :128], s[:, 128:])
            top = most if top is None else jnp.maximum(top, most)
        scores.append(tiles)
        tops.append(jnp.max(top, axis=1, keepdims=True))
    for (q, qid, first), tiles, top in zip(jobs, scores, tops):
        total = acc = None
        for t in range(n):
            at = pl.multiple_of(first + t * TILE, 128)
            p = jnp.exp2((tiles[t] - top) * scale)
            part_sum = p[:, :128] + p[:, 128:]
            out = jnp.dot(p.astype(jnp.bfloat16), kv_ref[pl.ds(at, TILE), :], preferred_element_type=jnp.float32)
            total = part_sum if total is None else total + part_sum
            acc = out if acc is None else acc + out
        outs.append(acc * (1.0 / jnp.sum(total, axis=1, keepdims=True)))
    return outs


def attend_kernel(head, group, info_ref, qid_ref, kid_ref, q_ref, *refs):
    *parts, out_ref, kv_ref = refs
    kv_ref[SEQ:, :] = jnp.zeros((TILE, 256), jnp.bfloat16)
    for s in range(NZ):
        for side in range(2):
            at = pl.ds(pl.multiple_of(info_ref[side * NZ + s] * FR, FR), FR)
            which, i = (side, s) if s < 7 else (2, side)
            rows = slice(i * FR, (i + 1) * FR)
            if head == 0:
                kv_ref[at, :] = parts[which][rows, :]
            else:
                kv_ref[at, :128] = parts[which][rows, 128:]
                kv_ref[at, 128:] = parts[3 + which][rows, :]

    def some(g, _):
        slots = [info_ref[32 + group * g + i] for i in range(group)]
        count = info_ref[24 + slots[-1]]
        jobs = []
        for s in slots:
            rows = pl.ds(pl.multiple_of(s * FR, FR), FR)
            query_rows = pl.ds(pl.multiple_of(info_ref[40 + s] * FR, FR), FR)
            first = jnp.minimum(info_ref[16 + s], PAD - count * TILE)
            jobs.append((q_ref[query_rows, head * 128 : head * 128 + 128], qid_ref[rows, :], first))

        def attend_some(n):
            outs = attend_jobs(jobs, n, kid_ref, kv_ref, head * 128)
            lane = lax.broadcasted_iota(jnp.int32, (FR, 128), 1)
            for s, acc in zip(slots, outs):
                z = info_ref[40 + s]
                if head == 0:
                    out_ref[z] = jnp.where(lane < 64, acc[:, 128:], acc[:, :128]).astype(jnp.bfloat16)
                    continue
                spare = (lane >= 64) & (lane < 96)
                first = jnp.where(spare, pltpu.roll(acc[:, 128:], 64, 1), parts[6][z].astype(jnp.float32))
                out_ref[z, :FR, :] = first.astype(jnp.bfloat16)
                upper, lower = acc[: FR // 2, :128], acc[FR // 2 :, :128]
                both_rows = jnp.where(lane[: FR // 2] < 64, pltpu.roll(lower, 64, 1), upper)
                out_ref[z, FR:, :] = both_rows.astype(jnp.bfloat16)

        for n in range(1, MAX_TILES + 1):
            pl.when(count == n)(functools.partial(attend_some, n))
        return 0

    lax.fori_loop(0, NZ // group, some, 0)


def attend(head, info, qid, kid, *parts, group=2):
    return pl.pallas_call(
        functools.partial(attend_kernel, head, group),
        in_specs=[SMEM, VMEM, VMEM] + [VMEM] * len(parts),
        out_specs=VMEM,
        out_shape=jax.ShapeDtypeStruct((NZ, (FR, FR * 3 // 2)[head], 128), jnp.bfloat16),
        scratch_shapes=[pltpu.VMEM((PAD, 256), jnp.bfloat16)],
        compiler_params=pltpu.CompilerParams(vmem_limit_bytes=28 << 20),
        cost_estimate=pl.CostEstimate(flops=4 << 30, bytes_accessed=4 << 20, transcendentals=2 << 20),
    )(info, qid, kid, *parts)


def unpack_kernel(in_ref, out_ref):
    lane = lax.broadcasted_iota(jnp.int32, (FR, 128), 1)
    for z in range(0, NZ, 2):
        tiles = []
        for i in range(2):
            a = in_ref[z + i, :FR, :].astype(jnp.float32)
            b = in_ref[z + i, FR:, :].astype(jnp.float32)
            tiles.append((pltpu.roll(a, 32, 1), pltpu.roll(a, 96, 1)))
            tiles.append([jnp.concatenate([pltpu.roll(b, by, 1), pltpu.roll(b, by + 64, 1)], axis=0) for by in (32, 96)[i : i + 1]])
        (a32, a96), (b32,), (c32, c96), (d96,) = tiles
        out = (
            jnp.where(lane < 96, a32, b32),
            jnp.where(lane < 32, b32, jnp.where(lane < 64, a96, c96)),
            jnp.where(lane < 32, c96, jnp.where(lane < 96, d96, c32)),
        )
        for i, tile in enumerate(out):
            out_ref[:, z * 192 + i * 128 : z * 192 + (i + 1) * 128] = tile.astype(jnp.bfloat16)


def unpack(packed):
    return pl.pallas_call(
        unpack_kernel,
        in_specs=[VMEM],
        out_specs=VMEM,
        out_shape=jax.ShapeDtypeStruct((FR, D), jnp.bfloat16),
        compiler_params=pltpu.CompilerParams(vmem_limit_bytes=8 << 20),
    )(packed)


def plan(ids, order, z, xh):
    blocks = ids.reshape(16, FR)
    zs = (z + 1 + jnp.arange(NZ, dtype=jnp.int32)) % NZ
    places = jnp.take(order.reshape(NZ, 2), zs, axis=0)
    own = jnp.where(xh == 0, places[:, 0], places[:, 1])
    other = jnp.where(xh == 0, places[:, 1], places[:, 0])
    qid = jnp.take(blocks, own, axis=0)
    first = jnp.sum(ids[None, :] < qid[:, :1], axis=1, dtype=jnp.int32)
    last = jnp.sum(ids[None, :] <= qid[:, FR - 1 :], axis=1, dtype=jnp.int32)
    first = first // 128 * 128
    count = (last - first + TILE - 1) // TILE
    i = jnp.arange(NZ, dtype=jnp.int32)
    ahead = (count[None, :] < count[:, None]) | ((count[None, :] == count[:, None]) & (i[None, :] < i[:, None]))
    rank = jnp.sum(ahead, axis=1, dtype=jnp.int32)
    ranked = jnp.sum(jnp.where(rank[:, None] == i[None, :], i[:, None], 0), axis=0, dtype=jnp.int32)
    info = jnp.concatenate([own, other, first, count, ranked, zs])
    kid = jnp.concatenate([ids, jnp.full((TILE,), -1, jnp.int32)])[None]
    return info, qid.reshape(ROWS, 1), kid


def body(frames, seg_ids, assign, w_qkv):
    z, xh = lax.axis_index("z").astype(jnp.int32), lax.axis_index("xh")
    x = lax.all_gather(frames, "z", axis=0, tiled=True)
    w, partner = gather_weights(w_qkv, frames)
    near_most, near_last = project_near(frames, partner, w)
    info, qid, kid = plan(seg_ids[0], assign[0], z, xh)
    x, info, qid, kid, near_last = lax.optimization_barrier((x, info, qid, kid, near_last))
    most, last = project_far(z, x, w)
    other_most, other_last = swap(most, "xh"), swap(last, "xh")
    mosts, lasts = (most, other_most, near_most), (last, other_last, near_last)
    q = project_queries(x, w)
    packed = attend(0, info, qid, kid, q, *mosts)
    packed = attend(1, info, qid, kid, q, *mosts, *lasts, packed)
    return unpack(lax.all_to_all(packed, "z", 0, 0, tiled=True))


def solution(mesh):
    fine = Mesh(mesh.devices.reshape(SIZES), AXES)
    dp, ctx = AXES[:3], AXES[3:]
    return jax.shard_map(
        body,
        mesh=fine,
        in_specs=(P(AXES, None), P(dp, None), P(dp, None), P(None, dp, ctx)),
        out_specs=P(AXES, None),
        check_vma=False,
    )
```

time: 152 us -> 148 us (0.974)
  blocking collectives: 44.1 us -> 22.3 us
  starting transfers between devices: 15.3 us -> 25.9 us
  waiting for transfers between devices: 51.9 us -> 54.5 us
  local copies, waits for them, and re-layouts: 7.36 us -> 9 us
  Pallas kernels: 15.8 us -> 17.4 us
    all_to_all x1 -> x0, blocking collectives: 22.5 us -> none  [gather_weights(): lax.all_to_all(jnp.broadcast_to(shard[None], (8,) + shard.shape), 'y', 0,...]
    ppermute x5 -> x6, waiting for transfers between devices: 29.1 us -> 37 us  [swap(): return lax.ppermute(x, axis, [(0, 1), (1, 0)])]
    all_to_all x0 -> x1, starting transfers between devices: none -> 7.1 us  [gather_weights(): lax.all_to_all(jnp.broadcast_to(shard[None], (8,) + shard.shape), 'y', 0,...]
    all_gather x1, waiting for transfers between devices: 22.1 us -> 16.8 us  [body(): x = lax.all_gather(frames, 'z', axis=0, tiled=True)]
    ppermute x5 -> x6, starting transfers between devices: 15.3 us -> 18.8 us  [swap(): return lax.ppermute(x, axis, [(0, 1), (1, 0)])]
    pallas_call x1 -> x3, Pallas kernels: 4 us -> 5.32 us  [the longest x2 3.93 us: project(): pl.pallas_call(kernel, in_specs=specs, out_specs=[VMEM] * 2, out_shape=[j...]
  transfers between devices with their start and end apart: 6 -> 8, of which waited for: 6 -> 7; matrix products, arithmetic and copies ran while one was open for 4% -> 6% of each run, Pallas kernels for 3% -> 5%
where the time goes in v6:
time: 148 us; the launch traced here: 147 us
  waiting for transfers between devices  54.5 us (37%)
  starting transfers between devices  25.9 us (18%)
  blocking collectives  22.3 us (15%)
  Pallas kernels  17.4 us (12%)
  between operations  13.6 us (9%)
  local copies, waits for them, and re-layouts  9 us (6%)
  other arithmetic  4.33 us (3%)
    ppermute x6, waiting for transfers between devices, swap(): return lax.ppermute(x, axis, [(0, 1), (1, 0)])  37 us
    all_to_all x1, blocking collectives, body(): return unpack(lax.all_to_all(packed, 'z', 0, 0, tiled=True))  22.3 us
    ppermute x6, starting transfers between devices, swap(): return lax.ppermute(x, axis, [(0, 1), (1, 0)])  18.8 us
    all_gather x1, waiting for transfers between devices, body(): x = lax.all_gather(frames, 'z', axis=0, tiled=True)  16.8 us
    pallas_call x2, Pallas kernels, attend(): pl.pallas_call(functools.partial(attend_kernel, head, group), in_specs=[S...  10.9 us
    all_to_all x1, starting transfers between devices, gather_weights(): lax.all_to_all(jnp.broadcast_to(shard[None], (8,) + shard.shape), 'y', 0,...  7.1 us
    unnamed x11, local copies, waits for them, and re-layouts  5.16 us
    pallas_call x2, Pallas kernels, project(): pl.pallas_call(kernel, in_specs=specs, out_specs=[VMEM] * 2, out_shape=[j...  3.93 us
  transfers between devices with their start and end apart: 8, of which 7 were waited for; matrix products, arithmetic and copies ran while one was open for 6% of the time, Pallas kernels for 5%

profile of v6, /device:TPU:6, one launch (start us, length us, event | category | flops | bytes accessed | tf_op | source)
XLA Modules:
  0.0 147.1 jit_solution(13708334999546983941)
XLA Ops:
  6.5 0.7 all-gather.2.cloned.1.call-update
  7.3 0.8 copy.12
  8.1 0.1 reshape.166
  8.2 3.3 %collective-permute-start = (bf16[48,288]{1,0:T(8,128)(2,1)S(1)}, bf16[48,288]{1,0:T(8,128)(2,1)S(1)}, u32[]{:S(2)}, u32[]{:S(2)}) collective-permute-start(bf16[48,288]{1,0:T(8,128)(2,1)S(1)} %reshape.166), channel_id=1, source_target_pairs={{0,1},{1,0},{2,3},{3,2},{4,5},{5,4},{6,7},{7,6},{8,9},{9,8},{10,11... | collective-permute-start | bytes 82952 | tf_op jit(solution)/shard_map/ppermute | solution.py:27
  11.5 4.0 %collective-permute-done = bf16[48,288]{1,0:T(8,128)(2,1)S(1)} collective-permute-done((bf16[48,288]{1,0:T(8,128)(2,1)S(1)}, bf16[48,288]{1,0:T(8,128)(2,1)S(1)}, u32[]{:S(2)}, u32[]{:S(2)}) %collective-permute-start) | collective-permute-done | bytes 27680 | tf_op jit(solution)/shard_map/ppermute | solution.py:27
  15.5 0.1 slice_bitcast_fusion
  15.6 0.1 concatenate.11
  15.8 0.8 broadcast_in_dim.57
  16.6 7.1 %all-to-all-start = ((bf16[8,48,640]{2,1,0:T(8,128)(2,1)}), bf16[8,48,640]{2,1,0:T(8,128)(2,1)S(1)}, u32[]{:S(2)}, u32[]{:S(2)}) async-start(bf16[8,48,640]{2,1,0:T(8,128)(2,1)} %broadcast_in_dim.57), calls=%async_computation | async-start | bytes 983040 | tf_op jit(solution)/shard_map/all_to_all | solution.py:43
  23.7 3.3 %collective-permute-start.1 = (bf16[192,1536]{1,0:T(8,128)(2,1)S(1)}, bf16[192,1536]{1,0:T(8,128)(2,1)S(1)}, u32[]{:S(2)}, u32[]{:S(2)}) collective-permute-start(bf16[192,1536]{1,0:T(8,128)(2,1)S(1)} %copy-done.2), channel_id=1, source_target_pairs={{0,1},{1,0},{2,3},{3,2},{4,5},{5,4},{6,7},{7,6},{8,9},{9,8},{10,11... | collective-permute-start | bytes 1769480 | tf_op jit(solution)/shard_map/ppermute | solution.py:27
  27.0 0.5 broadcast.309
  27.5 0.6 reduce.19
  28.1 0.1 fusion.1
  28.3 0.6 gather_fusion
  28.9 11.9 %collective-permute-done.1.other_ref = bf16[192,1536]{1,0:T(8,128)(2,1)S(1)} collective-permute-done((bf16[192,1536]{1,0:T(8,128)(2,1)S(1)}, bf16[192,1536]{1,0:T(8,128)(2,1)S(1)}, u32[]{:S(2)}, u32[]{:S(2)}) %collective-permute-start.1) | collective-permute-done | bytes 589856 | tf_op jit(solution)/shard_map/ppermute | solution.py:27
  40.7 2.7 %collective-permute-start.2 = (bf16[8,48,640]{2,1,0:T(8,128)(2,1)S(1)}, bf16[8,48,640]{2,1,0:T(8,128)(2,1)S(1)}, u32[]{:S(2)}, u32[]{:S(2)}) collective-permute-start(bf16[8,48,640]{2,1,0:T(8,128)(2,1)S(1)} %all-to-all-done), channel_id=1, source_target_pairs={{0,32},{32,0},{1,33},{33,1},{2,34},{34,2},{3,35},{35,3},{4,36},{36... | collective-permute-start | bytes 1474568 | tf_op jit(solution)/shard_map/ppermute | solution.py:27
  43.5 0.6 reduce.20
  44.2 0.2 and_reduce_fusion
  44.4 0.1 fusion.7
  44.5 0.6 gather_fusion.1
  45.1 8.1 %collective-permute-done.2 = bf16[8,48,640]{2,1,0:T(8,128)(2,1)S(1)} collective-permute-done((bf16[8,48,640]{2,1,0:T(8,128)(2,1)S(1)}, bf16[8,48,640]{2,1,0:T(8,128)(2,1)S(1)}, u32[]{:S(2)}, u32[]{:S(2)}) %collective-permute-start.2) | collective-permute-done | bytes 491552 | tf_op jit(solution)/shard_map/ppermute | solution.py:27
  53.2 0.1 select_bitcast_fusion.3
  53.3 0.1 pad_maximum_fusion.1
  53.4 1.9 %collective-permute-start.3 = (bf16[8,2,48,640]{3,2,1,0:T(8,128)(2,1)S(1)}, bf16[8,2,48,640]{3,2,1,0:T(8,128)(2,1)}, u32[]{:S(2)}, u32[]{:S(2)}) collective-permute-start(bf16[8,2,48,640]{3,2,1,0:T(8,128)(2,1)S(1)} %pad_maximum_fusion.1), channel_id=1, source_target_pairs={{0,16},{16,0},{1,17},{17,1},{2,18},{18,2},{3,19},{19,3},{4,20},{20... | collective-permute-start | bytes 2949128 | tf_op jit(solution)/shard_map/ppermute | solution.py:27
  55.4 0.1 select_n.156
  55.5 0.2 slice_reduce_fusion
  55.7 0.2 select_reduce_fusion.1
  55.9 0.2 convert_reduce_fusion
  56.2 0.2 convert_reduce_fusion.2
  56.4 0.1 select_reduce_fusion
  56.5 1.5 %collective-permute-done.3 = bf16[8,2,48,640]{3,2,1,0:T(8,128)(2,1)} collective-permute-done((bf16[8,2,48,640]{3,2,1,0:T(8,128)(2,1)S(1)}, bf16[8,2,48,640]{3,2,1,0:T(8,128)(2,1)}, u32[]{:S(2)}, u32[]{:S(2)}) %collective-permute-start.3) | collective-permute-done | bytes 983072 | tf_op jit(solution)/shard_map/ppermute | solution.py:27
  58.0 1.4 select_bitcast_fusion.1
  59.4 0.2 pad_maximum_fusion
  59.6 0.8 shard_map.46
  60.4 16.8 %all-gather.2.cloned.1.call-done.x_ref = bf16[1536,1536]{1,0:T(8,128)(2,1)} async-done(((bf16[192,1536]{1,0:T(8,128)(2,1)}), bf16[1536,1536]{1,0:T(8,128)(2,1)}) %all-gather.2.cloned.1.call-update) | async-done | bytes 4718608 | tf_op jit(solution)/shard_map/all_gather | solution.py:238
  77.2 2.3 %copy-done = bf16[1536,1536]{1,0:T(8,128)(2,1)S(1)} copy-done((bf16[1536,1536]{1,0:T(8,128)(2,1)S(1)}, bf16[1536,1536]{1,0:T(8,128)(2,1)}, u32[]{:S(2)}) %copy-start) | copy-done | bytes 4718616
  79.6 3.2 %shard_map.48 = (bf16[1344,256]{1,0:T(8,128)(2,1)}, bf16[1344,128]{1,0:T(8,128)(2,1)S(1)}) custom-call(s32[1]{0:T(128)} %bitcast.17.z_ref, bf16[1536,1536]{1,0:T(8,128)(2,1)S(1)} %copy-done, bf16[1536,640]{1,0:T(8,128)(2,1)S(1)} %bitcast.33), custom_call_target="tpu_custom_call" | custom-call | flops 1585446912 | bytes 8257536 | tf_op jit(solution)/shard_map/pallas_call | solution.py:72
  82.7 3.3 %collective-permute-start.4 = (bf16[1344,256]{1,0:T(8,128)(2,1)}, bf16[1344,256]{1,0:T(8,128)(2,1)}, u32[]{:S(2)}, u32[]{:S(2)}) collective-permute-start(bf16[1344,256]{1,0:T(8,128)(2,1)} %get-tuple-element.27.refs_0_), channel_id=1, source_target_pairs={{0,1},{1,0},{2,3},{3,2},{4,5},{5,4},{6,7},{7,6},{8,9},{9,8},{10,11... | collective-permute-start | bytes 2064392 | tf_op jit(solution)/shard_map/ppermute | solution.py:27
  86.1 0.3 copy.16.qid_ref
  86.4 4.2 %collective-permute-start.5 = (bf16[1344,128]{1,0:T(8,128)(2,1)S(1)}, bf16[1344,128]{1,0:T(8,128)(2,1)S(1)}, u32[]{:S(2)}, u32[]{:S(2)}) collective-permute-start(bf16[1344,128]{1,0:T(8,128)(2,1)S(1)} %get-tuple-element.29.refs_3_), channel_id=1, source_target_pairs={{0,1},{1,0},{2,3},{3,2},{4,5},{5,4},{6,7},{7,6},{8,9},{9,8},{10,11... | collective-permute-start | bytes 1032200 | tf_op jit(solution)/shard_map/ppermute | solution.py:27
  90.6 2.3 %copy-done.1 = bf16[1536,1536]{1,0:T(8,128)(2,1)S(1)} copy-done((bf16[1536,1536]{1,0:T(8,128)(2,1)S(1)}, bf16[1536,1536]{1,0:T(8,128)(2,1)}, u32[]{:S(2)}) %copy-start.1) | copy-done | bytes 4718616
  92.9 1.4 shard_map.47.q_ref
  94.3 10.5 %collective-permute-done.4.refs_1_ = bf16[1344,256]{1,0:T(8,128)(2,1)} collective-permute-done((bf16[1344,256]{1,0:T(8,128)(2,1)}, bf16[1344,256]{1,0:T(8,128)(2,1)}, u32[]{:S(2)}, u32[]{:S(2)}) %collective-permute-start.4) | collective-permute-done | bytes 688160 | tf_op jit(solution)/shard_map/ppermute | solution.py:27
  104.8 5.1 %shard_map.49.refs_6_ = bf16[8,192,128]{2,1,0:T(8,128)(2,1)S(1)} custom-call(s32[48]{0:T(128)S(1)} %concatenate.9.info_ref, s32[1536,1]{1,0:T(8,128)S(1)} %copy.16.qid_ref, s32[1,3328]{1,0:T(1,128)S(1)} %broadcast_in_dim.55.kid_ref, bf16[1536,256]{1,0:T(8,128)(2,1)S(1)} %shard_map.47.q_ref, bf16[1344,256]{1,0:T(8,128)(2,1)} %get-tuple-element.27.refs_0_, ...), custom_call_target="tpu_custom_call" | custom-call | flops 4294967296 | bytes 4194304 | tf_op jit(solution)/shard_map/pallas_call | solution.py:176
  109.8 1.1 collective-permute-done.5.refs_4_
  110.9 5.8 %shard_map.50 = bf16[8,288,128]{2,1,0:T(8,128)(2,1)S(1)} custom-call(s32[48]{0:T(128)S(1)} %concatenate.9.info_ref, s32[1536,1]{1,0:T(8,128)S(1)} %copy.16.qid_ref, s32[1,3328]{1,0:T(1,128)S(1)} %broadcast_in_dim.55.kid_ref, bf16[1536,256]{1,0:T(8,128)(2,1)S(1)} %shard_map.47.q_ref, bf16[1344,256]{1,0:T(8,128)(2,1)} %get-tuple-element.27.refs_0_, ...), custom_call_target="tpu_custom_call" | custom-call | flops 4294967296 | bytes 4194304 | tf_op jit(solution)/shard_map/pallas_call | solution.py:176
  116.7 22.3 %all_to_all.10.in_ref = bf16[8,288,128]{2,1,0:T(8,128)(2,1)S(1)} all-to-all(bf16[8,288,128]{2,1,0:T(8,128)(2,1)S(1)} %shard_map.50), channel_id=1, replica_groups=mesh['y'=8,'xl'=2,'core'=2,'z'=8,'xh'=2] {'z'}, dimensions={0} | all-to-all | bytes 1179648 | tf_op jit(solution)/shard_map/all_to_all | solution.py:249
  139.0 1.2 shard_map.51
  (24 shorter events, 0.5 us)
Async XLA Ops:
  6.5 17.1 %copy-start.2 = (bf16[192,1536]{1,0:T(8,128)(2,1)S(1)}, bf16[192,1536]{1,0:T(8,128)(2,1)}, u32[]{:S(2)}) copy-start(bf16[192,1536]{1,0:T(8,128)(2,1)} %own_ref.1) | copy-start | bytes 1769476
  6.5 21.0 %copy-start.4 = (s32[1,16]{1,0:T(1,128)S(1)}, s32[1,16]{1,0:T(1,128)}, u32[]{:S(2)}) copy-start(s32[1,16]{1,0:T(1,128)} %param.6) | copy-start | bytes 196
  6.5 37.0 %copy-start.3 = (s32[1,3072]{1,0:T(1,128)S(1)}, s32[1,3072]{1,0:T(1,128)}, u32[]{:S(2)}) copy-start(s32[1,3072]{1,0:T(1,128)} %param.5) | copy-start | bytes 36868
  6.5 70.7 %all-gather.2.cloned.1.call-start = ((), (), s32[]{:S(2)}) async-start(), calls=%async_computation.2 | async-start | bytes 5308416 | tf_op jit(solution)/shard_map/all_gather | solution.py:238
  8.2 7.4 %collective-permute-start = (bf16[48,288]{1,0:T(8,128)(2,1)S(1)}, bf16[48,288]{1,0:T(8,128)(2,1)S(1)}, u32[]{:S(2)}, u32[]{:S(2)}) collective-permute-start(bf16[48,288]{1,0:T(8,128)(2,1)S(1)} %reshape.166), channel_id=1, source_target_pairs={{0,1},{1,0},{2,3},{3,2},{4,5},{5,4},{6,7},{7,6},{8,9},{9,8},{10,11... | collective-permute-start | bytes 82952 | tf_op jit(solution)/shard_map/ppermute | solution.py:27
  16.6 24.1 %all-to-all-start = ((bf16[8,48,640]{2,1,0:T(8,128)(2,1)}), bf16[8,48,640]{2,1,0:T(8,128)(2,1)S(1)}, u32[]{:S(2)}, u32[]{:S(2)}) async-start(bf16[8,48,640]{2,1,0:T(8,128)(2,1)} %broadcast_in_dim.57), calls=%async_computation | async-start | bytes 983040 | tf_op jit(solution)/shard_map/all_to_all | solution.py:43
  23.7 17.0 %collective-permute-start.1 = (bf16[192,1536]{1,0:T(8,128)(2,1)S(1)}, bf16[192,1536]{1,0:T(8,128)(2,1)S(1)}, u32[]{:S(2)}, u32[]{:S(2)}) collective-permute-start(bf16[192,1536]{1,0:T(8,128)(2,1)S(1)} %copy-done.2), channel_id=1, source_target_pairs={{0,1},{1,0},{2,3},{3,2},{4,5},{5,4},{6,7},{7,6},{8,9},{9,8},{10,11... | collective-permute-start | bytes 1769480 | tf_op jit(solution)/shard_map/ppermute | solution.py:27
  40.7 12.5 %collective-permute-start.2 = (bf16[8,48,640]{2,1,0:T(8,128)(2,1)S(1)}, bf16[8,48,640]{2,1,0:T(8,128)(2,1)S(1)}, u32[]{:S(2)}, u32[]{:S(2)}) collective-permute-start(bf16[8,48,640]{2,1,0:T(8,128)(2,1)S(1)} %all-to-all-done), channel_id=1, source_target_pairs={{0,32},{32,0},{1,33},{33,1},{2,34},{34,2},{3,35},{35,3},{4,36},{36... | collective-permute-start | bytes 1474568 | tf_op jit(solution)/shard_map/ppermute | solution.py:27
  53.4 4.6 %collective-permute-start.3 = (bf16[8,2,48,640]{3,2,1,0:T(8,128)(2,1)S(1)}, bf16[8,2,48,640]{3,2,1,0:T(8,128)(2,1)}, u32[]{:S(2)}, u32[]{:S(2)}) collective-permute-start(bf16[8,2,48,640]{3,2,1,0:T(8,128)(2,1)S(1)} %pad_maximum_fusion.1), channel_id=1, source_target_pairs={{0,16},{16,0},{1,17},{17,1},{2,18},{18,2},{3,19},{19,3},{4,20},{20... | collective-permute-start | bytes 2949128 | tf_op jit(solution)/shard_map/ppermute | solution.py:27
  77.2 2.3 %copy-start = (bf16[1536,1536]{1,0:T(8,128)(2,1)S(1)}, bf16[1536,1536]{1,0:T(8,128)(2,1)}, u32[]{:S(2)}) copy-start(bf16[1536,1536]{1,0:T(8,128)(2,1)} %all-gather.2.cloned.1.call-done.x_ref) | copy-start | bytes 14155780
  82.7 22.0 %collective-permute-start.4 = (bf16[1344,256]{1,0:T(8,128)(2,1)}, bf16[1344,256]{1,0:T(8,128)(2,1)}, u32[]{:S(2)}, u32[]{:S(2)}) collective-permute-start(bf16[1344,256]{1,0:T(8,128)(2,1)} %get-tuple-element.27.refs_0_), channel_id=1, source_target_pairs={{0,1},{1,0},{2,3},{3,2},{4,5},{5,4},{6,7},{7,6},{8,9},{9,8},{10,11... | collective-permute-start | bytes 2064392 | tf_op jit(solution)/shard_map/ppermute | solution.py:27
  86.4 24.5 %collective-permute-start.5 = (bf16[1344,128]{1,0:T(8,128)(2,1)S(1)}, bf16[1344,128]{1,0:T(8,128)(2,1)S(1)}, u32[]{:S(2)}, u32[]{:S(2)}) collective-permute-start(bf16[1344,128]{1,0:T(8,128)(2,1)S(1)} %get-tuple-element.29.refs_3_), channel_id=1, source_target_pairs={{0,1},{1,0},{2,3},{3,2},{4,5},{5,4},{6,7},{7,6},{8,9},{9,8},{10,11... | collective-permute-start | bytes 1032200 | tf_op jit(solution)/shard_map/ppermute | solution.py:27
  90.6 2.3 %copy-start.1 = (bf16[1536,1536]{1,0:T(8,128)(2,1)S(1)}, bf16[1536,1536]{1,0:T(8,128)(2,1)}, u32[]{:S(2)}) copy-start(bf16[1536,1536]{1,0:T(8,128)(2,1)} %all-gather.2.cloned.1.call-done.x_ref) | copy-start | bytes 14155780
Sparse Core Ops, SparseCore 0:
  9.4 67.7 all-gather.1

commit v7 on v6

--- a/solution.py
+++ b/solution.py
@@ -47,55 +47,56 @@
     return rows.reshape(D, shard.shape[1]), partner
 
 
-def project_rows(x, w_ref, rows, most_ref, last_ref):
-    y = jnp.dot(x, w_ref[:, :384], preferred_element_type=jnp.float32).astype(jnp.bfloat16)
-    most_ref[rows, :] = y[:, :256]
-    last_ref[rows, :] = y[:, 256:]
-
-
-def project_near_kernel(own_ref, other_ref, w_ref, *outs):
-    x = jnp.concatenate([own_ref[...], other_ref[...]], axis=0)
-    project_rows(x, w_ref, slice(0, 2 * FR), *outs)
-
-
-def project_far_kernel(z_ref, x_ref, w_ref, most_ref, last_ref):
+def project_near_kernel(x_ref, w_ref, most_ref, last_ref):
+    y = jnp.dot(x_ref[...], w_ref[:, :384], preferred_element_type=jnp.float32).astype(jnp.bfloat16)
+    most_ref[...] = y[:, :256]
+    last_ref[...] = y[:, 256:]
+
+
+def project_wires_kernel(z_ref, x_ref, w_ref, first_ref, second_ref):
     starts = [pl.multiple_of(lax.rem(z_ref[0] + 1 + i, NZ) * FR, FR) for i in range(7)]
     x = jnp.concatenate([x_ref[pl.ds(start, FR), :] for start in starts], axis=0)
-    project_rows(x, w_ref, slice(0, 7 * FR), most_ref, last_ref)
-
-
-def project_queries_kernel(x_ref, w_ref, q_ref):
-    q_ref[...] = jnp.dot(x_ref[...], w_ref[:, 384:], preferred_element_type=jnp.float32).astype(jnp.bfloat16)
-
-
-def project(kernel, specs, args, rows):
+    y = jnp.dot(x, w_ref[:, :384], preferred_element_type=jnp.float32)
+    half = lax.broadcasted_iota(jnp.int32, (FR // 2, 128), 1) < 64
+    for b in range(7):
+        block = y[b * FR : (b + 1) * FR]
+        first_ref[b, :FR, :] = block[:, :128].astype(jnp.bfloat16)
+        second_ref[b, :FR, :] = block[:, 256:].astype(jnp.bfloat16)
+        upper, turned = block[: FR // 2, 128:256], pltpu.roll(block[FR // 2 :, 128:256], 64, 1)
+        first_ref[b, FR:, :] = jnp.where(half, upper, turned).astype(jnp.bfloat16)
+        second_ref[b, FR:, :] = jnp.where(half, turned, upper).astype(jnp.bfloat16)
+
+
+def project_own_kernel(x_ref, w_ref, most_ref, last_ref, q_ref):
+    y = jnp.dot(x_ref[...], w_ref[...], preferred_element_type=jnp.float32).astype(jnp.bfloat16)
+    most_ref[...] = y[:, :256]
+    last_ref[...] = y[:, 256:384]
+    q_ref[...] = y[:, 384:]
+
+
+def project(kernel, rows, columns, shapes, *args):
     return pl.pallas_call(
         kernel,
-        in_specs=specs,
-        out_specs=[VMEM] * 2,
-        out_shape=[jax.ShapeDtypeStruct((rows, width), jnp.bfloat16) for width in (256, 128)],
-        compiler_params=pltpu.CompilerParams(vmem_limit_bytes=24 << 20),
-        cost_estimate=pl.CostEstimate(flops=2 * rows * D * 384, bytes_accessed=rows * D * 4, transcendentals=0),
+        in_specs=[SMEM] * (len(args) - 2) + [VMEM] * 2,
+        out_specs=[VMEM] * len(shapes),
+        out_shape=[jax.ShapeDtypeStruct(shape, jnp.bfloat16) for shape in shapes],
+        compiler_params=pltpu.CompilerParams(vmem_limit_bytes=16 << 20),
+        cost_estimate=pl.CostEstimate(
+            flops=2 * rows * D * columns, bytes_accessed=rows * D * 4, transcendentals=0
+        ),
     )(*args)
 
 
-def project_near(own, other, w):
-    return project(project_near_kernel, [VMEM] * 3, (own, other, w), 2 * FR)
-
-
-def project_far(z, x, w):
-    return project(project_far_kernel, [SMEM, VMEM, VMEM], (z[None], x, w), 7 * FR)
-
-
-def project_queries(x, w):
-    return pl.pallas_call(
-        project_queries_kernel,
-        in_specs=[VMEM, VMEM],
-        out_specs=VMEM,
-        out_shape=jax.ShapeDtypeStruct((ROWS, 256), jnp.bfloat16),
-        compiler_params=pltpu.CompilerParams(vmem_limit_bytes=24 << 20),
-        cost_estimate=pl.CostEstimate(flops=2 * ROWS * D * 256, bytes_accessed=ROWS * D * 3, transcendentals=0),
-    )(x, w)
+def project_near(x, w):
+    return project(project_near_kernel, FR, 384, [(FR, 256), (FR, 128)], x, w)
+
+
+def project_wires(z, x, w):
+    return project(project_wires_kernel, 7 * FR, 384, [(7, FR * 3 // 2, 128)] * 2, z[None], x, w)
+
+
+def project_own(x, w):
+    return project(project_own_kernel, ROWS, 640, [(ROWS, 256), (ROWS, 128), (ROWS, 256)], x, w)
 
 
 def attend_jobs(jobs, n, kid_ref, kv_ref, key_lane):
@@ -129,16 +130,27 @@
 def attend_kernel(head, group, info_ref, qid_ref, kid_ref, q_ref, *refs):
     *parts, out_ref, kv_ref = refs
     kv_ref[SEQ:, :] = jnp.zeros((TILE, 256), jnp.bfloat16)
+    whole, shared = (slice(0, 128), slice(128, 256)) if head == 0 else (slice(128, 256), slice(0, 128))
+
+    def keep(place, most, last, start):
+        at, rows = (pl.ds(pl.multiple_of(i, FR), FR) for i in (place * FR, start))
+        if head == 0:
+            kv_ref[at, :] = most[rows, :]
+        else:
+            kv_ref[at, :128] = most[rows, 128:]
+            kv_ref[at, 128:] = last[rows, :]
+
+    wire_ref, most_ref, near_most_ref, last_ref, near_last_ref, packed_ref = parts if head else (*parts, None, None, None)
     for s in range(NZ):
-        for side in range(2):
-            at = pl.ds(pl.multiple_of(info_ref[side * NZ + s] * FR, FR), FR)
-            which, i = (side, s) if s < 7 else (2, side)
-            rows = slice(i * FR, (i + 1) * FR)
-            if head == 0:
-                kv_ref[at, :] = parts[which][rows, :]
-            else:
-                kv_ref[at, :128] = parts[which][rows, 128:]
-                kv_ref[at, 128:] = parts[3 + which][rows, :]
+        keep(info_ref[s], most_ref, last_ref, info_ref[40 + s] * FR)
+    keep(info_ref[NZ + 7], near_most_ref, near_last_ref, 0)
+    for s in range(7):
+        place = info_ref[NZ + s] * FR
+        packed = wire_ref[s, FR:, :]
+        kv_ref[pl.ds(pl.multiple_of(place, FR), FR), whole] = wire_ref[s, :FR, :]
+        kv_ref[pl.ds(pl.multiple_of(place, 96), 96), shared] = packed
+        turned = pltpu.roll(packed.astype(jnp.float32), 64, 1).astype(jnp.bfloat16)
+        kv_ref[pl.ds(pl.multiple_of(place + 96, 96), 96), shared] = turned
 
     def some(g, _):
         slots = [info_ref[32 + group * g + i] for i in range(group)]
@@ -159,7 +171,7 @@
                     out_ref[z] = jnp.where(lane < 64, acc[:, 128:], acc[:, :128]).astype(jnp.bfloat16)
                     continue
                 spare = (lane >= 64) & (lane < 96)
-                first = jnp.where(spare, pltpu.roll(acc[:, 128:], 64, 1), parts[6][z].astype(jnp.float32))
+                first = jnp.where(spare, pltpu.roll(acc[:, 128:], 64, 1), packed_ref[z].astype(jnp.float32))
                 out_ref[z, :FR, :] = first.astype(jnp.bfloat16)
                 upper, lower = acc[: FR // 2, :128], acc[FR // 2 :, :128]
                 both_rows = jnp.where(lane[: FR // 2] < 64, pltpu.roll(lower, 64, 1), upper)
@@ -179,7 +191,7 @@
         out_specs=VMEM,
         out_shape=jax.ShapeDtypeStruct((NZ, (FR, FR * 3 // 2)[head], 128), jnp.bfloat16),
         scratch_shapes=[pltpu.VMEM((PAD, 256), jnp.bfloat16)],
-        compiler_params=pltpu.CompilerParams(vmem_limit_bytes=28 << 20),
+        compiler_params=pltpu.CompilerParams(vmem_limit_bytes=14 << 20),
         cost_estimate=pl.CostEstimate(flops=4 << 30, bytes_accessed=4 << 20, transcendentals=2 << 20),
     )(info, qid, kid, *parts)
 
@@ -237,15 +249,14 @@
     z, xh = lax.axis_index("z").astype(jnp.int32), lax.axis_index("xh")
     x = lax.all_gather(frames, "z", axis=0, tiled=True)
     w, partner = gather_weights(w_qkv, frames)
-    near_most, near_last = project_near(frames, partner, w)
+    near_most, near_last = project_near(partner, w)
     info, qid, kid = plan(seg_ids[0], assign[0], z, xh)
     x, info, qid, kid, near_last = lax.optimization_barrier((x, info, qid, kid, near_last))
-    most, last = project_far(z, x, w)
-    other_most, other_last = swap(most, "xh"), swap(last, "xh")
-    mosts, lasts = (most, other_most, near_most), (last, other_last, near_last)
-    q = project_queries(x, w)
-    packed = attend(0, info, qid, kid, q, *mosts)
-    packed = attend(1, info, qid, kid, q, *mosts, *lasts, packed)
+    wire0, wire1 = project_wires(z, x, w)
+    other0, other1 = swap(wire0, "xh"), swap(wire1, "xh")
+    most, last, q = project_own(x, w)
+    packed = attend(0, info, qid, kid, q, other0, most, near_most)
+    packed = attend(1, info, qid, kid, q, other1, most, near_most, last, near_last, packed)
     return unpack(lax.all_to_all(packed, "z", 0, 0, tiled=True))
 
 

time: 148 us -> 147 us (level)
  waiting for transfers between devices: 54.5 us -> 50 us
  local copies, waits for them, and re-layouts: 9 us -> 11.5 us
    ppermute x6, waiting for transfers between devices: 37 us -> 32.2 us  [swap(): return lax.ppermute(x, axis, [(0, 1), (1, 0)])]
    unnamed x11 -> x21, local copies, waits for them, and re-layouts: 5.16 us -> 7.63 us
    pallas_call x3, Pallas kernels: 5.32 us -> 7.47 us  [project(): pl.pallas_call(kernel, in_specs=[SMEM] * (len(args) - 2) + [VMEM] * 2, ou...]
  transfers between devices with their start and end apart: 8 -> 8, of which waited for: 7 -> 7; matrix products, arithmetic and copies ran while one was open for 6% -> 6% of each run, Pallas kernels for 5% -> 6%
where the time goes in v7:
time: 147 us; the launch traced here: 146 us
  waiting for transfers between devices  50 us (34%)
  starting transfers between devices  25.9 us (18%)
  blocking collectives  21.7 us (15%)
  Pallas kernels  18.7 us (13%)
  between operations  13.6 us (9%)
  local copies, waits for them, and re-layouts  11.5 us (8%)
  other arithmetic  4.33 us (3%)
    ppermute x6, waiting for transfers between devices, swap(): return lax.ppermute(x, axis, [(0, 1), (1, 0)])  32.2 us
    all_to_all x1, blocking collectives, body(): return unpack(lax.all_to_all(packed, 'z', 0, 0, tiled=True))  21.7 us
    ppermute x6, starting transfers between devices, swap(): return lax.ppermute(x, axis, [(0, 1), (1, 0)])  18.8 us
    all_gather x1, waiting for transfers between devices, body(): x = lax.all_gather(frames, 'z', axis=0, tiled=True)  17.1 us
    pallas_call x2, Pallas kernels, attend(): pl.pallas_call(functools.partial(attend_kernel, head, group), in_specs=[S...  9.98 us
    unnamed x21, local copies, waits for them, and re-layouts  7.63 us
    pallas_call x3, Pallas kernels, project(): pl.pallas_call(kernel, in_specs=[SMEM] * (len(args) - 2) + [VMEM] * 2, ou...  7.47 us
    all_to_all x1, starting transfers between devices, gather_weights(): lax.all_to_all(jnp.broadcast_to(shard[None], (8,) + shard.shape), 'y', 0,...  7.1 us
  transfers between devices with their start and end apart: 8, of which 7 were waited for; matrix products, arithmetic and copies ran while one was open for 6% of the time, Pallas kernels for 6%

profile of v7, /device:TPU:6, one launch (start us, length us, event | category | flops | bytes accessed | tf_op | source)
XLA Modules:
  0.0 145.7 jit_solution(5951038532732566816)
XLA Ops:
  6.5 0.7 all-gather.2.cloned.1.call-update
  7.3 0.8 copy.12
  8.1 0.1 reshape.166
  8.2 3.3 %collective-permute-start = (bf16[48,288]{1,0:T(8,128)(2,1)S(1)}, bf16[48,288]{1,0:T(8,128)(2,1)S(1)}, u32[]{:S(2)}, u32[]{:S(2)}) collective-permute-start(bf16[48,288]{1,0:T(8,128)(2,1)S(1)} %reshape.166), channel_id=1, source_target_pairs={{0,1},{1,0},{2,3},{3,2},{4,5},{5,4},{6,7},{7,6},{8,9},{9,8},{10,11... | collective-permute-start | bytes 82952 | tf_op jit(solution)/shard_map/ppermute | solution.py:27
  11.5 4.0 %collective-permute-done = bf16[48,288]{1,0:T(8,128)(2,1)S(1)} collective-permute-done((bf16[48,288]{1,0:T(8,128)(2,1)S(1)}, bf16[48,288]{1,0:T(8,128)(2,1)S(1)}, u32[]{:S(2)}, u32[]{:S(2)}) %collective-permute-start) | collective-permute-done | bytes 27680 | tf_op jit(solution)/shard_map/ppermute | solution.py:27
  15.6 0.1 concatenate.11
  15.8 0.8 broadcast_in_dim.57
  16.6 7.1 %all-to-all-start = ((bf16[8,48,640]{2,1,0:T(8,128)(2,1)}), bf16[8,48,640]{2,1,0:T(8,128)(2,1)S(1)}, u32[]{:S(2)}, u32[]{:S(2)}) async-start(bf16[8,48,640]{2,1,0:T(8,128)(2,1)} %broadcast_in_dim.57), calls=%async_computation | async-start | bytes 983040 | tf_op jit(solution)/shard_map/all_to_all | solution.py:43
  23.7 3.3 %collective-permute-start.1 = (bf16[192,1536]{1,0:T(8,128)(2,1)S(1)}, bf16[192,1536]{1,0:T(8,128)(2,1)S(1)}, u32[]{:S(2)}, u32[]{:S(2)}) collective-permute-start(bf16[192,1536]{1,0:T(8,128)(2,1)S(1)} %copy-done.7), channel_id=1, source_target_pairs={{0,1},{1,0},{2,3},{3,2},{4,5},{5,4},{6,7},{7,6},{8,9},{9,8},{10,11... | collective-permute-start | bytes 1769480 | tf_op jit(solution)/shard_map/ppermute | solution.py:27
  27.0 0.5 broadcast.309
  27.5 0.6 reduce.19
  28.1 0.1 fusion.1
  28.3 0.6 gather_fusion
  28.9 11.9 %collective-permute-done.1.x_ref = bf16[192,1536]{1,0:T(8,128)(2,1)S(1)} collective-permute-done((bf16[192,1536]{1,0:T(8,128)(2,1)S(1)}, bf16[192,1536]{1,0:T(8,128)(2,1)S(1)}, u32[]{:S(2)}, u32[]{:S(2)}) %collective-permute-start.1) | collective-permute-done | bytes 589856 | tf_op jit(solution)/shard_map/ppermute | solution.py:27
  40.7 2.7 %collective-permute-start.2 = (bf16[8,48,640]{2,1,0:T(8,128)(2,1)S(1)}, bf16[8,48,640]{2,1,0:T(8,128)(2,1)S(1)}, u32[]{:S(2)}, u32[]{:S(2)}) collective-permute-start(bf16[8,48,640]{2,1,0:T(8,128)(2,1)S(1)} %all-to-all-done), channel_id=1, source_target_pairs={{0,32},{32,0},{1,33},{33,1},{2,34},{34,2},{3,35},{35,3},{4,36},{36... | collective-permute-start | bytes 1474568 | tf_op jit(solution)/shard_map/ppermute | solution.py:27
  43.5 0.6 reduce.20
  44.2 0.2 and_reduce_fusion
  44.4 0.1 fusion.7
  44.5 0.6 gather_fusion.1
  45.1 8.1 %collective-permute-done.2 = bf16[8,48,640]{2,1,0:T(8,128)(2,1)S(1)} collective-permute-done((bf16[8,48,640]{2,1,0:T(8,128)(2,1)S(1)}, bf16[8,48,640]{2,1,0:T(8,128)(2,1)S(1)}, u32[]{:S(2)}, u32[]{:S(2)}) %collective-permute-start.2) | collective-permute-done | bytes 491552 | tf_op jit(solution)/shard_map/ppermute | solution.py:27
  53.3 0.1 pad_maximum_fusion.1
  53.4 1.9 %collective-permute-start.3 = (bf16[8,2,48,640]{3,2,1,0:T(8,128)(2,1)S(1)}, bf16[8,2,48,640]{3,2,1,0:T(8,128)(2,1)}, u32[]{:S(2)}, u32[]{:S(2)}) collective-permute-start(bf16[8,2,48,640]{3,2,1,0:T(8,128)(2,1)S(1)} %pad_maximum_fusion.1), channel_id=1, source_target_pairs={{0,16},{16,0},{1,17},{17,1},{2,18},{18,2},{3,19},{19,3},{4,20},{20... | collective-permute-start | bytes 2949128 | tf_op jit(solution)/shard_map/ppermute | solution.py:27
  55.5 0.2 slice_reduce_fusion
  55.7 0.2 select_reduce_fusion.1
  55.9 0.2 convert_reduce_fusion
  56.2 0.2 convert_reduce_fusion.2
  56.5 1.5 %collective-permute-done.3 = bf16[8,2,48,640]{3,2,1,0:T(8,128)(2,1)} collective-permute-done((bf16[8,2,48,640]{3,2,1,0:T(8,128)(2,1)S(1)}, bf16[8,2,48,640]{3,2,1,0:T(8,128)(2,1)}, u32[]{:S(2)}, u32[]{:S(2)}) %collective-permute-start.3) | collective-permute-done | bytes 983072 | tf_op jit(solution)/shard_map/ppermute | solution.py:27
  58.0 1.4 select_bitcast_fusion.1
  59.4 0.2 pad_maximum_fusion
  59.6 0.5 shard_map.46
  60.1 17.1 %all-gather.2.cloned.1.call-done.x_ref = bf16[1536,1536]{1,0:T(8,128)(2,1)} async-done(((bf16[192,1536]{1,0:T(8,128)(2,1)}), bf16[1536,1536]{1,0:T(8,128)(2,1)}) %all-gather.2.cloned.1.call-update) | async-done | bytes 4718608 | tf_op jit(solution)/shard_map/all_gather | solution.py:250
  77.2 2.3 %copy-done = bf16[1536,1536]{1,0:T(8,128)(2,1)S(1)} copy-done((bf16[1536,1536]{1,0:T(8,128)(2,1)S(1)}, bf16[1536,1536]{1,0:T(8,128)(2,1)}, u32[]{:S(2)}) %copy-start) | copy-done | bytes 4718616
  79.6 3.2 %shard_map.48 = (bf16[7,288,128]{2,1,0:T(8,128)(2,1)}, bf16[7,288,128]{2,1,0:T(8,128)(2,1)S(1)}) custom-call(s32[1]{0:T(128)} %bitcast.17.z_ref, bf16[1536,1536]{1,0:T(8,128)(2,1)S(1)} %copy-done, bf16[1536,640]{1,0:T(8,128)(2,1)S(1)} %bitcast.33), custom_call_target="tpu_custom_call" | custom-call | flops 1585446912 | bytes 8257536 | tf_op jit(solution)/shard_map/pallas_call | solution.py:78
  82.7 3.3 %collective-permute-start.5 = (bf16[7,288,128]{2,1,0:T(8,128)(2,1)}, bf16[7,288,128]{2,1,0:T(8,128)(2,1)}, u32[]{:S(2)}, u32[]{:S(2)}) collective-permute-start(bf16[7,288,128]{2,1,0:T(8,128)(2,1)} %get-tuple-element.36), channel_id=1, source_target_pairs={{0,1},{1,0},{2,3},{3,2},{4,5},{5,4},{6,7},{7,6},{8,9},{9,8},{10,11... | collective-permute-start | bytes 1548296 | tf_op jit(solution)/shard_map/ppermute | solution.py:27
  86.1 4.2 %collective-permute-start.4 = (bf16[7,288,128]{2,1,0:T(8,128)(2,1)S(1)}, bf16[7,288,128]{2,1,0:T(8,128)(2,1)S(1)}, u32[]{:S(2)}, u32[]{:S(2)}) collective-permute-start(bf16[7,288,128]{2,1,0:T(8,128)(2,1)S(1)} %get-tuple-element.31), channel_id=1, source_target_pairs={{0,1},{1,0},{2,3},{3,2},{4,5},{5,4},{6,7},{7,6},{8,9},{9,8},{10,11... | collective-permute-start | bytes 1548296 | tf_op jit(solution)/shard_map/ppermute | solution.py:27
  90.3 3.8 %shard_map.47 = (bf16[1536,256]{1,0:T(8,128)(2,1)S(1)}, bf16[1536,128]{1,0:T(8,128)(2,1)S(1)}, bf16[1536,256]{1,0:T(8,128)(2,1)S(1)}) custom-call(bf16[1536,1536]{1,0:T(8,128)(2,1)S(1)} %copy-done, bf16[1536,640]{1,0:T(8,128)(2,1)S(1)} %bitcast.34), custom_call_target="tpu_custom_call" | custom-call | flops 3019898880 | bytes 9437184 | tf_op jit(solution)/shard_map/pallas_call | solution.py:78
  94.1 0.9 copy-done.1
  95.0 0.9 copy-done.3
  95.9 0.8 copy-done.5
  96.7 0.3 copy.16.qid_ref
  97.0 4.1 %collective-permute-done.5.refs_0_ = bf16[7,288,128]{2,1,0:T(8,128)(2,1)} collective-permute-done((bf16[7,288,128]{2,1,0:T(8,128)(2,1)}, bf16[7,288,128]{2,1,0:T(8,128)(2,1)}, u32[]{:S(2)}, u32[]{:S(2)}) %collective-permute-start.5) | collective-permute-done | bytes 516128 | tf_op jit(solution)/shard_map/ppermute | solution.py:27
  101.1 1.1 copy-done.2
  102.2 1.1 copy-done.4
  103.3 4.9 %shard_map.49.refs_5_ = bf16[8,192,128]{2,1,0:T(8,128)(2,1)S(1)} custom-call(s32[48]{0:T(128)S(1)} %concatenate.9.info_ref, s32[1536,1]{1,0:T(8,128)S(1)} %copy.16.qid_ref, s32[1,3328]{1,0:T(1,128)S(1)} %broadcast_in_dim.55.kid_ref, bf16[1536,256]{1,0:T(8,128)(2,1)S(1)} %copy-done.4, bf16[7,288,128]{2,1,0:T(8,128)(2,1)} %collective-permute-done.5.refs_0_, ...), custom_call_target="tpu_custom_call" | custom-call | flops 4294967296 | bytes 4194304 | tf_op jit(solution)/shard_map/pallas_call | solution.py:188
  108.3 2.6 %collective-permute-done.4.refs_0_ = bf16[7,288,128]{2,1,0:T(8,128)(2,1)S(1)} collective-permute-done((bf16[7,288,128]{2,1,0:T(8,128)(2,1)S(1)}, bf16[7,288,128]{2,1,0:T(8,128)(2,1)S(1)}, u32[]{:S(2)}, u32[]{:S(2)}) %collective-permute-start.4) | collective-permute-done | bytes 516128 | tf_op jit(solution)/shard_map/ppermute | solution.py:27
  110.9 5.0 %shard_map.50 = bf16[8,288,128]{2,1,0:T(8,128)(2,1)S(1)} custom-call(s32[48]{0:T(128)S(1)} %concatenate.9.info_ref, s32[1536,1]{1,0:T(8,128)S(1)} %copy.16.qid_ref, s32[1,3328]{1,0:T(1,128)S(1)} %broadcast_in_dim.55.kid_ref, bf16[1536,256]{1,0:T(8,128)(2,1)S(1)} %copy-done.4, bf16[7,288,128]{2,1,0:T(8,128)(2,1)S(1)} %collective-permute-done.4.refs_0_, ...), custom_call_target="tpu_custom_call" | custom-call | flops 4294967296 | bytes 4194304 | tf_op jit(solution)/shard_map/pallas_call | solution.py:188
  115.9 21.7 %all_to_all.10.in_ref = bf16[8,288,128]{2,1,0:T(8,128)(2,1)S(1)} all-to-all(bf16[8,288,128]{2,1,0:T(8,128)(2,1)S(1)} %shard_map.50), channel_id=1, replica_groups=mesh['y'=8,'xl'=2,'core'=2,'z'=8,'xh'=2] {'z'}, dimensions={0} | all-to-all | bytes 1179648 | tf_op jit(solution)/shard_map/all_to_all | solution.py:260
  137.6 1.2 shard_map.51
  (34 shorter events, 0.9 us)
Async XLA Ops:
  6.5 17.1 %copy-start.7 = (bf16[192,1536]{1,0:T(8,128)(2,1)S(1)}, bf16[192,1536]{1,0:T(8,128)(2,1)}, u32[]{:S(2)}) copy-start(bf16[192,1536]{1,0:T(8,128)(2,1)} %param.4) | copy-start | bytes 1769476
  6.5 21.0 %copy-start.9 = (s32[1,16]{1,0:T(1,128)S(1)}, s32[1,16]{1,0:T(1,128)}, u32[]{:S(2)}) copy-start(s32[1,16]{1,0:T(1,128)} %param.6) | copy-start | bytes 196
  6.5 37.0 %copy-start.8 = (s32[1,3072]{1,0:T(1,128)S(1)}, s32[1,3072]{1,0:T(1,128)}, u32[]{:S(2)}) copy-start(s32[1,3072]{1,0:T(1,128)} %param.5) | copy-start | bytes 36868
  6.5 70.7 %all-gather.2.cloned.1.call-start = ((), (), s32[]{:S(2)}) async-start(), calls=%async_computation.2 | async-start | bytes 5308416 | tf_op jit(solution)/shard_map/all_gather | solution.py:250
  8.2 7.4 %collective-permute-start = (bf16[48,288]{1,0:T(8,128)(2,1)S(1)}, bf16[48,288]{1,0:T(8,128)(2,1)S(1)}, u32[]{:S(2)}, u32[]{:S(2)}) collective-permute-start(bf16[48,288]{1,0:T(8,128)(2,1)S(1)} %reshape.166), channel_id=1, source_target_pairs={{0,1},{1,0},{2,3},{3,2},{4,5},{5,4},{6,7},{7,6},{8,9},{9,8},{10,11... | collective-permute-start | bytes 82952 | tf_op jit(solution)/shard_map/ppermute | solution.py:27
  16.6 24.1 %all-to-all-start = ((bf16[8,48,640]{2,1,0:T(8,128)(2,1)}), bf16[8,48,640]{2,1,0:T(8,128)(2,1)S(1)}, u32[]{:S(2)}, u32[]{:S(2)}) async-start(bf16[8,48,640]{2,1,0:T(8,128)(2,1)} %broadcast_in_dim.57), calls=%async_computation | async-start | bytes 983040 | tf_op jit(solution)/shard_map/all_to_all | solution.py:43
  23.7 17.0 %collective-permute-start.1 = (bf16[192,1536]{1,0:T(8,128)(2,1)S(1)}, bf16[192,1536]{1,0:T(8,128)(2,1)S(1)}, u32[]{:S(2)}, u32[]{:S(2)}) collective-permute-start(bf16[192,1536]{1,0:T(8,128)(2,1)S(1)} %copy-done.7), channel_id=1, source_target_pairs={{0,1},{1,0},{2,3},{3,2},{4,5},{5,4},{6,7},{7,6},{8,9},{9,8},{10,11... | collective-permute-start | bytes 1769480 | tf_op jit(solution)/shard_map/ppermute | solution.py:27
  40.7 12.5 %collective-permute-start.2 = (bf16[8,48,640]{2,1,0:T(8,128)(2,1)S(1)}, bf16[8,48,640]{2,1,0:T(8,128)(2,1)S(1)}, u32[]{:S(2)}, u32[]{:S(2)}) collective-permute-start(bf16[8,48,640]{2,1,0:T(8,128)(2,1)S(1)} %all-to-all-done), channel_id=1, source_target_pairs={{0,32},{32,0},{1,33},{33,1},{2,34},{34,2},{3,35},{35,3},{4,36},{36... | collective-permute-start | bytes 1474568 | tf_op jit(solution)/shard_map/ppermute | solution.py:27
  53.4 4.6 %collective-permute-start.3 = (bf16[8,2,48,640]{3,2,1,0:T(8,128)(2,1)S(1)}, bf16[8,2,48,640]{3,2,1,0:T(8,128)(2,1)}, u32[]{:S(2)}, u32[]{:S(2)}) collective-permute-start(bf16[8,2,48,640]{3,2,1,0:T(8,128)(2,1)S(1)} %pad_maximum_fusion.1), channel_id=1, source_target_pairs={{0,16},{16,0},{1,17},{17,1},{2,18},{18,2},{3,19},{19,3},{4,20},{20... | collective-permute-start | bytes 2949128 | tf_op jit(solution)/shard_map/ppermute | solution.py:27
  77.2 2.3 %copy-start = (bf16[1536,1536]{1,0:T(8,128)(2,1)S(1)}, bf16[1536,1536]{1,0:T(8,128)(2,1)}, u32[]{:S(2)}) copy-start(bf16[1536,1536]{1,0:T(8,128)(2,1)} %all-gather.2.cloned.1.call-done.x_ref) | copy-start | bytes 14155780
  82.7 18.3 %collective-permute-start.5 = (bf16[7,288,128]{2,1,0:T(8,128)(2,1)}, bf16[7,288,128]{2,1,0:T(8,128)(2,1)}, u32[]{:S(2)}, u32[]{:S(2)}) collective-permute-start(bf16[7,288,128]{2,1,0:T(8,128)(2,1)} %get-tuple-element.36), channel_id=1, source_target_pairs={{0,1},{1,0},{2,3},{3,2},{4,5},{5,4},{6,7},{7,6},{8,9},{9,8},{10,11... | collective-permute-start | bytes 1548296 | tf_op jit(solution)/shard_map/ppermute | solution.py:27
  86.1 24.8 %collective-permute-start.4 = (bf16[7,288,128]{2,1,0:T(8,128)(2,1)S(1)}, bf16[7,288,128]{2,1,0:T(8,128)(2,1)S(1)}, u32[]{:S(2)}, u32[]{:S(2)}) collective-permute-start(bf16[7,288,128]{2,1,0:T(8,128)(2,1)S(1)} %get-tuple-element.31), channel_id=1, source_target_pairs={{0,1},{1,0},{2,3},{3,2},{4,5},{5,4},{6,7},{7,6},{8,9},{9,8},{10,11... | collective-permute-start | bytes 1548296 | tf_op jit(solution)/shard_map/ppermute | solution.py:27
  94.1 0.9 copy-start.1
  95.0 0.9 copy-start.3
  95.9 0.8 copy-start.5
  101.1 1.1 copy-start.2
  102.2 1.1 copy-start.4
  103.3 7.5 %copy-start.6 = (bf16[1536,128]{1,0:T(8,128)(2,1)S(1)}, bf16[1536,128]{1,0:T(8,128)(2,1)}, u32[]{:S(2)}) copy-start(bf16[1536,128]{1,0:T(8,128)(2,1)} %copy-done.5) | copy-start | bytes 1179652
Sparse Core Ops, SparseCore 0:
  9.4 67.7 all-gather.1

commit v8 on v7

--- a/solution.py
+++ b/solution.py
@@ -53,25 +53,32 @@
     last_ref[...] = y[:, 256:]
 
 
-def project_wires_kernel(z_ref, x_ref, w_ref, first_ref, second_ref):
-    starts = [pl.multiple_of(lax.rem(z_ref[0] + 1 + i, NZ) * FR, FR) for i in range(7)]
-    x = jnp.concatenate([x_ref[pl.ds(start, FR), :] for start in starts], axis=0)
-    y = jnp.dot(x, w_ref[:, :384], preferred_element_type=jnp.float32)
+def rotated(z_ref, x_ref, blocks):
+    starts = [pl.multiple_of(lax.rem(z_ref[0] + 1 + i, NZ) * FR, FR) for i in range(blocks)]
+    return jnp.concatenate([x_ref[pl.ds(start, FR), :] for start in starts], axis=0)
+
+
+def project_wire_kernel(z_ref, x_ref, w_ref, wire_ref):
+    y = jnp.dot(rotated(z_ref, x_ref, 7), w_ref[:, :256], preferred_element_type=jnp.float32)
     half = lax.broadcasted_iota(jnp.int32, (FR // 2, 128), 1) < 64
     for b in range(7):
         block = y[b * FR : (b + 1) * FR]
-        first_ref[b, :FR, :] = block[:, :128].astype(jnp.bfloat16)
-        second_ref[b, :FR, :] = block[:, 256:].astype(jnp.bfloat16)
+        wire_ref[b, :FR, :] = block[:, :128].astype(jnp.bfloat16)
+        upper, turned = block[: FR // 2, 128:], pltpu.roll(block[FR // 2 :, 128:], 64, 1)
+        wire_ref[b, FR:, :] = jnp.where(half, upper, turned).astype(jnp.bfloat16)
+
+
+def project_own_kernel(z_ref, x_ref, w_ref, most_ref, last_ref, q_ref, wire_ref):
+    y = jnp.dot(rotated(z_ref, x_ref, NZ), w_ref[...], preferred_element_type=jnp.float32)
+    most_ref[...] = y[:, :256].astype(jnp.bfloat16)
+    last_ref[...] = y[:, 256:384].astype(jnp.bfloat16)
+    q_ref[...] = y[:, 384:].astype(jnp.bfloat16)
+    half = lax.broadcasted_iota(jnp.int32, (FR // 2, 128), 1) < 64
+    for b in range(7):
+        block = y[b * FR : (b + 1) * FR]
+        wire_ref[b, :FR, :] = block[:, 256:384].astype(jnp.bfloat16)
         upper, turned = block[: FR // 2, 128:256], pltpu.roll(block[FR // 2 :, 128:256], 64, 1)
-        first_ref[b, FR:, :] = jnp.where(half, upper, turned).astype(jnp.bfloat16)
-        second_ref[b, FR:, :] = jnp.where(half, turned, upper).astype(jnp.bfloat16)
-
-
-def project_own_kernel(x_ref, w_ref, most_ref, last_ref, q_ref):
-    y = jnp.dot(x_ref[...], w_ref[...], preferred_element_type=jnp.float32).astype(jnp.bfloat16)
-    most_ref[...] = y[:, :256]
-    last_ref[...] = y[:, 256:384]
-    q_ref[...] = y[:, 384:]
+        wire_ref[b, FR:, :] = jnp.where(half, turned, upper).astype(jnp.bfloat16)
 
 
 def project(kernel, rows, columns, shapes, *args):
@@ -80,7 +87,7 @@
         in_specs=[SMEM] * (len(args) - 2) + [VMEM] * 2,
         out_specs=[VMEM] * len(shapes),
         out_shape=[jax.ShapeDtypeStruct(shape, jnp.bfloat16) for shape in shapes],
-        compiler_params=pltpu.CompilerParams(vmem_limit_bytes=16 << 20),
+        compiler_params=pltpu.CompilerParams(vmem_limit_bytes=24 << 20),
         cost_estimate=pl.CostEstimate(
             flops=2 * rows * D * columns, bytes_accessed=rows * D * 4, transcendentals=0
         ),
@@ -91,12 +98,13 @@
     return project(project_near_kernel, FR, 384, [(FR, 256), (FR, 128)], x, w)
 
 
-def project_wires(z, x, w):
-    return project(project_wires_kernel, 7 * FR, 384, [(7, FR * 3 // 2, 128)] * 2, z[None], x, w)
-
-
-def project_own(x, w):
-    return project(project_own_kernel, ROWS, 640, [(ROWS, 256), (ROWS, 128), (ROWS, 256)], x, w)
+def project_wire(z, x, w):
+    return project(project_wire_kernel, 7 * FR, 256, [(7, FR * 3 // 2, 128)], z[None], x, w)[0]
+
+
+def project_own(z, x, w):
+    shapes = [(ROWS, 256), (ROWS, 128), (ROWS, 256), (7, FR * 3 // 2, 128)]
+    return project(project_own_kernel, ROWS, 640, shapes, z[None], x, w)
 
 
 def attend_jobs(jobs, n, kid_ref, kv_ref, key_lane):
@@ -142,7 +150,7 @@
 
     wire_ref, most_ref, near_most_ref, last_ref, near_last_ref, packed_ref = parts if head else (*parts, None, None, None)
     for s in range(NZ):
-        keep(info_ref[s], most_ref, last_ref, info_ref[40 + s] * FR)
+        keep(info_ref[s], most_ref, last_ref, s * FR)
     keep(info_ref[NZ + 7], near_most_ref, near_last_ref, 0)
     for s in range(7):
         place = info_ref[NZ + s] * FR
@@ -158,9 +166,8 @@
         jobs = []
         for s in slots:
             rows = pl.ds(pl.multiple_of(s * FR, FR), FR)
-            query_rows = pl.ds(pl.multiple_of(info_ref[40 + s] * FR, FR), FR)
             first = jnp.minimum(info_ref[16 + s], PAD - count * TILE)
-            jobs.append((q_ref[query_rows, head * 128 : head * 128 + 128], qid_ref[rows, :], first))
+            jobs.append((q_ref[rows, head * 128 : head * 128 + 128], qid_ref[rows, :], first))
 
         def attend_some(n):
             outs = attend_jobs(jobs, n, kid_ref, kv_ref, head * 128)
@@ -252,9 +259,9 @@
     near_most, near_last = project_near(partner, w)
     info, qid, kid = plan(seg_ids[0], assign[0], z, xh)
     x, info, qid, kid, near_last = lax.optimization_barrier((x, info, qid, kid, near_last))
-    wire0, wire1 = project_wires(z, x, w)
-    other0, other1 = swap(wire0, "xh"), swap(wire1, "xh")
-    most, last, q = project_own(x, w)
+    other0 = swap(project_wire(z, x, w), "xh")
+    most, last, q, wire1 = project_own(z, x, w)
+    other1 = swap(wire1, "xh")
     packed = attend(0, info, qid, kid, q, other0, most, near_most)
     packed = attend(1, info, qid, kid, q, other1, most, near_most, last, near_last, packed)
     return unpack(lax.all_to_all(packed, "z", 0, 0, tiled=True))

time: 147 us -> 146 us (level)
  Pallas kernels: 18.7 us -> 16.5 us
where the time goes in v8:
time: 146 us; the launch traced here: 144 us
  waiting for transfers between devices  49.9 us (34%)
  starting transfers between devices  25.9 us (18%)
  blocking collectives  22.6 us (15%)
  Pallas kernels  16.5 us (11%)
  between operations  13.6 us (9%)
  local copies, waits for them, and re-layouts  11.5 us (8%)
  other arithmetic  4.33 us (3%)
    ppermute x6, waiting for transfers between devices, swap(): return lax.ppermute(x, axis, [(0, 1), (1, 0)])  32.1 us
    all_to_all x1, blocking collectives, body(): return unpack(lax.all_to_all(packed, 'z', 0, 0, tiled=True))  22.6 us
    ppermute x6, starting transfers between devices, swap(): return lax.ppermute(x, axis, [(0, 1), (1, 0)])  18.8 us
    all_gather x1, waiting for transfers between devices, body(): x = lax.all_gather(frames, 'z', axis=0, tiled=True)  17.1 us
    pallas_call x2, Pallas kernels, attend(): pl.pallas_call(functools.partial(attend_kernel, head, group), in_specs=[S...  8.82 us
    unnamed x21, local copies, waits for them, and re-layouts  7.62 us
    all_to_all x1, starting transfers between devices, gather_weights(): lax.all_to_all(jnp.broadcast_to(shard[None], (8,) + shard.shape), 'y', 0,...  7.1 us
    pallas_call x3, Pallas kernels, project(): pl.pallas_call(kernel, in_specs=[SMEM] * (len(args) - 2) + [VMEM] * 2, ou...  6.47 us
  transfers between devices with their start and end apart: 8, of which 7 were waited for; matrix products, arithmetic and copies ran while one was open for 6% of the time, Pallas kernels for 6%

profile of v8, /device:TPU:6, one launch (start us, length us, event | category | flops | bytes accessed | tf_op | source)
XLA Modules:
  0.0 144.2 jit_solution(13921330993356014818)
XLA Ops:
  6.5 0.7 all-gather.2.cloned.1.call-update
  7.3 0.8 copy.12
  8.1 0.1 reshape.166
  8.2 3.3 %collective-permute-start = (bf16[48,288]{1,0:T(8,128)(2,1)S(1)}, bf16[48,288]{1,0:T(8,128)(2,1)S(1)}, u32[]{:S(2)}, u32[]{:S(2)}) collective-permute-start(bf16[48,288]{1,0:T(8,128)(2,1)S(1)} %reshape.166), channel_id=1, source_target_pairs={{0,1},{1,0},{2,3},{3,2},{4,5},{5,4},{6,7},{7,6},{8,9},{9,8},{10,11... | collective-permute-start | bytes 82952 | tf_op jit(solution)/shard_map/ppermute | solution.py:27
  11.5 4.0 %collective-permute-done = bf16[48,288]{1,0:T(8,128)(2,1)S(1)} collective-permute-done((bf16[48,288]{1,0:T(8,128)(2,1)S(1)}, bf16[48,288]{1,0:T(8,128)(2,1)S(1)}, u32[]{:S(2)}, u32[]{:S(2)}) %collective-permute-start) | collective-permute-done | bytes 27680 | tf_op jit(solution)/shard_map/ppermute | solution.py:27
  15.6 0.1 concatenate.11
  15.8 0.8 broadcast_in_dim.58
  16.6 7.1 %all-to-all-start = ((bf16[8,48,640]{2,1,0:T(8,128)(2,1)}), bf16[8,48,640]{2,1,0:T(8,128)(2,1)S(1)}, u32[]{:S(2)}, u32[]{:S(2)}) async-start(bf16[8,48,640]{2,1,0:T(8,128)(2,1)} %broadcast_in_dim.58), calls=%async_computation | async-start | bytes 983040 | tf_op jit(solution)/shard_map/all_to_all | solution.py:43
  23.7 3.3 %collective-permute-start.1 = (bf16[192,1536]{1,0:T(8,128)(2,1)S(1)}, bf16[192,1536]{1,0:T(8,128)(2,1)S(1)}, u32[]{:S(2)}, u32[]{:S(2)}) collective-permute-start(bf16[192,1536]{1,0:T(8,128)(2,1)S(1)} %copy-done.7), channel_id=1, source_target_pairs={{0,1},{1,0},{2,3},{3,2},{4,5},{5,4},{6,7},{7,6},{8,9},{9,8},{10,11... | collective-permute-start | bytes 1769480 | tf_op jit(solution)/shard_map/ppermute | solution.py:27
  27.0 0.5 broadcast.309
  27.5 0.6 reduce.19
  28.1 0.1 fusion.1
  28.3 0.6 gather_fusion
  28.9 11.9 %collective-permute-done.1.x_ref = bf16[192,1536]{1,0:T(8,128)(2,1)S(1)} collective-permute-done((bf16[192,1536]{1,0:T(8,128)(2,1)S(1)}, bf16[192,1536]{1,0:T(8,128)(2,1)S(1)}, u32[]{:S(2)}, u32[]{:S(2)}) %collective-permute-start.1) | collective-permute-done | bytes 589856 | tf_op jit(solution)/shard_map/ppermute | solution.py:27
  40.7 2.7 %collective-permute-start.2 = (bf16[8,48,640]{2,1,0:T(8,128)(2,1)S(1)}, bf16[8,48,640]{2,1,0:T(8,128)(2,1)S(1)}, u32[]{:S(2)}, u32[]{:S(2)}) collective-permute-start(bf16[8,48,640]{2,1,0:T(8,128)(2,1)S(1)} %all-to-all-done), channel_id=1, source_target_pairs={{0,32},{32,0},{1,33},{33,1},{2,34},{34,2},{3,35},{35,3},{4,36},{36... | collective-permute-start | bytes 1474568 | tf_op jit(solution)/shard_map/ppermute | solution.py:27
  43.5 0.6 reduce.20
  44.2 0.2 and_reduce_fusion
  44.4 0.1 fusion.7
  44.5 0.6 gather_fusion.1
  45.1 8.1 %collective-permute-done.2 = bf16[8,48,640]{2,1,0:T(8,128)(2,1)S(1)} collective-permute-done((bf16[8,48,640]{2,1,0:T(8,128)(2,1)S(1)}, bf16[8,48,640]{2,1,0:T(8,128)(2,1)S(1)}, u32[]{:S(2)}, u32[]{:S(2)}) %collective-permute-start.2) | collective-permute-done | bytes 491552 | tf_op jit(solution)/shard_map/ppermute | solution.py:27
  53.3 0.1 pad_maximum_fusion.1
  53.4 1.9 %collective-permute-start.3 = (bf16[8,2,48,640]{3,2,1,0:T(8,128)(2,1)S(1)}, bf16[8,2,48,640]{3,2,1,0:T(8,128)(2,1)}, u32[]{:S(2)}, u32[]{:S(2)}) collective-permute-start(bf16[8,2,48,640]{3,2,1,0:T(8,128)(2,1)S(1)} %pad_maximum_fusion.1), channel_id=1, source_target_pairs={{0,16},{16,0},{1,17},{17,1},{2,18},{18,2},{3,19},{19,3},{4,20},{20... | collective-permute-start | bytes 2949128 | tf_op jit(solution)/shard_map/ppermute | solution.py:27
  55.5 0.2 slice_reduce_fusion
  55.7 0.2 select_reduce_fusion.1
  55.9 0.2 convert_reduce_fusion
  56.2 0.2 convert_reduce_fusion.2
  56.5 1.5 %collective-permute-done.3 = bf16[8,2,48,640]{3,2,1,0:T(8,128)(2,1)} collective-permute-done((bf16[8,2,48,640]{3,2,1,0:T(8,128)(2,1)S(1)}, bf16[8,2,48,640]{3,2,1,0:T(8,128)(2,1)}, u32[]{:S(2)}, u32[]{:S(2)}) %collective-permute-start.3) | collective-permute-done | bytes 983072 | tf_op jit(solution)/shard_map/ppermute | solution.py:27
  58.0 1.4 select_bitcast_fusion.1
  59.4 0.2 pad_maximum_fusion
  59.6 0.5 shard_map.46
  60.1 17.1 %all-gather.2.cloned.1.call-done.x_ref = bf16[1536,1536]{1,0:T(8,128)(2,1)} async-done(((bf16[192,1536]{1,0:T(8,128)(2,1)}), bf16[1536,1536]{1,0:T(8,128)(2,1)}) %all-gather.2.cloned.1.call-update) | async-done | bytes 4718608 | tf_op jit(solution)/shard_map/all_gather | solution.py:257
  77.2 2.3 %copy-done = bf16[1536,1536]{1,0:T(8,128)(2,1)S(1)} copy-done((bf16[1536,1536]{1,0:T(8,128)(2,1)S(1)}, bf16[1536,1536]{1,0:T(8,128)(2,1)}, u32[]{:S(2)}) %copy-start) | copy-done | bytes 4718616
  79.6 1.3 shard_map.48
  80.9 3.4 %collective-permute-start.5 = (bf16[7,288,128]{2,1,0:T(8,128)(2,1)S(1)}, bf16[7,288,128]{2,1,0:T(8,128)(2,1)S(1)}, u32[]{:S(2)}, u32[]{:S(2)}) collective-permute-start(bf16[7,288,128]{2,1,0:T(8,128)(2,1)S(1)} %shard_map.48), channel_id=1, source_target_pairs={{0,1},{1,0},{2,3},{3,2},{4,5},{5,4},{6,7},{7,6},{8,9},{9,8},{10,11... | collective-permute-start | bytes 1548296 | tf_op jit(solution)/shard_map/ppermute | solution.py:27
  84.3 4.7 %shard_map.47 = (bf16[1536,256]{1,0:T(8,128)(2,1)S(1)}, bf16[1536,128]{1,0:T(8,128)(2,1)S(1)}, bf16[1536,256]{1,0:T(8,128)(2,1)S(1)}, bf16[7,288,128]{2,1,0:T(8,128)(2,1)}) custom-call(s32[1]{0:T(128)} %bitcast.17.z_ref, bf16[1536,1536]{1,0:T(8,128)(2,1)S(1)} %copy-done, bf16[1536,640]{1,0:T(8,128)(2,1)S(1)} %bitcast.34), custom_call_target="tpu_custom_call" | custom-call | flops 3019898880 | bytes 9437184 | tf_op jit(solution)/shard_map/pallas_call | solution.py:85
  89.0 0.9 copy-done.1
  89.9 0.9 copy-done.3
  90.7 0.7 copy-done.5
  91.5 4.2 %collective-permute-start.4 = (bf16[7,288,128]{2,1,0:T(8,128)(2,1)}, bf16[7,288,128]{2,1,0:T(8,128)(2,1)S(1)}, u32[]{:S(2)}, u32[]{:S(2)}) collective-permute-start(bf16[7,288,128]{2,1,0:T(8,128)(2,1)} %get-tuple-element.30), channel_id=1, source_target_pairs={{0,1},{1,0},{2,3},{3,2},{4,5},{5,4},{6,7},{7,6},{8,9},{9,8},{10,11... | collective-permute-start | bytes 1548296 | tf_op jit(solution)/shard_map/ppermute | solution.py:27
  95.6 0.3 copy.16.qid_ref
  95.9 2.4 %collective-permute-done.5.refs_0_ = bf16[7,288,128]{2,1,0:T(8,128)(2,1)S(1)} collective-permute-done((bf16[7,288,128]{2,1,0:T(8,128)(2,1)S(1)}, bf16[7,288,128]{2,1,0:T(8,128)(2,1)S(1)}, u32[]{:S(2)}, u32[]{:S(2)}) %collective-permute-start.5) | collective-permute-done | bytes 516128 | tf_op jit(solution)/shard_map/ppermute | solution.py:27
  98.3 1.1 copy-done.2
  99.5 1.1 copy-done.4
  100.6 4.1 %shard_map.49.refs_5_ = bf16[8,192,128]{2,1,0:T(8,128)(2,1)S(1)} custom-call(s32[48]{0:T(128)S(1)} %concatenate.9.info_ref, s32[1536,1]{1,0:T(8,128)S(1)} %copy.16.qid_ref, s32[1,3328]{1,0:T(1,128)S(1)} %broadcast_in_dim.56.kid_ref, bf16[1536,256]{1,0:T(8,128)(2,1)S(1)} %copy-done.4, bf16[7,288,128]{2,1,0:T(8,128)(2,1)S(1)} %collective-permute-done.5.refs_0_, ...), custom_call_target="tpu_custom_call" | custom-call | flops 4294967296 | bytes 4194304 | tf_op jit(solution)/shard_map/pallas_call | solution.py:195
  104.7 4.2 %collective-permute-done.4.refs_0_ = bf16[7,288,128]{2,1,0:T(8,128)(2,1)S(1)} collective-permute-done((bf16[7,288,128]{2,1,0:T(8,128)(2,1)}, bf16[7,288,128]{2,1,0:T(8,128)(2,1)S(1)}, u32[]{:S(2)}, u32[]{:S(2)}) %collective-permute-start.4) | collective-permute-done | bytes 516128 | tf_op jit(solution)/shard_map/ppermute | solution.py:27
  108.9 4.7 %shard_map.50 = bf16[8,288,128]{2,1,0:T(8,128)(2,1)S(1)} custom-call(s32[48]{0:T(128)S(1)} %concatenate.9.info_ref, s32[1536,1]{1,0:T(8,128)S(1)} %copy.16.qid_ref, s32[1,3328]{1,0:T(1,128)S(1)} %broadcast_in_dim.56.kid_ref, bf16[1536,256]{1,0:T(8,128)(2,1)S(1)} %copy-done.4, bf16[7,288,128]{2,1,0:T(8,128)(2,1)S(1)} %collective-permute-done.4.refs_0_, ...), custom_call_target="tpu_custom_call" | custom-call | flops 4294967296 | bytes 4194304 | tf_op jit(solution)/shard_map/pallas_call | solution.py:195
  113.6 22.6 %all_to_all.10.in_ref = bf16[8,288,128]{2,1,0:T(8,128)(2,1)S(1)} all-to-all(bf16[8,288,128]{2,1,0:T(8,128)(2,1)S(1)} %shard_map.50), channel_id=1, replica_groups=mesh['y'=8,'xl'=2,'core'=2,'z'=8,'xh'=2] {'z'}, dimensions={0} | all-to-all | bytes 1179648 | tf_op jit(solution)/shard_map/all_to_all | solution.py:267
  136.2 1.2 shard_map.51
  (34 shorter events, 0.9 us)
Async XLA Ops:
  6.5 17.1 %copy-start.7 = (bf16[192,1536]{1,0:T(8,128)(2,1)S(1)}, bf16[192,1536]{1,0:T(8,128)(2,1)}, u32[]{:S(2)}) copy-start(bf16[192,1536]{1,0:T(8,128)(2,1)} %param.4) | copy-start | bytes 1769476
  6.5 21.0 %copy-start.9 = (s32[1,16]{1,0:T(1,128)S(1)}, s32[1,16]{1,0:T(1,128)}, u32[]{:S(2)}) copy-start(s32[1,16]{1,0:T(1,128)} %param.6) | copy-start | bytes 196
  6.5 37.0 %copy-start.8 = (s32[1,3072]{1,0:T(1,128)S(1)}, s32[1,3072]{1,0:T(1,128)}, u32[]{:S(2)}) copy-start(s32[1,3072]{1,0:T(1,128)} %param.5) | copy-start | bytes 36868
  6.5 70.7 %all-gather.2.cloned.1.call-start = ((), (), s32[]{:S(2)}) async-start(), calls=%async_computation.2 | async-start | bytes 5308416 | tf_op jit(solution)/shard_map/all_gather | solution.py:257
  8.2 7.4 %collective-permute-start = (bf16[48,288]{1,0:T(8,128)(2,1)S(1)}, bf16[48,288]{1,0:T(8,128)(2,1)S(1)}, u32[]{:S(2)}, u32[]{:S(2)}) collective-permute-start(bf16[48,288]{1,0:T(8,128)(2,1)S(1)} %reshape.166), channel_id=1, source_target_pairs={{0,1},{1,0},{2,3},{3,2},{4,5},{5,4},{6,7},{7,6},{8,9},{9,8},{10,11... | collective-permute-start | bytes 82952 | tf_op jit(solution)/shard_map/ppermute | solution.py:27
  16.6 24.1 %all-to-all-start = ((bf16[8,48,640]{2,1,0:T(8,128)(2,1)}), bf16[8,48,640]{2,1,0:T(8,128)(2,1)S(1)}, u32[]{:S(2)}, u32[]{:S(2)}) async-start(bf16[8,48,640]{2,1,0:T(8,128)(2,1)} %broadcast_in_dim.58), calls=%async_computation | async-start | bytes 983040 | tf_op jit(solution)/shard_map/all_to_all | solution.py:43
  23.7 17.0 %collective-permute-start.1 = (bf16[192,1536]{1,0:T(8,128)(2,1)S(1)}, bf16[192,1536]{1,0:T(8,128)(2,1)S(1)}, u32[]{:S(2)}, u32[]{:S(2)}) collective-permute-start(bf16[192,1536]{1,0:T(8,128)(2,1)S(1)} %copy-done.7), channel_id=1, source_target_pairs={{0,1},{1,0},{2,3},{3,2},{4,5},{5,4},{6,7},{7,6},{8,9},{9,8},{10,11... | collective-permute-start | bytes 1769480 | tf_op jit(solution)/shard_map/ppermute | solution.py:27
  40.7 12.5 %collective-permute-start.2 = (bf16[8,48,640]{2,1,0:T(8,128)(2,1)S(1)}, bf16[8,48,640]{2,1,0:T(8,128)(2,1)S(1)}, u32[]{:S(2)}, u32[]{:S(2)}) collective-permute-start(bf16[8,48,640]{2,1,0:T(8,128)(2,1)S(1)} %all-to-all-done), channel_id=1, source_target_pairs={{0,32},{32,0},{1,33},{33,1},{2,34},{34,2},{3,35},{35,3},{4,36},{36... | collective-permute-start | bytes 1474568 | tf_op jit(solution)/shard_map/ppermute | solution.py:27
  53.4 4.6 %collective-permute-start.3 = (bf16[8,2,48,640]{3,2,1,0:T(8,128)(2,1)S(1)}, bf16[8,2,48,640]{3,2,1,0:T(8,128)(2,1)}, u32[]{:S(2)}, u32[]{:S(2)}) collective-permute-start(bf16[8,2,48,640]{3,2,1,0:T(8,128)(2,1)S(1)} %pad_maximum_fusion.1), channel_id=1, source_target_pairs={{0,16},{16,0},{1,17},{17,1},{2,18},{18,2},{3,19},{19,3},{4,20},{20... | collective-permute-start | bytes 2949128 | tf_op jit(solution)/shard_map/ppermute | solution.py:27
  77.2 2.3 %copy-start = (bf16[1536,1536]{1,0:T(8,128)(2,1)S(1)}, bf16[1536,1536]{1,0:T(8,128)(2,1)}, u32[]{:S(2)}) copy-start(bf16[1536,1536]{1,0:T(8,128)(2,1)} %all-gather.2.cloned.1.call-done.x_ref) | copy-start | bytes 14155780
  80.9 17.4 %collective-permute-start.5 = (bf16[7,288,128]{2,1,0:T(8,128)(2,1)S(1)}, bf16[7,288,128]{2,1,0:T(8,128)(2,1)S(1)}, u32[]{:S(2)}, u32[]{:S(2)}) collective-permute-start(bf16[7,288,128]{2,1,0:T(8,128)(2,1)S(1)} %shard_map.48), channel_id=1, source_target_pairs={{0,1},{1,0},{2,3},{3,2},{4,5},{5,4},{6,7},{7,6},{8,9},{9,8},{10,11... | collective-permute-start | bytes 1548296 | tf_op jit(solution)/shard_map/ppermute | solution.py:27
  88.9 0.9 copy-start.1
  89.9 0.9 copy-start.3
  90.7 0.7 copy-start.5
  91.5 17.4 %collective-permute-start.4 = (bf16[7,288,128]{2,1,0:T(8,128)(2,1)}, bf16[7,288,128]{2,1,0:T(8,128)(2,1)S(1)}, u32[]{:S(2)}, u32[]{:S(2)}) collective-permute-start(bf16[7,288,128]{2,1,0:T(8,128)(2,1)} %get-tuple-element.30), channel_id=1, source_target_pairs={{0,1},{1,0},{2,3},{3,2},{4,5},{5,4},{6,7},{7,6},{8,9},{9,8},{10,11... | collective-permute-start | bytes 1548296 | tf_op jit(solution)/shard_map/ppermute | solution.py:27
  98.3 1.1 copy-start.2
  99.5 1.1 copy-start.4
  100.6 8.3 %copy-start.6 = (bf16[1536,128]{1,0:T(8,128)(2,1)S(1)}, bf16[1536,128]{1,0:T(8,128)(2,1)}, u32[]{:S(2)}) copy-start(bf16[1536,128]{1,0:T(8,128)(2,1)} %copy-done.5) | copy-start | bytes 1179652
Sparse Core Ops, SparseCore 0:
  9.4 67.7 all-gather.1
